TPU v7x, 32 devices: a whole 2x2x4 slice. The times are simulated.
32 devices in a mesh: row: 16 (over z, y, x), col: 2 (over core).
Axes of the slice: x: 2, y: 2, z: 4, core: 2. Of those that a mesh axis runs over, the one named last changes fastest.
Arguments:
- a_tiles: bfloat16 [256, 7, 4096], P('row'), may hold values from -0.25 to 0.25
- neighbors: int32 [256, 7], P('row'), may hold values from 0 to 143, as said below
- send_rows: int32 [16, 128], P('row'), may hold values from 0 to 15
- p_tiles: bfloat16 [256, 2, 4096], P('row', 'col'), may hold values from -0.75 to 0.75
- p_index: int32 [256, 2], P('row', 'col'), may hold values from 0 to 1
Outputs:
- coarse: float32 [256, 256], P('row', 'col')
Inputs may be any that keep to these rules, and one draw needn't show every extreme that they name: `neighbors`: column 0 of a row names the row itself (local index). Other entries below 16 are local rows. An entry v >= 16 names slot s = (v - 16) % 8 filled by device p = (v - 16) // 8, never the reading device itself; s < 8 when p is next to the reader along the row axis (with wrap), s < 4 otherwise.
All inputs are finite; a program needn't handle non-finite values.
Results may differ from a plain program's by a relative error of at most 0.0029.
Values may be sent and summed in bfloat16 or wider, within the bound.
No kernel may reach another device: no remote copies, remote signals or barrier semaphores. Data moves between devices by JAX's collectives and lax.ppermute only.
A program may use at most 64 MiB of HBM per device.

v0:
```python
import jax
import jax.numpy as jnp
from jax import lax
from jax.sharding import PartitionSpec as P

B = 64
CP = 2


def widen(tiles, index):
    count = tiles.shape[0]
    blocks = tiles.reshape(count, B, 1, B)
    hit = index[:, None] == jnp.arange(CP)[None, :]
    placed = jnp.where(hit[:, None, :, None], blocks, jnp.zeros((), jnp.bfloat16))
    return placed.reshape(count, B, CP * B)


def shards(a_tiles, neighbors, send_rows, p_tiles, p_index):
    rows = a_tiles.shape[0]
    span = a_tiles.shape[1]
    own_tiles = p_tiles[:, 0, :]
    own_index = p_index[:, 0]
    outgoing = send_rows[0]
    send_tiles = jnp.take(own_tiles, outgoing, axis=0)
    send_index = jnp.take(own_index, outgoing, axis=0)
    ghost_tiles, ghost_index = (
        lax.all_to_all(send_tiles, "row", split_axis=0, concat_axis=0, tiled=True),
        lax.all_to_all(send_index, "row", split_axis=0, concat_axis=0, tiled=True),
    )
    all_tiles = jnp.concatenate([own_tiles, ghost_tiles], axis=0)
    all_index = jnp.concatenate([own_index, ghost_index], axis=0)
    dense_panel = widen(all_tiles, all_index)
    picked = jnp.take(dense_panel, neighbors, axis=0)
    coupling = a_tiles.reshape(rows, span, B, B)
    product = jnp.einsum("rkij,rkjc->ric", coupling, picked, preferred_element_type=jnp.float32)
    product = product.astype(jnp.bfloat16).reshape(rows * B, CP * B)
    panel_tiles, panel_index = (
        lax.all_gather(p_tiles, "col", axis=1, tiled=True),
        lax.all_gather(p_index, "col", axis=1, tiled=True),
    )
    panels = panel_tiles.shape[1]
    blocks = (
        panel_tiles.reshape(rows, panels, B, B).transpose(0, 2, 1, 3).reshape(rows, B, panels, 1, B)
    )
    hit = panel_index[:, :, None] == jnp.arange(CP)[None, None, :]
    wide = jnp.where(hit[:, None, :, :, None], blocks, jnp.zeros((), jnp.bfloat16)).reshape(
        rows * B, panels * CP * B
    )
    return lax.psum_scatter(
        lax.dot_general(
            wide, product, (((0,), (0,)), ((), ())), preferred_element_type=jnp.float32
        ),
        "row",
        scatter_dimension=0,
        tiled=True,
    )


def solution(mesh):
    in_specs = (
        P("row", None, None),
        P("row", None),
        P("row", None),
        P("row", "col", None),
        P("row", "col"),
    )
    out_specs = P("row", "col")
    return jax.shard_map(shards, mesh=mesh, in_specs=in_specs, out_specs=out_specs, check_vma=False)
```

profile of v0, /device:TPU:0, one launch (start us, length us, event | category | flops | bytes accessed | tf_op | source)
XLA Modules:
  0.0 170.5 jit_solution(3934693713508479507)
XLA Ops:
  6.5 2.0 %fusion.17 = (s32[1,1]{0,1:T(1,128)}, s32[1,1]{0,1:T(1,128)}, s32[1,1]{0,1:T(1,128)}, s32[1,1]{0,1:T(1,128)}, s32[1,1]{0,1:T(1,128)}, /*index=5*/s32[1,1]{0,1:T(...) fusion(s32[16,1]{0,1:T(1,128)} %param.9), kind=kLoop, calls=%fused_computation.42 | loop fusion | bytes 128 | tf_op jit(solution)/shard_map/jit(_take)/gather | solution.py:25
  8.5 10.6 %compare_select_fusion.4 = s32[128]{0:T(128)S(1)} fusion(s32[]{:T(128)} %bitcast.7, s32[]{:T(128)} %bitcast.8, s32[]{:T(128)} %bitcast.9, s32[]{:T(128)} %bitcast.10, s32[]{:T(128)} %bitcast.11, s32[]{:T(128)} %bitcast.12, s32[]{:T(128)} %bitcast.13, s32[]{:T(128)} %bitcast.14, s32[]{:T(128)} %bitcast.15, s32[]{:T(128)} %bitcast.16, s32[]{:T(128)} %bitcast.17, ...), kind=kLoop, calls=%fused_computation.24 | loop fusion | flops 4224 | bytes 1088 | tf_op jit(solution)/shard_map/jit(_take)/gather | solution.py:25
  19.2 0.6 broadcast.189
  19.8 1.4 reduce.8
  21.2 0.6 and_select_fusion
  21.8 8.3 %all-to-all-start = ((s32[16,8,1]{1,2,0:T(1,128)}), s32[16,8,1]{1,2,0:T(1,128)S(1)}, u32[]{:S(2)}, u32[]{:S(2)}) async-start(s32[16,8,1]{1,2,0:T(1,128)} %bitcast.23), calls=%async_computation | async-start | bytes 16384 | tf_op jit(solution)/shard_map/all_to_all | solution.py:28
  30.1 0.7 fusion.15
  30.8 0.7 squeeze.16
  31.6 1.2 gather_fusion
  32.8 1.1 bitcast_select_fusion
  33.9 3.4 %all-to-all-done = s32[16,8,1]{1,2,0:T(1,128)S(1)} async-done(((s32[16,8,1]{1,2,0:T(1,128)}), s32[16,8,1]{1,2,0:T(1,128)S(1)}, u32[]{:S(2)}, u32[]{:S(2)}) %all-to-all-start) | async-done | bytes 544 | tf_op jit(solution)/shard_map/all_to_all | solution.py:28
  37.3 3.7 %all-to-all-start.1 = ((bf16[16,8,4096]{2,1,0:T(8,128)(2,1)}), bf16[16,8,4096]{2,1,0:T(8,128)(2,1)S(1)}, u32[]{:S(2)}, u32[]{:S(2)}) async-start(bf16[16,8,4096]{2,1,0:T(8,128)(2,1)} %bitcast_select_fusion), calls=%async_computation.1 | async-start | bytes 2097152 | tf_op jit(solution)/shard_map/all_to_all | solution.py:27
  41.1 1.8 %all-gather = s32[2,1,16]{2,1,0:T(1,128)S(1)} all-gather(s32[1,1,16]{2,1,0:T(1,128)S(1)} %bitcast.60), channel_id=1, replica_groups=mesh['row'=16,'col'=2] {'col'}, dimensions={0}, use_global_device_ids=true | all-gather | bytes 192 | tf_op jit(solution)/shard_map/all_gather | solution.py:39
  42.8 0.2 concatenate.12
  43.3 2.9 %reshape.153 = bf16[16,7,64,64]{3,2,0,1:T(8,128)(2,1)} reshape(bf16[16,7,4096]{2,0,1:T(8,128)(2,1)S(1)} %copy-done.2) | data formatting | bytes 1835008 | tf_op jit(solution)/shard_map/reshape | solution.py:34
  46.3 2.0 %all_gather.7 = bf16[16,2,4096]{2,0,1:T(8,128)(2,1)S(1)} all-gather(bf16[16,1,4096]{2,0,1:T(8,128)(2,1)S(1)} %copy-done), channel_id=1, replica_groups=mesh['row'=16,'col'=2] {'col'}, dimensions={1}, use_global_device_ids=true | all-gather | bytes 393216 | tf_op jit(solution)/shard_map/all_gather | solution.py:38
  48.3 0.5 reshape.152
  48.9 0.5 copy.18
  49.6 1.1 broadcast_select_fusion.1
  50.7 1.5 select_n.73
  52.2 0.7 reduce.9
  53.1 0.1 copy.21
  53.2 11.5 %all-to-all-done.1 = bf16[16,8,4096]{2,1,0:T(8,128)(2,1)S(1)} async-done(((bf16[16,8,4096]{2,1,0:T(8,128)(2,1)}), bf16[16,8,4096]{2,1,0:T(8,128)(2,1)S(1)}, u32[]{:S(2)}, u32[]{:S(2)}) %all-to-all-start.1) | async-done | bytes 1048608 | tf_op jit(solution)/shard_map/all_to_all | solution.py:27
  64.8 2.3 %concatenate.13 = bf16[128,64,1,64]{3,1,0,2:T(8,128)(2,1)S(1)} reshape(bf16[16,8,4096]{2,1,0:T(8,128)(2,1)S(1)} %all-to-all-done.1) | data formatting | bytes 2097152 | tf_op jit(solution)/shard_map/concatenate | solution.py:30
  67.0 0.5 maximum_bitcast_fusion
  67.5 4.6 %broadcast_in_dim.93 = bf16[144,64,2,64]{3,2,1,0:T(2,128)(2,1)} broadcast(bf16[144,64,64]{2,1,0:T(8,128)(2,1)S(1)} %maximum_bitcast_fusion), dimensions={0,1,3} | broadcast | bytes 3538944 | tf_op jit(solution)/shard_map/jit(_where)/broadcast_in_dim | solution.py:14
  72.1 7.6 %broadcast_in_dim.94 = bf16[144,64,128]{2,1,0:T(8,128)(2,1)S(1)} reshape(bf16[144,64,2,64]{3,2,1,0:T(2,128)(2,1)} %broadcast_in_dim.93) | data formatting | bytes 4718592 | tf_op jit(solution)/shard_map/jit(_where)/broadcast_in_dim | solution.py:14
  79.7 1.6 broadcast_select_fusion
  81.3 2.6 %gather_fusion.1 = bf16[112,64,128]{2,1,0:T(8,128)(2,1)S(1)} fusion(bf16[144,64,128]{2,1,0:T(8,128)(2,1)} %broadcast_select_fusion, s32[1024]{0:T(1024)S(1)} %pad_clamp_fusion), kind=kCustom, calls=%fused_computation.1 | custom fusion | bytes 3670464 | tf_op jit(solution)/shard_map/jit(_take)/gather | solution.py:33
  83.9 2.3 %fusion.9 = bf16[16,128,64]{1,2,0:T(8,128)(2,1)S(1)} fusion(bf16[16,7,64,128]{3,2,1,0:T(8,128)(2,1)S(1)} %bitcast.58, pred[16,7]{1,0:T(8,128)(4,1)S(1)} %copy.19, bf16[16,7,64,64]{3,2,0,1:T(8,128)(2,1)} %reshape.153), kind=kOutput, calls=%fused_computation.10 | convolution fusion | flops 118489088 | bytes 3014768 | tf_op jit(solution)/shard_map/rkij,rkjc->ric/dot_general | solution.py:35
  86.3 1.0 fusion.18
  87.3 76.3 %reduce-scatter.2.cloned.1.call-done = f32[16,128]{1,0:T(8,128)} async-done(((f32[256,128]{1,0:T(8,128)}), f32[16,128]{1,0:T(8,128)}) %reduce-scatter.2.cloned.1.call-update) | async-done | bytes 8208 | tf_op jit(solution)/shard_map/reduce_scatter | solution.py:49
  (28 shorter events, 0.9 us)
Async XLA Ops:
  6.5 25.0 %copy-start = (bf16[16,1,4096]{2,0,1:T(8,128)(2,1)S(1)}, bf16[16,1,4096]{2,0,1:T(8,128)(2,1)}, u32[]{:S(2)}) copy-start(bf16[16,1,4096]{2,0,1:T(8,128)(2,1)} %param.8) | copy-start | bytes 393220
  21.8 15.5 %all-to-all-start = ((s32[16,8,1]{1,2,0:T(1,128)}), s32[16,8,1]{1,2,0:T(1,128)S(1)}, u32[]{:S(2)}, u32[]{:S(2)}) async-start(s32[16,8,1]{1,2,0:T(1,128)} %bitcast.23), calls=%async_computation | async-start | bytes 16384 | tf_op jit(solution)/shard_map/all_to_all | solution.py:28
  32.8 8.3 %copy-start.3 = (s32[16,1]{0,1:T(1,128)S(1)}, s32[16,1]{0,1:T(1,128)}, u32[]{:S(2)}) copy-start(s32[16,1]{0,1:T(1,128)} %param.9) | copy-start | bytes 196
  32.8 10.3 %copy-start.4 = (s32[16,7]{0,1:T(8,128)S(1)}, s32[16,7]{0,1:T(8,128)}, u32[]{:S(2)}) copy-start(s32[16,7]{0,1:T(8,128)} %param.6) | copy-start | bytes 1348
  32.8 10.5 %copy-start.2 = (bf16[16,7,4096]{2,0,1:T(8,128)(2,1)S(1)}, bf16[16,7,4096]{2,0,1:T(8,128)(2,1)}, u32[]{:S(2)}) copy-start(bf16[16,7,4096]{2,0,1:T(8,128)(2,1)} %param.5) | copy-start | bytes 2752516
  37.3 27.4 %all-to-all-start.1 = ((bf16[16,8,4096]{2,1,0:T(8,128)(2,1)}), bf16[16,8,4096]{2,1,0:T(8,128)(2,1)S(1)}, u32[]{:S(2)}, u32[]{:S(2)}) async-start(bf16[16,8,4096]{2,1,0:T(8,128)(2,1)} %bitcast_select_fusion), calls=%async_computation.1 | async-start | bytes 2097152 | tf_op jit(solution)/shard_map/all_to_all | solution.py:27
  41.0 122.6 %reduce-scatter.2.cloned.1.call-start = ((), (), s32[]{:S(2)}) async-start(), calls=%async_computation.3 | async-start | bytes 139264 | tf_op jit(solution)/shard_map/reduce_scatter | solution.py:49
  83.9 2.4 %copy-start.1 = (bf16[1024,256]{1,0:T(8,128)(2,1)S(1)}, bf16[1024,256]{1,0:T(8,128)(2,1)}, u32[]{:S(2)}) copy-start(bf16[1024,256]{1,0:T(8,128)(2,1)} %select_n.73) | copy-start | bytes 1572868
Sparse Core Ops, SparseCore 0:
  87.4 76.1 reduce-scatter.1
where the time goes:
time: 171 us; the launch traced here: 170 us
  waiting for transfers between devices  91.3 us (53%)
  local copies, waits for them, and re-layouts  28 us (16%)
  other arithmetic  18.5 us (11%)
  between operations  13.6 us (8%)
  starting transfers between devices  12 us (7%)
  blocking collectives  3.75 us (2%)
  matrix products  3.34 us (2%)
    reduce_scatter x1, waiting for transfers between devices, shards(): lax.psum_scatter(lax.dot_general(wide, product, (((0,), (0,)), ((), ())),...  76.3 us
    broadcast_in_dim x4, local copies, waits for them, and re-layouts, widen(): jnp.where(hit[:, None, :, None], blocks, jnp.zeros((), jnp.bfloat16))  12.3 us
    all_to_all x1, waiting for transfers between devices, shards(): lax.all_to_all(send_tiles, 'row', split_axis=0, concat_axis=0, tiled=True)  11.5 us
    gather x1, other arithmetic, shards(): send_index = jnp.take(own_index, outgoing, axis=0)  10.6 us
    all_to_all x1, starting transfers between devices, shards(): lax.all_to_all(send_index, 'row', split_axis=0, concat_axis=0, tiled=True)  8.31 us
    all_to_all x1, starting transfers between devices, shards(): lax.all_to_all(send_tiles, 'row', split_axis=0, concat_axis=0, tiled=True)  3.65 us
  transfers between devices with their start and end apart: 3, of which 3 were waited for; matrix products, arithmetic and copies ran while one was open for 7% of the time, Pallas kernels for 0%

commit v1 on v0

v1 whole, which is shorter than its diff:
```python
import functools

import jax
import jax.numpy as jnp
from jax import lax
from jax.experimental import pallas as pl
from jax.experimental.pallas import tpu as pltpu
from jax.sharding import PartitionSpec as P

B = 64
CP = 2
S = 8
S2 = 4
LANES = 128
PACK = B * B // LANES
BF16 = jnp.bfloat16
VMEM = pl.BlockSpec(memory_space=pltpu.VMEM)
SMEM = pl.BlockSpec(memory_space=pltpu.SMEM)
PARAMS = pltpu.CompilerParams(vmem_limit_bytes=40 * 2**20)


def unpack_rows(flat, scratch):
    for l in range(PACK):
        scratch[:, l, :] = flat[:, l * LANES : (l + 1) * LANES].astype(jnp.float32)


def swap_halves(x):
    return jnp.concatenate([x[:, B:], x[:, :B]], axis=1)


def turn_rows(flat, index_of, scratch, out, base):
    rows = scratch.shape[0]
    unpack_rows(flat, scratch)
    for r in range(rows):
        x = scratch[r]
        x = jnp.where(index_of(r) == 0, x, swap_halves(x))
        out[base + r * PACK : base + (r + 1) * PACK, :] = x.astype(BF16)


def mask_row(index, shape):
    lane = lax.broadcasted_iota(jnp.int32, shape, len(shape) - 1)
    return jnp.where((lane >= B) == (index != 0), 1.0, 0.0)


def widen(x, mask):
    return x * mask, swap_halves(x) * mask


def mask_table(index_of, rows):
    sub = lax.broadcasted_iota(jnp.int32, (rows, LANES), 0)
    table = jnp.zeros((rows, LANES), jnp.float32)
    for r in range(rows):
        table = jnp.where(sub == r, mask_row(index_of(r), (rows, LANES)), table)
    return table


def fill(ref, block, table, picks, marks):
    sub = lax.broadcasted_iota(jnp.int32, (marks, LANES), 0)
    mark = jnp.zeros((marks, LANES), jnp.float32)
    for s, (row, index) in enumerate(picks):
        tile = table[pl.ds(pl.multiple_of(row * PACK, PACK), PACK), :]
        ref[(*block, pl.ds(s * PACK, PACK), slice(None))] = tile
        mark = jnp.where(sub == s, mask_row(index, (marks, LANES)), mark)
    ref[(*block, pl.ds(len(picks) * PACK, marks), slice(None))] = mark.astype(BF16)


def own_kernel(n, send_ref, index_ref, flat_ref, own_ref, left_ref, right_ref, scratch):
    rows = flat_ref.shape[0]
    me = lax.axis_index("row")
    turn_rows(flat_ref, lambda r: index_ref[0, r], scratch, own_ref, 0)
    own_ref[rows * PACK :, :] = mask_table(lambda r: index_ref[0, r], rows).astype(BF16)

    def look(slot):
        row = send_ref[0, slot]
        return row, index_ref[0, row]

    for ref, step in ((left_ref, n - 1), (right_ref, 1)):
        first = lax.rem(me + step, n) * S
        fill(ref, (), own_ref, [look(first + s) for s in range(S2, S)], 8)


def pack_kernel(n, send_ref, index_ref, far_ref, own_ref, flat_ref, out_ref, scratch, table):
    rows = flat_ref.shape[0]
    half = n // 2
    me = lax.axis_index("row")
    base = me - lax.rem(me, half)
    turn_rows(flat_ref, lambda r: far_ref[0, n * S + r], scratch, table, rows * PACK)
    table[: rows * PACK, :] = own_ref[: rows * PACK, :]

    def near_row(slot):
        row = send_ref[0, slot]
        return row, index_ref[0, row]

    def far_row(slot):
        row = far_ref[0, slot]
        return rows + row, far_ref[0, n * S + row]

    for j in range(half):
        first = (base + j) * S
        picks = [near_row(first + s) for s in range(S2)] + [far_row(first + s) for s in range(S2)]
        fill(out_ref, (j,), table, picks, 8)


def coupling_kernel(a_ref, coupling_ref, scratch):
    span, rows, _ = a_ref.shape
    src = lax.broadcasted_iota(jnp.int32, (LANES, LANES), 0)
    dst = lax.broadcasted_iota(jnp.int32, (LANES, LANES), 1)
    part = lax.rem(dst, B)
    want = (dst - part) + jnp.where(part < B // 2, 2 * part, 2 * part - B + 1)
    order = (src == want).astype(BF16)
    for k in range(span):
        unpack_rows(a_ref.at[k], scratch.at[k % 2])
        packed = scratch[k % 2].reshape(rows * PACK, LANES).astype(BF16)
        ordered = jnp.dot(packed, order, preferred_element_type=jnp.float32)
        even = ordered[:, :B].astype(BF16).reshape(rows, PACK, B)
        odd = ordered[:, B:].astype(BF16).reshape(rows, PACK, B)
        coupling_ref[:, :PACK, k * B : (k + 1) * B] = even
        coupling_ref[:, PACK:, k * B : (k + 1) * B] = odd


def restrict_kernel(rows, col_size, *refs):
    panel_refs, restrict_ref = refs[:col_size], refs[col_size]
    mine = lax.axis_index("col")
    for j, panel_ref in enumerate(panel_refs):
        panel = lax.rem(mine + col_size - j, col_size)
        pieces = []
        for r in range(rows):
            mask = panel_ref[rows * PACK + r : rows * PACK + r + 1, :].astype(jnp.float32)
            x = panel_ref[r * PACK : (r + 1) * PACK, :].astype(jnp.float32)
            pieces.extend(widen(x, mask))
        wide = jnp.concatenate(pieces, axis=0)
        restrict_ref[pl.ds(pl.multiple_of(panel * CP * B, LANES), CP * B), :] = wide.T.astype(BF16)


def product_kernel(
    n, code_ref, ghost_ref, left_ref, right_ref, own_ref, coupling_ref, restrict_ref, out_ref, wide, ap
):
    half = n // 2
    rows = coupling_ref.shape[0]
    span = code_ref.shape[0]
    me = lax.axis_index("row")
    base = me - lax.rem(me, half)

    def place(slot, tile, mask):
        even, odd = widen(tile, mask)
        to = pl.multiple_of(slot * B, B)
        wide[pl.ds(to, PACK), :] = even
        wide[pl.ds(pl.multiple_of(to + PACK, PACK), PACK), :] = odd

    def place_slots(first, ref, block, at, marks_at):
        for s in range(S2):
            tile = ref[(*block, pl.ds((at + s) * PACK, PACK), slice(None))]
            place(rows + first + s, tile, ref[(*block, pl.ds(marks_at + at + s, 1), slice(None))])

    for r in range(rows):
        place(r, own_ref[r * PACK : (r + 1) * PACK, :], own_ref[rows * PACK + r : rows * PACK + r + 1, :])
    for j in range(half):
        place_slots((base + j) * S, ghost_ref, (j,), 0, 2 * S2 * PACK)
        place_slots(lax.rem(base + half + j, n) * S, ghost_ref, (j,), S2, 2 * S2 * PACK)
    for ref, step in ((left_ref, n - 1), (right_ref, 1)):
        place_slots(lax.rem(me + step, n) * S + S2, ref, (), 0, S2 * PACK)

    def row_body(r, carry):
        picked = jnp.concatenate(
            [wide[pl.ds(pl.multiple_of(code_ref[k, r] * B, B), B), :] for k in range(span)], axis=0
        )
        block = jnp.dot(coupling_ref[r], picked, preferred_element_type=jnp.float32)
        ap[pl.ds(pl.multiple_of(r * B, B), B), :] = block.astype(BF16)
        return carry

    lax.fori_loop(0, rows, row_body, 0, unroll=8)
    out_ref[...] = jnp.dot(restrict_ref[...], ap[...], preferred_element_type=jnp.float32)


def shards(n, col_size, a_tiles, neighbors, send_rows, p_tiles, p_index):
    rows, span = a_tiles.shape[0], a_tiles.shape[1]
    half = n // 2
    halves = [list(range(half)), list(range(half, n))]
    flat = p_tiles[:, 0, :]
    index = p_index.T
    f32 = jnp.float32

    def call(body, out_shape, scratch_shapes, operands, smem, name, flops=10**7):
        return pl.pallas_call(
            body,
            out_shape=out_shape,
            in_specs=[SMEM] * smem + [VMEM] * (len(operands) - smem),
            out_specs=jax.tree.map(lambda _: VMEM, out_shape),
            scratch_shapes=scratch_shapes,
            compiler_params=PARAMS,
            cost_estimate=pl.CostEstimate(flops=flops, bytes_accessed=2**20, transcendentals=0),
            name=name,
        )(*operands)

    def shape(*dims, dtype=BF16):
        return jax.ShapeDtypeStruct(dims, dtype)

    def ring(x, step):
        return lax.ppermute(x, "row", [(i, (i + step) % n) for i in range(n)])

    unpacked = pltpu.VMEM((rows, PACK, LANES), f32)
    far_flat = ring(flat, half)
    far_ints = ring(jnp.concatenate([send_rows, index], axis=1), half)
    edge = shape(S2 * PACK + 8, LANES)
    own, left, right = call(
        functools.partial(own_kernel, n),
        [shape(rows * PACK + rows, LANES), edge, edge],
        [unpacked],
        (send_rows, index, flat),
        2,
        "own",
    )
    from_right, from_left = ring(left, n - 1), ring(right, 1)
    panels = [own] + [
        lax.ppermute(own, "col", [(i, (i + j) % col_size) for i in range(col_size)])
        for j in range(1, col_size)
    ]
    far_flat, far_ints, from_left, from_right = lax.optimization_barrier(
        (far_flat, far_ints, from_left, from_right)
    )
    out = call(
        functools.partial(pack_kernel, n),
        shape(half, 2 * S2 * PACK + 8, LANES),
        [unpacked, pltpu.VMEM((2 * rows * PACK, LANES), BF16)],
        (send_rows, index, far_ints, own, far_flat),
        3,
        "pack",
    )
    out, a_tiles = lax.optimization_barrier((out, a_tiles))
    ghosts = lax.all_to_all(out, "row", split_axis=0, concat_axis=0, tiled=True, axis_index_groups=halves)
    coupling = call(
        coupling_kernel,
        shape(rows, B, span * B),
        [pltpu.VMEM((2, rows, PACK, LANES), f32)],
        (a_tiles.transpose(1, 0, 2),),
        0,
        "coupling",
        2 * 10**9,
    )
    restrict = call(
        functools.partial(restrict_kernel, rows, col_size),
        shape(col_size * CP * B, rows * B),
        [],
        panels,
        0,
        "restrict",
        2 * 10**8,
    )
    partial = call(
        functools.partial(product_kernel, n),
        shape(col_size * CP * B, CP * B, dtype=f32),
        [pltpu.VMEM(((rows + n * S) * B, LANES), BF16), pltpu.VMEM((rows * B, CP * B), BF16)],
        (neighbors.T, ghosts, from_left, from_right, own, coupling, restrict),
        1,
        "product",
        2 * 10**8,
    )
    share = col_size * CP * B // n
    parts = lax.all_to_all(
        partial.reshape(n, share, CP * B), "row", split_axis=0, concat_axis=0, tiled=True
    )
    return jnp.sum(parts, axis=0)


def solution(mesh):
    in_specs = (
        P("row", None, None),
        P("row", None),
        P("row", None),
        P("row", "col", None),
        P("row", "col"),
    )
    out_specs = P("row", "col")
    body = functools.partial(shards, mesh.shape["row"], mesh.shape["col"])
    return jax.shard_map(body, mesh=mesh, in_specs=in_specs, out_specs=out_specs, check_vma=False)
```

time: 171 us -> 43.2 us (0.25)
  waiting for transfers between devices: 91.3 us -> 9.53 us
  local copies, waits for them, and re-layouts: 28 us -> 0.95 us
  other arithmetic: 18.5 us -> 0.62 us
  between operations: 13.6 us -> 0.07 us
  blocking collectives: 3.75 us -> 11.5 us
  Pallas kernels: 0 us -> 7.03 us
  matrix products: 3.34 us -> 0 us
    reduce_scatter x1 -> x0, waiting for transfers between devices: 76.3 us -> none  [shards(): lax.psum_scatter(lax.dot_general(wide, product, (((0,), (0,)), ((), ())),...]
    broadcast_in_dim x5 -> x0, local copies, waits for them, and re-layouts: 12.4 us -> none  [the longest x4 12.3 us: widen(): jnp.where(hit[:, None, :, None], blocks, jnp.zeros((), jnp.bfloat16))]
    all_to_all x0 -> x1, blocking collectives: none -> 11.5 us  [shards(): lax.all_to_all(partial.reshape(n, share, CP * B), 'row', split_axis=0, co...]
    gather x3 -> x0, other arithmetic: 10.6 us -> none  [the longest x1 10.6 us: shards(): send_index = jnp.take(own_index, outgoing, axis=0)]
    all_to_all x2 -> x1, waiting for transfers between devices: 14.9 us -> 5.06 us  [shards(): lax.all_to_all(out, 'row', split_axis=0, concat_axis=0, tiled=True, axis_...]
    ppermute x0 -> x5, starting transfers between devices: none -> 9.78 us  [the longest x4 9.71 us: ring(): return lax.ppermute(x, 'row', [(i, (i + step) % n) for i in range(n)])]
    all_to_all x2 -> x1, starting transfers between devices: 12 us -> 3.54 us  [shards(): lax.all_to_all(out, 'row', split_axis=0, concat_axis=0, tiled=True, axis_...]
    pallas_call x0 -> x5, Pallas kernels: none -> 7.03 us  [call(): pl.pallas_call(body, out_shape=out_shape, in_specs=[SMEM] * smem + [VMEM]...]
  transfers between devices with their start and end apart: 3 -> 6, of which waited for: 3 -> 2; matrix products, arithmetic and copies ran while one was open for 7% -> 0% of each run, Pallas kernels for 0% -> 8%
where the time goes in v1:
time: 43.2 us; the launch traced here: 43 us
  starting transfers between devices  13.3 us (31%)
  blocking collectives  11.5 us (27%)
  waiting for transfers between devices  9.53 us (22%)
  Pallas kernels  7.03 us (16%)
  local copies, waits for them, and re-layouts  0.95 us (2%)
  other arithmetic  0.62 us (1%)
    all_to_all x1, blocking collectives, shards(): lax.all_to_all(partial.reshape(n, share, CP * B), 'row', split_axis=0, co...  11.5 us
    ppermute x4, starting transfers between devices, ring(): return lax.ppermute(x, 'row', [(i, (i + step) % n) for i in range(n)])  9.71 us
    pallas_call x5, Pallas kernels, call(): pl.pallas_call(body, out_shape=out_shape, in_specs=[SMEM] * smem + [VMEM]...  7.03 us
    all_to_all x1, waiting for transfers between devices, shards(): lax.all_to_all(out, 'row', split_axis=0, concat_axis=0, tiled=True, axis_...  5.06 us
    ppermute x4, waiting for transfers between devices, ring(): return lax.ppermute(x, 'row', [(i, (i + step) % n) for i in range(n)])  4.47 us
    all_to_all x1, starting transfers between devices, shards(): lax.all_to_all(out, 'row', split_axis=0, concat_axis=0, tiled=True, axis_...  3.54 us
    unnamed x10, local copies, waits for them, and re-layouts  0.95 us
  transfers between devices with their start and end apart: 6, of which 2 were waited for; matrix products, arithmetic and copies ran while one was open for 0% of the time, Pallas kernels for 8%

profile of v1, /device:TPU:0, one launch (start us, length us, event | category | flops | bytes accessed | tf_op | source)
XLA Modules:
  0.0 43.0 jit_solution(4955219051631802462)
XLA Ops:
  0.0 0.0 copy-start.1
  0.0 0.0 copy-start.2
  0.0 4.0 %collective-permute-start = (bf16[16,4096]{1,0:T(8,128)(2,1)}, bf16[16,4096]{1,0:T(8,128)(2,1)S(1)}, u32[]{:S(2)}, u32[]{:S(2)}) collective-permute-start(bf16[16,4096]{1,0:T(8,128)(2,1)} %bitcast.6), channel_id=1, source_target_pairs={{0,16},{2,18},{4,20},{6,22},{8,24},{10,26},{12,28},{14,30},{16,0},... | collective-permute-start | bytes 393224 | tf_op jit(solution)/shard_map/ppermute | solution.py:199
  4.0 0.0 copy-done.1
  4.0 0.0 copy-done.2
  4.0 0.0 copy-start
  4.0 0.9 %copy-done = bf16[16,1,4096]{2,0,1:T(8,128)(2,1)S(1)} copy-done((bf16[16,1,4096]{2,0,1:T(8,128)(2,1)S(1)}, bf16[16,1,4096]{2,0,1:T(8,128)(2,1)}, u32[]{:S(2)}) %copy-start) | copy-done | bytes 131096
  5.0 0.9 %own.1 = (bf16[528,128]{1,0:T(8,128)(2,1)S(1)}, bf16[136,128]{1,0:T(8,128)(2,1)S(1)}, bf16[136,128]{1,0:T(8,128)(2,1)S(1)}) custom-call(s32[1,128]{1,0:T(1,128)S(1)} %copy-done.1, s32[1,16]{1,0:T(1,128)S(1)} %bitcast.8, bf16[16,4096]{1,0:T(8,128)(2,1)S(1)} %bitcast.7), custom_call_target="tpu_custom_call" | custom-call | flops 10000000 | bytes 1048576 | tf_op jit(solution)/shard_map/own/pallas_call | solution.py:184
  5.9 1.5 %collective-permute-start.2 = (bf16[136,128]{1,0:T(8,128)(2,1)S(1)}, bf16[136,128]{1,0:T(8,128)(2,1)S(1)}, u32[]{:S(2)}, u32[]{:S(2)}) collective-permute-start(bf16[136,128]{1,0:T(8,128)(2,1)S(1)} %get-tuple-element.14), channel_id=1, source_target_pairs={{0,2},{2,4},{4,6},{6,8},{8,10},{10,12},{12,14},{14,16},{16,18},{18... | collective-permute-start | bytes 104456 | tf_op jit(solution)/shard_map/ppermute | solution.py:199
  7.4 4.1 %collective-permute-start.3 = (bf16[136,128]{1,0:T(8,128)(2,1)S(1)}, bf16[136,128]{1,0:T(8,128)(2,1)S(1)}, u32[]{:S(2)}, u32[]{:S(2)}) collective-permute-start(bf16[136,128]{1,0:T(8,128)(2,1)S(1)} %get-tuple-element.15), channel_id=1, source_target_pairs={{0,30},{2,0},{4,2},{6,4},{8,6},{10,8},{12,10},{14,12},{16,14},{18,... | collective-permute-start | bytes 104456 | tf_op jit(solution)/shard_map/ppermute | solution.py:199
  11.6 0.0 collective-permute-start.1
  11.6 4.5 %collective-permute-done.1.far_ref = s32[1,144]{1,0:T(1,128)S(1)} collective-permute-done((s32[1,144]{1,0:T(1,128)S(1)}, s32[1,144]{1,0:T(1,128)S(1)}, u32[]{:S(2)}, u32[]{:S(2)}) %collective-permute-start.1) | collective-permute-done | bytes 608 | tf_op jit(solution)/shard_map/ppermute | solution.py:199
  16.0 0.0 collective-permute-done.2.left_ref
  16.0 0.0 collective-permute-done.3.right_ref
  16.0 0.0 collective-permute-done.flat_ref
  16.0 0.0 copy-start.4
  16.0 1.8 %pack.1 = bf16[8,264,128]{2,1,0:T(8,128)(2,1)} custom-call(s32[1,128]{1,0:T(1,128)S(1)} %copy-done.1, s32[1,16]{1,0:T(1,128)S(1)} %bitcast.10, s32[1,144]{1,0:T(1,128)S(1)} %collective-permute-done.1.far_ref, bf16[528,128]{1,0:T(8,128)(2,1)S(1)} %get-tuple-element.17.own_ref.refs_0_, bf16[16,4096]{1,0:T(8,128)(2,1)S(1)} %collective-permute-done.flat_ref), custom_call_target="tpu_custom_call" | custom-call | flops 10000000 | bytes 1048576 | tf_op jit(solution)/shard_map/pack/pallas_call | solution.py:184
  17.8 3.5 %all-to-all-start = ((bf16[8,264,128]{2,1,0:T(8,128)(2,1)}), bf16[8,264,128]{2,1,0:T(8,128)(2,1)S(1)}, u32[]{:S(2)}, u32[]{:S(2)}) async-start(bf16[8,264,128]{2,1,0:T(8,128)(2,1)} %pack.1), calls=%async_computation | async-start | bytes 1081344 | tf_op jit(solution)/shard_map/all_to_all | solution.py:230
  21.4 0.1 collective-permute-start.4
  21.5 0.0 copy-done.4
  21.5 2.2 %coupling.1.coupling_ref = bf16[16,64,448]{2,1,0:T(8,128)(2,1)S(1)} custom-call(bf16[7,16,4096]{2,1,0:T(8,128)(2,1)S(1)} %bitcast.12), custom_call_target="tpu_custom_call" | custom-call | flops 2000000000 | bytes 1048576 | tf_op jit(solution)/shard_map/coupling/pallas_call | solution.py:184
  23.7 0.0 collective-permute-done.4.refs_1_
  23.7 0.0 copy-start.3
  23.7 0.3 restrict.1.restrict_ref
  24.0 5.1 %all-to-all-done.ghost_ref = bf16[8,264,128]{2,1,0:T(8,128)(2,1)S(1)} async-done(((bf16[8,264,128]{2,1,0:T(8,128)(2,1)}), bf16[8,264,128]{2,1,0:T(8,128)(2,1)S(1)}, u32[]{:S(2)}, u32[]{:S(2)}) %all-to-all-start) | async-done | bytes 540704 | tf_op jit(solution)/shard_map/all_to_all | solution.py:230
  29.1 0.0 copy-done.3
  29.1 1.8 %product.1 = f32[256,128]{1,0:T(8,128)S(1)} custom-call(s32[7,16]{1,0:T(8,128)S(1)} %bitcast.11, bf16[8,264,128]{2,1,0:T(8,128)(2,1)S(1)} %all-to-all-done.ghost_ref, bf16[136,128]{1,0:T(8,128)(2,1)S(1)} %collective-permute-done.2.left_ref, bf16[136,128]{1,0:T(8,128)(2,1)S(1)} %collective-permute-done.3.right_ref, ...), custom_call_target="tpu_custom_call" | custom-call | flops 200000000 | bytes 1048576 | tf_op jit(solution)/shard_map/product/pallas_call | solution.py:184
  30.9 11.5 %all_to_all.10 = f32[16,16,128]{2,1,0:T(8,128)S(1)} all-to-all(f32[16,16,128]{2,1,0:T(8,128)S(1)} %bitcast.5), channel_id=1, replica_groups=mesh['row'=16,'col'=2] {'row'}, dimensions={0} | all-to-all | bytes 262144 | tf_op jit(solution)/shard_map/all_to_all | solution.py:259
  42.4 0.6 %reduce_sum.9 = f32[16,128]{1,0:T(8,128)} reduce(f32[16,16,128]{2,1,0:T(8,128)S(1)} %all_to_all.10, f32[]{:T(128)} %constant.0.clone.1), dimensions={0}, to_apply=%region_0.0 | reduce | flops 30720 | bytes 139268 | tf_op jit(solution)/shard_map/reduce_sum | solution.py:262
  (1 shorter events, 0.0 us)
Async XLA Ops:
  0.0 4.0 %copy-start.1 = (s32[1,128]{1,0:T(1,128)S(1)}, s32[1,128]{1,0:T(1,128)}, u32[]{:S(2)}) copy-start(s32[1,128]{1,0:T(1,128)} %send_ref.3) | copy-start | bytes 1540
  0.0 4.0 %copy-start.2 = (s32[16,1]{0,1:T(1,128)S(1)}, s32[16,1]{0,1:T(1,128)}, u32[]{:S(2)}) copy-start(s32[16,1]{0,1:T(1,128)} %param.9) | copy-start | bytes 196
  0.0 16.0 %collective-permute-start = (bf16[16,4096]{1,0:T(8,128)(2,1)}, bf16[16,4096]{1,0:T(8,128)(2,1)S(1)}, u32[]{:S(2)}, u32[]{:S(2)}) collective-permute-start(bf16[16,4096]{1,0:T(8,128)(2,1)} %bitcast.6), channel_id=1, source_target_pairs={{0,16},{2,18},{4,20},{6,22},{8,24},{10,26},{12,28},{14,30},{16,0},... | collective-permute-start | bytes 393224 | tf_op jit(solution)/shard_map/ppermute | solution.py:199
  4.0 0.9 %copy-start = (bf16[16,1,4096]{2,0,1:T(8,128)(2,1)S(1)}, bf16[16,1,4096]{2,0,1:T(8,128)(2,1)}, u32[]{:S(2)}) copy-start(bf16[16,1,4096]{2,0,1:T(8,128)(2,1)} %param.8) | copy-start | bytes 393220
  5.9 10.2 %collective-permute-start.2 = (bf16[136,128]{1,0:T(8,128)(2,1)S(1)}, bf16[136,128]{1,0:T(8,128)(2,1)S(1)}, u32[]{:S(2)}, u32[]{:S(2)}) collective-permute-start(bf16[136,128]{1,0:T(8,128)(2,1)S(1)} %get-tuple-element.14), channel_id=1, source_target_pairs={{0,2},{2,4},{4,6},{6,8},{8,10},{10,12},{12,14},{14,16},{16,18},{18... | collective-permute-start | bytes 104456 | tf_op jit(solution)/shard_map/ppermute | solution.py:199
  7.4 8.6 %collective-permute-start.3 = (bf16[136,128]{1,0:T(8,128)(2,1)S(1)}, bf16[136,128]{1,0:T(8,128)(2,1)S(1)}, u32[]{:S(2)}, u32[]{:S(2)}) collective-permute-start(bf16[136,128]{1,0:T(8,128)(2,1)S(1)} %get-tuple-element.15), channel_id=1, source_target_pairs={{0,30},{2,0},{4,2},{6,4},{8,6},{10,8},{12,10},{14,12},{16,14},{18,... | collective-permute-start | bytes 104456 | tf_op jit(solution)/shard_map/ppermute | solution.py:199
  11.6 4.5 %collective-permute-start.1 = (s32[1,144]{1,0:T(1,128)S(1)}, s32[1,144]{1,0:T(1,128)S(1)}, u32[]{:S(2)}, u32[]{:S(2)}) collective-permute-start(s32[1,144]{1,0:T(1,128)S(1)} %pad_add_fusion), channel_id=1, source_target_pairs={{0,16},{2,18},{4,20},{6,22},{8,24},{10,26},{12,28},{14,30},{16,0},... | collective-permute-start | bytes 1736 | tf_op jit(solution)/shard_map/ppermute | solution.py:199
  16.0 5.4 %copy-start.4 = (bf16[16,7,4096]{2,0,1:T(8,128)(2,1)S(1)}, bf16[16,7,4096]{2,0,1:T(8,128)(2,1)}, u32[]{:S(2)}) copy-start(bf16[16,7,4096]{2,0,1:T(8,128)(2,1)} %param.5) | copy-start | bytes 2752516
  17.8 11.2 %all-to-all-start = ((bf16[8,264,128]{2,1,0:T(8,128)(2,1)}), bf16[8,264,128]{2,1,0:T(8,128)(2,1)S(1)}, u32[]{:S(2)}, u32[]{:S(2)}) async-start(bf16[8,264,128]{2,1,0:T(8,128)(2,1)} %pack.1), calls=%async_computation | async-start | bytes 1081344 | tf_op jit(solution)/shard_map/all_to_all | solution.py:230
  21.4 2.3 %collective-permute-start.4 = (bf16[528,128]{1,0:T(8,128)(2,1)S(1)}, bf16[528,128]{1,0:T(8,128)(2,1)S(1)}, u32[]{:S(2)}, u32[]{:S(2)}) collective-permute-start(bf16[528,128]{1,0:T(8,128)(2,1)S(1)} %get-tuple-element.17.own_ref.refs_0_), channel_id=1, source_target_pairs={{0,1},{1,0},{2,3},{3,2},{4,5},{5,4},{6,7},{7,6},{8,9},{9,8},{10,11... | collective-permute-start | bytes 405512 | tf_op jit(solution)/shard_map/ppermute | solution.py:215
  23.7 5.4 %copy-start.3 = (s32[16,7]{0,1:T(8,128)S(1)}, s32[16,7]{0,1:T(8,128)}, u32[]{:S(2)}) copy-start(s32[16,7]{0,1:T(8,128)} %param.6) | copy-start | bytes 1348

commit v2 on v1

--- a/solution.py
+++ b/solution.py
@@ -64,9 +64,11 @@
     ref[(*block, pl.ds(len(picks) * PACK, marks), slice(None))] = mark.astype(BF16)
 
 
-def own_kernel(n, send_ref, index_ref, flat_ref, own_ref, left_ref, right_ref, scratch):
+def own_kernel(n, send_ref, index_ref, flat_ref, own_ref, near_ref, left_ref, right_ref, scratch):
     rows = flat_ref.shape[0]
+    half = n // 2
     me = lax.axis_index("row")
+    base = me - lax.rem(me, half)
     turn_rows(flat_ref, lambda r: index_ref[0, r], scratch, own_ref, 0)
     own_ref[rows * PACK :, :] = mask_table(lambda r: index_ref[0, r], rows).astype(BF16)
 
@@ -74,48 +76,45 @@
         row = send_ref[0, slot]
         return row, index_ref[0, row]
 
+    for j in range(half):
+        fill(near_ref, (j,), own_ref, [look((base + j) * S + s) for s in range(S2)], 8)
     for ref, step in ((left_ref, n - 1), (right_ref, 1)):
         first = lax.rem(me + step, n) * S
         fill(ref, (), own_ref, [look(first + s) for s in range(S2, S)], 8)
 
 
-def pack_kernel(n, send_ref, index_ref, far_ref, own_ref, flat_ref, out_ref, scratch, table):
-    rows = flat_ref.shape[0]
+def far_kernel(n, far_ref, flat_ref, out_ref, scratch, table):
     half = n // 2
     me = lax.axis_index("row")
     base = me - lax.rem(me, half)
-    turn_rows(flat_ref, lambda r: far_ref[0, n * S + r], scratch, table, rows * PACK)
-    table[: rows * PACK, :] = own_ref[: rows * PACK, :]
-
-    def near_row(slot):
-        row = send_ref[0, slot]
-        return row, index_ref[0, row]
-
-    def far_row(slot):
+    turn_rows(flat_ref, lambda r: far_ref[0, n * S + r], scratch, table, 0)
+
+    def look(slot):
         row = far_ref[0, slot]
-        return rows + row, far_ref[0, n * S + row]
+        return row, far_ref[0, n * S + row]
 
     for j in range(half):
-        first = (base + j) * S
-        picks = [near_row(first + s) for s in range(S2)] + [far_row(first + s) for s in range(S2)]
-        fill(out_ref, (j,), table, picks, 8)
+        fill(out_ref, (j,), table, [look((base + j) * S + s) for s in range(S2)], 8)
 
 
 def coupling_kernel(a_ref, coupling_ref, scratch):
     span, rows, _ = a_ref.shape
-    src = lax.broadcasted_iota(jnp.int32, (LANES, LANES), 0)
-    dst = lax.broadcasted_iota(jnp.int32, (LANES, LANES), 1)
-    part = lax.rem(dst, B)
-    want = (dst - part) + jnp.where(part < B // 2, 2 * part, 2 * part - B + 1)
-    order = (src == want).astype(BF16)
-    for k in range(span):
-        unpack_rows(a_ref.at[k], scratch.at[k % 2])
-        packed = scratch[k % 2].reshape(rows * PACK, LANES).astype(BF16)
-        ordered = jnp.dot(packed, order, preferred_element_type=jnp.float32)
-        even = ordered[:, :B].astype(BF16).reshape(rows, PACK, B)
-        odd = ordered[:, B:].astype(BF16).reshape(rows, PACK, B)
-        coupling_ref[:, :PACK, k * B : (k + 1) * B] = even
-        coupling_ref[:, PACK:, k * B : (k + 1) * B] = odd
+    src = lax.broadcasted_iota(jnp.int32, (2 * LANES, 2 * LANES), 0)
+    dst = lax.broadcasted_iota(jnp.int32, (2 * LANES, 2 * LANES), 1)
+    odd, block, part = dst // LANES, lax.rem(dst // B, 2), lax.rem(dst, B)
+    column = jnp.where(part < B // 2, 2 * part, 2 * part - B + 1)
+    order = (src == block * LANES + odd * B + column).astype(BF16)
+    for pair in range(pl.cdiv(span, 2)):
+        blocks = range(2 * pair, min(2 * pair + 2, span))
+        buffer = scratch.at[pair % 2]
+        for k in blocks:
+            unpack_rows(a_ref.at[k], buffer.at[:, :, pl.ds((k % 2) * LANES, LANES)])
+        width = len(blocks) * LANES
+        packed = buffer[:, :, :width].reshape(rows * PACK, width).astype(BF16)
+        ordered = jnp.dot(packed, order[:width], preferred_element_type=jnp.float32).astype(BF16)
+        lanes = pl.ds(pair * LANES, LANES)
+        coupling_ref[:, :PACK, lanes] = ordered[:, :LANES].reshape(rows, PACK, LANES)
+        coupling_ref[:, PACK:, lanes] = ordered[:, LANES:].reshape(rows, PACK, LANES)
 
 
 def restrict_kernel(rows, col_size, *refs):
@@ -133,7 +132,7 @@
 
 
 def product_kernel(
-    n, code_ref, ghost_ref, left_ref, right_ref, own_ref, coupling_ref, restrict_ref, out_ref, wide, ap
+    n, code_ref, near_ref, far_ref, left_ref, right_ref, own_ref, coupling_ref, restrict_ref, out_ref, wide, ap
 ):
     half = n // 2
     rows = coupling_ref.shape[0]
@@ -147,24 +146,24 @@
         wide[pl.ds(to, PACK), :] = even
         wide[pl.ds(pl.multiple_of(to + PACK, PACK), PACK), :] = odd
 
-    def place_slots(first, ref, block, at, marks_at):
+    def place_slots(first, ref, block):
         for s in range(S2):
-            tile = ref[(*block, pl.ds((at + s) * PACK, PACK), slice(None))]
-            place(rows + first + s, tile, ref[(*block, pl.ds(marks_at + at + s, 1), slice(None))])
+            tile = ref[(*block, pl.ds(s * PACK, PACK), slice(None))]
+            place(rows + first + s, tile, ref[(*block, pl.ds(S2 * PACK + s, 1), slice(None))])
 
     for r in range(rows):
         place(r, own_ref[r * PACK : (r + 1) * PACK, :], own_ref[rows * PACK + r : rows * PACK + r + 1, :])
     for j in range(half):
-        place_slots((base + j) * S, ghost_ref, (j,), 0, 2 * S2 * PACK)
-        place_slots(lax.rem(base + half + j, n) * S, ghost_ref, (j,), S2, 2 * S2 * PACK)
+        place_slots((base + j) * S, near_ref, (j,))
+        place_slots(lax.rem(base + half + j, n) * S, far_ref, (j,))
     for ref, step in ((left_ref, n - 1), (right_ref, 1)):
-        place_slots(lax.rem(me + step, n) * S + S2, ref, (), 0, S2 * PACK)
+        place_slots(lax.rem(me + step, n) * S + S2, ref, ())
 
     def row_body(r, carry):
         picked = jnp.concatenate(
             [wide[pl.ds(pl.multiple_of(code_ref[k, r] * B, B), B), :] for k in range(span)], axis=0
         )
-        block = jnp.dot(coupling_ref[r], picked, preferred_element_type=jnp.float32)
+        block = jnp.dot(coupling_ref[r, :, : span * B], picked, preferred_element_type=jnp.float32)
         ap[pl.ds(pl.multiple_of(r * B, B), B), :] = block.astype(BF16)
         return carry
 
@@ -195,6 +194,9 @@
     def shape(*dims, dtype=BF16):
         return jax.ShapeDtypeStruct(dims, dtype)
 
+    def exchange(x):
+        return lax.all_to_all(x, "row", split_axis=0, concat_axis=0, tiled=True, axis_index_groups=halves)
+
     def ring(x, step):
         return lax.ppermute(x, "row", [(i, (i + step) % n) for i in range(n)])
 
@@ -202,36 +204,38 @@
     far_flat = ring(flat, half)
     far_ints = ring(jnp.concatenate([send_rows, index], axis=1), half)
     edge = shape(S2 * PACK + 8, LANES)
-    own, left, right = call(
+    blocks = shape(half, S2 * PACK + 8, LANES)
+    own, near, left, right = call(
         functools.partial(own_kernel, n),
-        [shape(rows * PACK + rows, LANES), edge, edge],
+        [shape(rows * PACK + rows, LANES), blocks, edge, edge],
         [unpacked],
         (send_rows, index, flat),
         2,
         "own",
     )
+    near = exchange(near)
     from_right, from_left = ring(left, n - 1), ring(right, 1)
     panels = [own] + [
         lax.ppermute(own, "col", [(i, (i + j) % col_size) for i in range(col_size)])
         for j in range(1, col_size)
     ]
-    far_flat, far_ints, from_left, from_right = lax.optimization_barrier(
-        (far_flat, far_ints, from_left, from_right)
-    )
-    out = call(
-        functools.partial(pack_kernel, n),
-        shape(half, 2 * S2 * PACK + 8, LANES),
-        [unpacked, pltpu.VMEM((2 * rows * PACK, LANES), BF16)],
-        (send_rows, index, far_ints, own, far_flat),
-        3,
-        "pack",
-    )
-    out, a_tiles = lax.optimization_barrier((out, a_tiles))
-    ghosts = lax.all_to_all(out, "row", split_axis=0, concat_axis=0, tiled=True, axis_index_groups=halves)
+    far = call(
+        functools.partial(far_kernel, n),
+        blocks,
+        [unpacked, pltpu.VMEM((rows * PACK, LANES), BF16)],
+        (far_ints, far_flat),
+        1,
+        "far",
+        10**13,
+    )
+    far, near, from_left, from_right, a_tiles = lax.optimization_barrier(
+        (far, near, from_left, from_right, a_tiles)
+    )
+    far = exchange(far)
     coupling = call(
         coupling_kernel,
-        shape(rows, B, span * B),
-        [pltpu.VMEM((2, rows, PACK, LANES), f32)],
+        shape(rows, B, pl.cdiv(span, 2) * LANES),
+        [pltpu.VMEM((2, rows, PACK, 2 * LANES), f32)],
         (a_tiles.transpose(1, 0, 2),),
         0,
         "coupling",
@@ -250,7 +254,7 @@
         functools.partial(product_kernel, n),
         shape(col_size * CP * B, CP * B, dtype=f32),
         [pltpu.VMEM(((rows + n * S) * B, LANES), BF16), pltpu.VMEM((rows * B, CP * B), BF16)],
-        (neighbors.T, ghosts, from_left, from_right, own, coupling, restrict),
+        (neighbors.T, near, far, from_left, from_right, own, coupling, restrict),
         1,
         "product",
         2 * 10**8,

time: 43.2 us -> 46.6 us (1.079)
  starting transfers between devices: 13.3 us -> 18.5 us
  waiting for transfers between devices: 9.53 us -> 6.17 us
  Pallas kernels: 7.03 us -> 7.88 us
  blocking collectives: 11.5 us -> 12 us
    all_to_all x1 -> x2, starting transfers between devices: 3.54 us -> 8.15 us  [exchange(): lax.all_to_all(x, 'row', split_axis=0, concat_axis=0, tiled=True, axis_in...]
    ppermute x4, waiting for transfers between devices: 4.47 us -> 2.05 us  [ring(): return lax.ppermute(x, 'row', [(i, (i + step) % n) for i in range(n)])]
    all_to_all x1 -> x2, waiting for transfers between devices: 5.06 us -> 2.78 us  [exchange(): lax.all_to_all(x, 'row', split_axis=0, concat_axis=0, tiled=True, axis_in...]
    ppermute x1, waiting for transfers between devices: 0.01 us -> 1.34 us  [shards(): lax.ppermute(own, 'col', [(i, (i + j) % col_size) for i in range(col_size)])]
    pallas_call x5, Pallas kernels: 7.03 us -> 7.88 us  [call(): pl.pallas_call(body, out_shape=out_shape, in_specs=[SMEM] * smem + [VMEM]...]
    ppermute x4, starting transfers between devices: 9.71 us -> 10.3 us  [ring(): return lax.ppermute(x, 'row', [(i, (i + step) % n) for i in range(n)])]
    all_to_all x1, blocking collectives: 11.5 us -> 12 us  [shards(): lax.all_to_all(partial.reshape(n, share, CP * B), 'row', split_axis=0, co...]
  transfers between devices with their start and end apart: 6 -> 7, of which waited for: 2 -> 3; matrix products, arithmetic and copies ran while one was open for 0% -> 0% of each run, Pallas kernels for 8% -> 12%
where the time goes in v2:
time: 46.6 us; the launch traced here: 46.2 us
  starting transfers between devices  18.5 us (40%)
  blocking collectives  12 us (26%)
  Pallas kernels  7.88 us (17%)
  waiting for transfers between devices  6.17 us (13%)
  local copies, waits for them, and re-layouts  0.92 us (2%)
  other arithmetic  0.62 us (1%)
    all_to_all x1, blocking collectives, shards(): lax.all_to_all(partial.reshape(n, share, CP * B), 'row', split_axis=0, co...  12 us
    ppermute x4, starting transfers between devices, ring(): return lax.ppermute(x, 'row', [(i, (i + step) % n) for i in range(n)])  10.3 us
    all_to_all x2, starting transfers between devices, exchange(): lax.all_to_all(x, 'row', split_axis=0, concat_axis=0, tiled=True, axis_in...  8.15 us
    pallas_call x5, Pallas kernels, call(): pl.pallas_call(body, out_shape=out_shape, in_specs=[SMEM] * smem + [VMEM]...  7.88 us
    all_to_all x2, waiting for transfers between devices, exchange(): lax.all_to_all(x, 'row', split_axis=0, concat_axis=0, tiled=True, axis_in...  2.78 us
    ppermute x4, waiting for transfers between devices, ring(): return lax.ppermute(x, 'row', [(i, (i + step) % n) for i in range(n)])  2.05 us
    ppermute x1, waiting for transfers between devices, shards(): lax.ppermute(own, 'col', [(i, (i + j) % col_size) for i in range(col_size)])  1.34 us
  transfers between devices with their start and end apart: 7, of which 3 were waited for; matrix products, arithmetic and copies ran while one was open for 0% of the time, Pallas kernels for 12%

profile of v2, /device:TPU:0, one launch (start us, length us, event | category | flops | bytes accessed | tf_op | source)
XLA Modules:
  0.0 46.2 jit_solution(18147987236915221315)
XLA Ops:
  0.0 0.0 copy-start.2
  0.0 0.0 copy-start.3
  0.0 4.0 %collective-permute-start.1 = (bf16[16,4096]{1,0:T(8,128)(2,1)}, bf16[16,4096]{1,0:T(8,128)(2,1)S(1)}, u32[]{:S(2)}, u32[]{:S(2)}) collective-permute-start(bf16[16,4096]{1,0:T(8,128)(2,1)} %bitcast.6), channel_id=1, source_target_pairs={{0,16},{2,18},{4,20},{6,22},{8,24},{10,26},{12,28},{14,30},{16,0},... | collective-permute-start | bytes 393224 | tf_op jit(solution)/shard_map/ppermute | solution.py:201
  4.0 0.0 copy-done.2
  4.0 0.0 copy-done.3
  4.1 0.7 %collective-permute-start = (s32[1,144]{1,0:T(1,128)S(1)}, s32[1,144]{1,0:T(1,128)S(1)}, u32[]{:S(2)}, u32[]{:S(2)}) collective-permute-start(s32[1,144]{1,0:T(1,128)S(1)} %pad_add_fusion), channel_id=1, source_target_pairs={{0,16},{2,18},{4,20},{6,22},{8,24},{10,26},{12,28},{14,30},{16,0},... | collective-permute-start | bytes 1736 | tf_op jit(solution)/shard_map/ppermute | solution.py:201
  4.7 0.0 copy-start
  4.7 0.9 %copy-done = bf16[16,1,4096]{2,0,1:T(8,128)(2,1)S(1)} copy-done((bf16[16,1,4096]{2,0,1:T(8,128)(2,1)S(1)}, bf16[16,1,4096]{2,0,1:T(8,128)(2,1)}, u32[]{:S(2)}) %copy-start) | copy-done | bytes 131096
  5.6 1.6 %own.1 = (bf16[528,128]{1,0:T(8,128)(2,1)S(1)}, bf16[8,136,128]{2,1,0:T(8,128)(2,1)}, bf16[136,128]{1,0:T(8,128)(2,1)}, bf16[136,128]{1,0:T(8,128)(2,1)}) custom-call(s32[1,128]{1,0:T(1,128)S(1)} %copy-done.2, s32[1,16]{1,0:T(1,128)S(1)} %bitcast.10, bf16[16,4096]{1,0:T(8,128)(2,1)S(1)} %bitcast.7), custom_call_target="tpu_custom_call" | custom-call | flops 10000000 | bytes 1048576 | tf_op jit(solution)/shard_map/own/pallas_call | solution.py:183
  7.3 4.7 %all-to-all-start = ((bf16[8,136,128]{2,1,0:T(8,128)(2,1)}), bf16[8,136,128]{2,1,0:T(8,128)(2,1)}, u32[]{:S(2)}, u32[]{:S(2)}) async-start(bf16[8,136,128]{2,1,0:T(8,128)(2,1)} %get-tuple-element.14), calls=%async_computation | async-start | bytes 557056 | tf_op jit(solution)/shard_map/all_to_all | solution.py:198
  12.0 2.0 %collective-permute-start.2 = (bf16[136,128]{1,0:T(8,128)(2,1)}, bf16[136,128]{1,0:T(8,128)(2,1)}, u32[]{:S(2)}, u32[]{:S(2)}) collective-permute-start(bf16[136,128]{1,0:T(8,128)(2,1)} %get-tuple-element.15), channel_id=1, source_target_pairs={{0,2},{2,4},{4,6},{6,8},{8,10},{10,12},{12,14},{14,16},{16,18},{18... | collective-permute-start | bytes 104456 | tf_op jit(solution)/shard_map/ppermute | solution.py:201
  14.0 3.6 %collective-permute-start.3 = (bf16[136,128]{1,0:T(8,128)(2,1)}, bf16[136,128]{1,0:T(8,128)(2,1)}, u32[]{:S(2)}, u32[]{:S(2)}) collective-permute-start(bf16[136,128]{1,0:T(8,128)(2,1)} %get-tuple-element.16), channel_id=1, source_target_pairs={{0,30},{2,0},{4,2},{6,4},{8,6},{10,8},{12,10},{14,12},{16,14},{18,... | collective-permute-start | bytes 104456 | tf_op jit(solution)/shard_map/ppermute | solution.py:201
  17.6 0.0 collective-permute-done.far_ref
  17.6 0.0 collective-permute-done.1.flat_ref
  17.6 1.6 %far.1 = bf16[8,136,128]{2,1,0:T(8,128)(2,1)} custom-call(s32[1,144]{1,0:T(1,128)S(1)} %collective-permute-done.far_ref, bf16[16,4096]{1,0:T(8,128)(2,1)S(1)} %collective-permute-done.1.flat_ref), custom_call_target="tpu_custom_call" | custom-call | flops 9999999827968 | bytes 1048576 | tf_op jit(solution)/shard_map/far/pallas_call | solution.py:183
  19.3 0.0 copy-start.4
  19.3 2.0 %collective-permute-done.2.left_ref = bf16[136,128]{1,0:T(8,128)(2,1)} collective-permute-done((bf16[136,128]{1,0:T(8,128)(2,1)}, bf16[136,128]{1,0:T(8,128)(2,1)}, u32[]{:S(2)}, u32[]{:S(2)}) %collective-permute-start.2) | collective-permute-done | bytes 34848 | tf_op jit(solution)/shard_map/ppermute | solution.py:201
  21.3 0.0 collective-permute-done.3.right_ref
  21.3 0.0 all-to-all-done.near_ref
  21.3 3.4 %all-to-all-start.1 = ((bf16[8,136,128]{2,1,0:T(8,128)(2,1)}), bf16[8,136,128]{2,1,0:T(8,128)(2,1)S(1)}, u32[]{:S(2)}, u32[]{:S(2)}) async-start(bf16[8,136,128]{2,1,0:T(8,128)(2,1)} %far.1), calls=%async_computation.1 | async-start | bytes 557056 | tf_op jit(solution)/shard_map/all_to_all | solution.py:198
  24.7 0.1 collective-permute-start.4
  24.8 1.3 %collective-permute-done.4.refs_1_ = bf16[528,128]{1,0:T(8,128)(2,1)S(1)} collective-permute-done((bf16[528,128]{1,0:T(8,128)(2,1)S(1)}, bf16[528,128]{1,0:T(8,128)(2,1)S(1)}, u32[]{:S(2)}, u32[]{:S(2)}) %collective-permute-start.4) | collective-permute-done | bytes 135200 | tf_op jit(solution)/shard_map/ppermute | solution.py:219
  26.2 0.3 restrict.1.restrict_ref
  26.5 0.0 copy-done.4
  26.5 0.0 copy-start.1
  26.5 2.1 %coupling.1.coupling_ref = bf16[16,64,512]{2,1,0:T(8,128)(2,1)S(1)} custom-call(bf16[7,16,4096]{2,1,0:T(8,128)(2,1)S(1)} %bitcast.11), custom_call_target="tpu_custom_call" | custom-call | flops 2000000000 | bytes 1048576 | tf_op jit(solution)/shard_map/coupling/pallas_call | solution.py:183
  28.6 2.8 %all-to-all-done.1.far_ref = bf16[8,136,128]{2,1,0:T(8,128)(2,1)S(1)} async-done(((bf16[8,136,128]{2,1,0:T(8,128)(2,1)}), bf16[8,136,128]{2,1,0:T(8,128)(2,1)S(1)}, u32[]{:S(2)}, u32[]{:S(2)}) %all-to-all-start.1) | async-done | bytes 278560 | tf_op jit(solution)/shard_map/all_to_all | solution.py:198
  31.4 0.0 copy-done.1
  31.4 2.2 %product.1 = f32[256,128]{1,0:T(8,128)S(1)} custom-call(s32[7,16]{1,0:T(8,128)S(1)} %bitcast.8, bf16[8,136,128]{2,1,0:T(8,128)(2,1)} %all-to-all-done.near_ref, bf16[8,136,128]{2,1,0:T(8,128)(2,1)S(1)} %all-to-all-done.1.far_ref, bf16[136,128]{1,0:T(8,128)(2,1)} %collective-permute-done.2.left_ref, bf16[136,128]{1,0:T(8,128)(2,1)} %collective-permute-done.3.right_ref, ...), custom_call_target="tpu_custom_call" | custom-call | flops 200000000 | bytes 1048576 | tf_op jit(solution)/shard_map/product/pallas_call | solution.py:183
  33.6 12.0 %all_to_all.15 = f32[16,16,128]{2,1,0:T(8,128)S(1)} all-to-all(f32[16,16,128]{2,1,0:T(8,128)S(1)} %bitcast.5), channel_id=1, replica_groups=mesh['row'=16,'col'=2] {'row'}, dimensions={0} | all-to-all | bytes 262144 | tf_op jit(solution)/shard_map/all_to_all | solution.py:263
  45.6 0.6 %reduce_sum.9 = f32[16,128]{1,0:T(8,128)} reduce(f32[16,16,128]{2,1,0:T(8,128)S(1)} %all_to_all.15, f32[]{:T(128)} %constant.0.clone.1), dimensions={0}, to_apply=%region_0.0 | reduce | flops 30720 | bytes 139268 | tf_op jit(solution)/shard_map/reduce_sum | solution.py:266
  (1 shorter events, 0.0 us)
Async XLA Ops:
  0.0 4.0 %copy-start.2 = (s32[1,128]{1,0:T(1,128)S(1)}, s32[1,128]{1,0:T(1,128)}, u32[]{:S(2)}) copy-start(s32[1,128]{1,0:T(1,128)} %send_ref.1) | copy-start | bytes 1540
  0.0 4.0 %copy-start.3 = (s32[16,1]{0,1:T(1,128)S(1)}, s32[16,1]{0,1:T(1,128)}, u32[]{:S(2)}) copy-start(s32[16,1]{0,1:T(1,128)} %param.9) | copy-start | bytes 196
  0.0 17.6 %collective-permute-start.1 = (bf16[16,4096]{1,0:T(8,128)(2,1)}, bf16[16,4096]{1,0:T(8,128)(2,1)S(1)}, u32[]{:S(2)}, u32[]{:S(2)}) collective-permute-start(bf16[16,4096]{1,0:T(8,128)(2,1)} %bitcast.6), channel_id=1, source_target_pairs={{0,16},{2,18},{4,20},{6,22},{8,24},{10,26},{12,28},{14,30},{16,0},... | collective-permute-start | bytes 393224 | tf_op jit(solution)/shard_map/ppermute | solution.py:201
  4.1 13.6 %collective-permute-start = (s32[1,144]{1,0:T(1,128)S(1)}, s32[1,144]{1,0:T(1,128)S(1)}, u32[]{:S(2)}, u32[]{:S(2)}) collective-permute-start(s32[1,144]{1,0:T(1,128)S(1)} %pad_add_fusion), channel_id=1, source_target_pairs={{0,16},{2,18},{4,20},{6,22},{8,24},{10,26},{12,28},{14,30},{16,0},... | collective-permute-start | bytes 1736 | tf_op jit(solution)/shard_map/ppermute | solution.py:201
  4.7 0.9 %copy-start = (bf16[16,1,4096]{2,0,1:T(8,128)(2,1)S(1)}, bf16[16,1,4096]{2,0,1:T(8,128)(2,1)}, u32[]{:S(2)}) copy-start(bf16[16,1,4096]{2,0,1:T(8,128)(2,1)} %param.8) | copy-start | bytes 393220
  7.3 14.0 %all-to-all-start = ((bf16[8,136,128]{2,1,0:T(8,128)(2,1)}), bf16[8,136,128]{2,1,0:T(8,128)(2,1)}, u32[]{:S(2)}, u32[]{:S(2)}) async-start(bf16[8,136,128]{2,1,0:T(8,128)(2,1)} %get-tuple-element.14), calls=%async_computation | async-start | bytes 557056 | tf_op jit(solution)/shard_map/all_to_all | solution.py:198
  12.0 9.3 %collective-permute-start.2 = (bf16[136,128]{1,0:T(8,128)(2,1)}, bf16[136,128]{1,0:T(8,128)(2,1)}, u32[]{:S(2)}, u32[]{:S(2)}) collective-permute-start(bf16[136,128]{1,0:T(8,128)(2,1)} %get-tuple-element.15), channel_id=1, source_target_pairs={{0,2},{2,4},{4,6},{6,8},{8,10},{10,12},{12,14},{14,16},{16,18},{18... | collective-permute-start | bytes 104456 | tf_op jit(solution)/shard_map/ppermute | solution.py:201
  14.0 7.3 %collective-permute-start.3 = (bf16[136,128]{1,0:T(8,128)(2,1)}, bf16[136,128]{1,0:T(8,128)(2,1)}, u32[]{:S(2)}, u32[]{:S(2)}) collective-permute-start(bf16[136,128]{1,0:T(8,128)(2,1)} %get-tuple-element.16), channel_id=1, source_target_pairs={{0,30},{2,0},{4,2},{6,4},{8,6},{10,8},{12,10},{14,12},{16,14},{18,... | collective-permute-start | bytes 104456 | tf_op jit(solution)/shard_map/ppermute | solution.py:201
  19.3 7.2 %copy-start.4 = (bf16[16,7,4096]{2,0,1:T(8,128)(2,1)S(1)}, bf16[16,7,4096]{2,0,1:T(8,128)(2,1)}, u32[]{:S(2)}) copy-start(bf16[16,7,4096]{2,0,1:T(8,128)(2,1)} %param.5) | copy-start | bytes 2752516
  21.3 10.1 %all-to-all-start.1 = ((bf16[8,136,128]{2,1,0:T(8,128)(2,1)}), bf16[8,136,128]{2,1,0:T(8,128)(2,1)S(1)}, u32[]{:S(2)}, u32[]{:S(2)}) async-start(bf16[8,136,128]{2,1,0:T(8,128)(2,1)} %far.1), calls=%async_computation.1 | async-start | bytes 557056 | tf_op jit(solution)/shard_map/all_to_all | solution.py:198
  24.7 1.4 %collective-permute-start.4 = (bf16[528,128]{1,0:T(8,128)(2,1)S(1)}, bf16[528,128]{1,0:T(8,128)(2,1)S(1)}, u32[]{:S(2)}, u32[]{:S(2)}) collective-permute-start(bf16[528,128]{1,0:T(8,128)(2,1)S(1)} %get-tuple-element.21.refs_0_.own_ref), channel_id=1, source_target_pairs={{0,1},{1,0},{2,3},{3,2},{4,5},{5,4},{6,7},{7,6},{8,9},{9,8},{10,11... | collective-permute-start | bytes 405512 | tf_op jit(solution)/shard_map/ppermute | solution.py:219
  26.5 4.9 %copy-start.1 = (s32[16,7]{0,1:T(8,128)S(1)}, s32[16,7]{0,1:T(8,128)}, u32[]{:S(2)}) copy-start(s32[16,7]{0,1:T(8,128)} %param.6) | copy-start | bytes 1348

commit v3 on v2

v3 whole, which is shorter than its diff:
```python
import functools

import jax
import jax.numpy as jnp
from jax import lax
from jax.experimental import pallas as pl
from jax.experimental.pallas import tpu as pltpu
from jax.sharding import PartitionSpec as P

B = 64
CP = 2
S = 8
S2 = 4
LANES = 128
PACK = B * B // LANES
BF16 = jnp.bfloat16
VMEM = pl.BlockSpec(memory_space=pltpu.VMEM)
SMEM = pl.BlockSpec(memory_space=pltpu.SMEM)
PARAMS = pltpu.CompilerParams(vmem_limit_bytes=40 * 2**20)


def unpack_rows(flat, scratch):
    for l in range(PACK):
        scratch[:, l, :] = flat[:, l * LANES : (l + 1) * LANES].astype(jnp.float32)


def swap_halves(x):
    return jnp.concatenate([x[:, B:], x[:, :B]], axis=1)


def turn_rows(flat, index_of, scratch, out, base):
    rows = scratch.shape[0]
    unpack_rows(flat, scratch)
    for r in range(rows):
        x = scratch[r]
        x = jnp.where(index_of(r) == 0, x, swap_halves(x))
        out[base + r * PACK : base + (r + 1) * PACK, :] = x.astype(BF16)


def mask_row(index, shape):
    lane = lax.broadcasted_iota(jnp.int32, shape, len(shape) - 1)
    return jnp.where((lane >= B) == (index != 0), 1.0, 0.0)


def widen(x, mask):
    return x * mask, swap_halves(x) * mask


def mask_table(index_of, rows):
    sub = lax.broadcasted_iota(jnp.int32, (rows, LANES), 0)
    table = jnp.zeros((rows, LANES), jnp.float32)
    for r in range(rows):
        table = jnp.where(sub == r, mask_row(index_of(r), (rows, LANES)), table)
    return table


def fill(ref, table, picks):
    marks = ref.shape[0] - len(picks) * PACK
    sub = lax.broadcasted_iota(jnp.int32, (marks, LANES), 0)
    mark = jnp.zeros((marks, LANES), jnp.float32)
    for s, (row, index) in enumerate(picks):
        ref[s * PACK : (s + 1) * PACK, :] = table[pl.ds(pl.multiple_of(row * PACK, PACK), PACK), :]
        mark = jnp.where(sub == s, mask_row(index, (marks, LANES)), mark)
    ref[len(picks) * PACK :, :] = mark.astype(BF16)


def beyond(n, me):
    half = n // 2
    low = lax.rem(me, half)
    return me + jnp.where((low == 0) | (low == half - 1), 0, 2 * lax.rem(me, 2) - 1)


def own_kernel(n, send_ref, index_ref, flat_ref, own_ref, pair_ref, edge_ref, restrict_ref, scratch):
    rows = flat_ref.shape[0]
    me = lax.axis_index("row")
    turn_rows(flat_ref, lambda r: index_ref[0, r], scratch, own_ref, 0)
    masks = mask_table(lambda r: index_ref[0, r], rows)
    own_ref[rows * PACK :, :] = masks.astype(BF16)

    def look(slot):
        row = send_ref[0, slot]
        return row, index_ref[0, row]

    fill(edge_ref, own_ref, [look(beyond(n, me) * S + s) for s in range(S2, S)])
    fill(pair_ref, own_ref, [look(lax.bitwise_xor(me, 1) * S + s) for s in range(S)])
    pieces = []
    for r in range(rows):
        x = own_ref[r * PACK : (r + 1) * PACK, :].astype(jnp.float32)
        pieces.extend(widen(x, masks[r : r + 1, :]))
    restrict_ref[...] = jnp.concatenate(pieces, axis=0).T.astype(BF16)


def coupling_kernel(a_ref, coupling_ref, scratch):
    span, rows, _ = a_ref.shape
    src = lax.broadcasted_iota(jnp.int32, (2 * LANES, 2 * LANES), 0)
    dst = lax.broadcasted_iota(jnp.int32, (2 * LANES, 2 * LANES), 1)
    odd, block, part = dst // LANES, lax.rem(dst // B, 2), lax.rem(dst, B)
    column = jnp.where(part < B // 2, 2 * part, 2 * part - B + 1)
    order = (src == block * LANES + odd * B + column).astype(BF16)
    for pair in range(pl.cdiv(span, 2)):
        blocks = range(2 * pair, min(2 * pair + 2, span))
        buffer = scratch.at[pair % 2]
        for k in blocks:
            unpack_rows(a_ref.at[k], buffer.at[:, :, pl.ds((k % 2) * LANES, LANES)])
        width = len(blocks) * LANES
        packed = buffer[:, :, :width].reshape(rows * PACK, width).astype(BF16)
        ordered = jnp.dot(packed, order[:width], preferred_element_type=jnp.float32).astype(BF16)
        lanes = pl.ds(pair * LANES, LANES)
        coupling_ref[:, :PACK, lanes] = ordered[:, :LANES].reshape(rows, PACK, LANES)
        coupling_ref[:, PACK:, lanes] = ordered[:, LANES:].reshape(rows, PACK, LANES)


def pack_kernel(n, steps, send_ref, index_ref, far_ref, own_ref, flat_ref, self_ref, *refs):
    rows = flat_ref.shape[0]
    out_refs, (scratch, table) = refs[: len(steps)], refs[len(steps) :]
    me = lax.axis_index("row")
    turn_rows(flat_ref, lambda r: far_ref[0, n * S + r], scratch, table, rows * PACK)
    table[: rows * PACK, :] = own_ref[: rows * PACK, :]

    def near_row(slot):
        row = send_ref[0, slot]
        return row, index_ref[0, row]

    def far_row(slot):
        row = far_ref[0, slot]
        return rows + row, far_ref[0, n * S + row]

    for step, ref in zip(steps, out_refs):
        first = lax.bitwise_xor(me, step) * S
        picks = [far_row(first + s) for s in range(S2)]
        if step > 1:
            picks += [near_row(first + s) for s in range(S2)]
        if step == n // 2 - 1:
            picks += [far_row(first + s) for s in range(S2, S)]
        fill(ref, table, picks)
    fill(self_ref, table, [far_row(me * S + s) for s in range(S2)])


def product_kernel(n, col_size, steps, code_ref, self_ref, pair_ref, edge_ref, *refs):
    message_refs, refs = refs[: len(steps)], refs[len(steps) :]
    own_ref, coupling_ref, *restrict_refs, out_ref, wide, ap = refs
    rows = coupling_ref.shape[0]
    span = code_ref.shape[0]
    me = lax.axis_index("row")

    def place(slot, tile, mask):
        even, odd = widen(tile, mask)
        to = pl.multiple_of(slot * B, B)
        wide[pl.ds(to, PACK), :] = even
        wide[pl.ds(pl.multiple_of(to + PACK, PACK), PACK), :] = odd

    def place_slots(ref, firsts):
        for i, first in enumerate(firsts):
            for s in range(S2):
                slot = i * S2 + s
                mask_at = len(firsts) * S2 * PACK + slot
                place(rows + first + s, ref[slot * PACK : (slot + 1) * PACK, :], ref[mask_at : mask_at + 1, :])

    for r in range(rows):
        place(r, own_ref[r * PACK : (r + 1) * PACK, :], own_ref[rows * PACK + r : rows * PACK + r + 1, :])
    place_slots(self_ref, [lax.bitwise_xor(me, n // 2) * S])
    near = lax.bitwise_xor(me, 1) * S
    place_slots(pair_ref, [near, near + S2])
    place_slots(edge_ref, [beyond(n, me) * S + S2])
    for ref, step in zip(message_refs, steps):
        near = lax.bitwise_xor(me, step)
        firsts = [lax.bitwise_xor(near, n // 2) * S]
        if step > 1:
            firsts.append(near * S)
        if step == n // 2 - 1:
            firsts.append(firsts[0] + S2)
        place_slots(ref, firsts)

    def row_body(r, carry):
        picked = jnp.concatenate(
            [wide[pl.ds(pl.multiple_of(code_ref[k, r] * B, B), B), :] for k in range(span)], axis=0
        )
        block = jnp.dot(coupling_ref[r, :, : span * B], picked, preferred_element_type=jnp.float32)
        ap[pl.ds(pl.multiple_of(r * B, B), B), :] = block.astype(BF16)
        return carry

    lax.fori_loop(0, rows, row_body, 0, unroll=8)
    mine = lax.axis_index("col")
    for j, restrict_ref in enumerate(restrict_refs):
        first = lax.rem(mine + col_size - j, col_size) * CP * B
        out_ref[pl.ds(pl.multiple_of(first, LANES), CP * B), :] = jnp.dot(
            restrict_ref[...], ap[...], preferred_element_type=jnp.float32
        )


def shards(n, col_size, a_tiles, neighbors, send_rows, p_tiles, p_index):
    rows, span = a_tiles.shape[0], a_tiles.shape[1]
    half = n // 2
    f32 = jnp.float32
    flat = p_tiles[:, 0, :]
    index = p_index.T

    def call(body, out_shape, scratch_shapes, operands, smem, name, flops=10**7):
        return pl.pallas_call(
            body,
            out_shape=out_shape,
            in_specs=[SMEM] * smem + [VMEM] * (len(operands) - smem),
            out_specs=jax.tree.map(lambda _: VMEM, out_shape),
            scratch_shapes=scratch_shapes,
            compiler_params=PARAMS,
            cost_estimate=pl.CostEstimate(flops=flops, bytes_accessed=2**20, transcendentals=0),
            name=name,
        )(*operands)

    def shape(*dims, dtype=BF16):
        return jax.ShapeDtypeStruct(dims, dtype)

    def message(slots):
        return shape(slots * PACK + (8 if slots <= 8 else 16), LANES)

    def swap(x, bits):
        return lax.ppermute(x, "row", [(i, i ^ bits) for i in range(n)])

    unpacked = pltpu.VMEM((rows, PACK, LANES), f32)
    far_flat = swap(flat, half)
    far_ints = swap(jnp.concatenate([send_rows, index], axis=1), half)
    own, pair, edge, restrict = call(
        functools.partial(own_kernel, n),
        [shape(rows * PACK + rows, LANES), message(S), message(S2), shape(CP * B, rows * B)],
        [unpacked],
        (send_rows, index, flat),
        2,
        "own",
    )
    pair = swap(pair, 1)
    edge = lax.ppermute(edge, "row", [(i, i + 2 * (i % 2) - 1) for i in range(n) if 0 < i % half < half - 1])
    restricts = [restrict] + [
        lax.ppermute(restrict, "col", [(i, (i + j) % col_size) for i in range(col_size)])
        for j in range(1, col_size)
    ]
    coupling = call(
        coupling_kernel,
        shape(rows, B, pl.cdiv(span, 2) * LANES),
        [pltpu.VMEM((2, rows, PACK, 2 * LANES), f32)],
        (a_tiles.transpose(1, 0, 2),),
        0,
        "coupling",
    )
    far_flat, far_ints, pair, edge, coupling = lax.optimization_barrier(
        (far_flat, far_ints, pair, edge, coupling)
    )
    steps = sorted(range(1, half), key=lambda d: (d == 1, -d.bit_count(), 1 - d % 2, -d))
    self_part, *out = call(
        functools.partial(pack_kernel, n, steps),
        [message(S2)] + [message((3 if step == half - 1 else 1 + (step > 1)) * S2) for step in steps],
        [unpacked, pltpu.VMEM((2 * rows * PACK, LANES), BF16)],
        (send_rows, index, far_ints, own, far_flat),
        3,
        "pack",
    )
    messages = [swap(x, step) for x, step in zip(out, steps)]
    partial = call(
        functools.partial(product_kernel, n, col_size, steps),
        shape(col_size * CP * B, CP * B, dtype=f32),
        [pltpu.VMEM(((rows + n * S) * B, LANES), BF16), pltpu.VMEM((rows * B, CP * B), BF16)],
        (neighbors.T, self_part, pair, edge, *messages, own, coupling, *restricts),
        1,
        "product",
        2 * 10**8,
    )
    share = col_size * CP * B // n
    parts = lax.all_to_all(
        partial.reshape(n, share, CP * B), "row", split_axis=0, concat_axis=0, tiled=True
    )
    return jnp.sum(parts, axis=0)


def solution(mesh):
    in_specs = (
        P("row", None, None),
        P("row", None),
        P("row", None),
        P("row", "col", None),
        P("row", "col"),
    )
    out_specs = P("row", "col")
    body = functools.partial(shards, mesh.shape["row"], mesh.shape["col"])
    return jax.shard_map(body, mesh=mesh, in_specs=in_specs, out_specs=out_specs, check_vma=False)
```

time: 46.6 us -> 46.6 us (level)
  Pallas kernels: 7.88 us -> 5.99 us
  local copies, waits for them, and re-layouts: 0.92 us -> 2.12 us
  starting transfers between devices: 18.5 us -> 19.6 us
  waiting for transfers between devices: 6.17 us -> 5.52 us
  blocking collectives: 12 us -> 12.5 us
    ppermute x5 -> x12, starting transfers between devices: 10.4 us -> 19.6 us  [the longest x10 18.9 us: swap(): return lax.ppermute(x, 'row', [(i, i ^ bits) for i in range(n)])]
    all_to_all x2 -> x0, starting transfers between devices: 8.15 us -> none  [exchange(): lax.all_to_all(x, 'row', split_axis=0, concat_axis=0, tiled=True, axis_in...]
    all_to_all x2 -> x0, waiting for transfers between devices: 2.78 us -> none  [exchange(): lax.all_to_all(x, 'row', split_axis=0, concat_axis=0, tiled=True, axis_in...]
    ppermute x5 -> x12, waiting for transfers between devices: 3.39 us -> 5.52 us  [the longest x10 5.51 us: swap(): return lax.ppermute(x, 'row', [(i, i ^ bits) for i in range(n)])]
    pallas_call x5 -> x4, Pallas kernels: 7.88 us -> 5.99 us  [call(): pl.pallas_call(body, out_shape=out_shape, in_specs=[SMEM] * smem + [VMEM]...]
    unnamed x10, local copies, waits for them, and re-layouts: 0.92 us -> 2.12 us
    all_to_all x1, blocking collectives: 12 us -> 12.5 us  [shards(): lax.all_to_all(partial.reshape(n, share, CP * B), 'row', split_axis=0, co...]
  transfers between devices with their start and end apart: 7 -> 12, of which waited for: 3 -> 5; matrix products, arithmetic and copies ran while one was open for 0% -> 0% of each run, Pallas kernels for 12% -> 9%
where the time goes in v3:
time: 46.6 us; the launch traced here: 46.4 us
  starting transfers between devices  19.6 us (42%)
  blocking collectives  12.5 us (27%)
  Pallas kernels  5.99 us (13%)
  waiting for transfers between devices  5.52 us (12%)
  local copies, waits for them, and re-layouts  2.12 us (5%)
  other arithmetic  0.62 us (1%)
    ppermute x10, starting transfers between devices, swap(): return lax.ppermute(x, 'row', [(i, i ^ bits) for i in range(n)])  18.9 us
    all_to_all x1, blocking collectives, shards(): lax.all_to_all(partial.reshape(n, share, CP * B), 'row', split_axis=0, co...  12.5 us
    pallas_call x4, Pallas kernels, call(): pl.pallas_call(body, out_shape=out_shape, in_specs=[SMEM] * smem + [VMEM]...  5.99 us
    ppermute x10, waiting for transfers between devices, swap(): return lax.ppermute(x, 'row', [(i, i ^ bits) for i in range(n)])  5.51 us
    unnamed x10, local copies, waits for them, and re-layouts  2.12 us
  transfers between devices with their start and end apart: 12, of which 5 were waited for; matrix products, arithmetic and copies ran while one was open for 0% of the time, Pallas kernels for 9%

profile of v3, /device:TPU:0, one launch (start us, length us, event | category | flops | bytes accessed | tf_op | source)
XLA Modules:
  0.0 46.4 jit_solution(12773823677395104494)
XLA Ops:
  0.0 4.0 %collective-permute-start = (bf16[16,4096]{1,0:T(8,128)(2,1)}, bf16[16,4096]{1,0:T(8,128)(2,1)S(1)}, u32[]{:S(2)}, u32[]{:S(2)}) collective-permute-start(bf16[16,4096]{1,0:T(8,128)(2,1)} %bitcast.7), channel_id=1, source_target_pairs={{0,16},{2,18},{4,20},{6,22},{8,24},{10,26},{12,28},{14,30},{16,0},... | collective-permute-start | bytes 393224 | tf_op jit(solution)/shard_map/ppermute | solution.py:217
  4.0 0.9 %copy-done.1 = bf16[16,1,4096]{2,0,1:T(8,128)(2,1)S(1)} copy-done((bf16[16,1,4096]{2,0,1:T(8,128)(2,1)S(1)}, bf16[16,1,4096]{2,0,1:T(8,128)(2,1)}, u32[]{:S(2)}) %copy-start.1) | copy-done | bytes 131096
  5.0 1.1 %own.1 = (bf16[528,128]{1,0:T(8,128)(2,1)S(1)}, bf16[264,128]{1,0:T(8,128)(2,1)S(1)}, bf16[136,128]{1,0:T(8,128)(2,1)S(1)}, bf16[128,1024]{1,0:T(8,128)(2,1)S(1)}) custom-call(s32[1,128]{1,0:T(1,128)S(1)} %copy-done.2, s32[1,16]{1,0:T(1,128)S(1)} %bitcast.9, bf16[16,4096]{1,0:T(8,128)(2,1)S(1)} %bitcast.8), custom_call_target="tpu_custom_call" | custom-call | flops 10000000 | bytes 1048576 | tf_op jit(solution)/shard_map/own/pallas_call | solution.py:199
  6.1 0.1 collective-permute-start.11
  6.1 1.6 %collective-permute-start.2 = (bf16[264,128]{1,0:T(8,128)(2,1)S(1)}, bf16[264,128]{1,0:T(8,128)(2,1)S(1)}, u32[]{:S(2)}, u32[]{:S(2)}) collective-permute-start(bf16[264,128]{1,0:T(8,128)(2,1)S(1)} %get-tuple-element.22), channel_id=1, source_target_pairs={{0,2},{2,0},{4,6},{6,4},{8,10},{10,8},{12,14},{14,12},{16,18},{18,... | collective-permute-start | bytes 202760 | tf_op jit(solution)/shard_map/ppermute | solution.py:217
  7.7 0.7 %collective-permute-start.3 = (bf16[136,128]{1,0:T(8,128)(2,1)S(1)}, bf16[136,128]{1,0:T(8,128)(2,1)S(1)}, u32[]{:S(2)}, u32[]{:S(2)}) collective-permute-start(bf16[136,128]{1,0:T(8,128)(2,1)S(1)} %get-tuple-element.23), channel_id=1, source_target_pairs={{2,4},{4,2},{6,8},{8,6},{10,12},{12,10},{18,20},{20,18},{22,24},{2... | collective-permute-start | bytes 104456 | tf_op jit(solution)/shard_map/ppermute | solution.py:231
  8.4 0.7 %collective-permute-start.1 = (s32[1,144]{1,0:T(1,128)S(1)}, s32[1,144]{1,0:T(1,128)S(1)}, u32[]{:S(2)}, u32[]{:S(2)}) collective-permute-start(s32[1,144]{1,0:T(1,128)S(1)} %pad_add_fusion), channel_id=1, source_target_pairs={{0,16},{2,18},{4,20},{6,22},{8,24},{10,26},{12,28},{14,30},{16,0},... | collective-permute-start | bytes 1736 | tf_op jit(solution)/shard_map/ppermute | solution.py:217
  9.1 1.2 %copy-done = bf16[16,7,4096]{2,0,1:T(8,128)(2,1)S(1)} copy-done((bf16[16,7,4096]{2,0,1:T(8,128)(2,1)S(1)}, bf16[16,7,4096]{2,0,1:T(8,128)(2,1)}, u32[]{:S(2)}) %copy-start) | copy-done | bytes 917528
  10.2 2.1 %coupling.1.refs_8_ = bf16[16,64,512]{2,1,0:T(8,128)(2,1)S(1)} custom-call(bf16[7,16,4096]{2,1,0:T(8,128)(2,1)S(1)} %bitcast.5), custom_call_target="tpu_custom_call" | custom-call | flops 10000000 | bytes 1048576 | tf_op jit(solution)/shard_map/coupling/pallas_call | solution.py:199
  12.3 0.5 %collective-permute-done.1.far_ref = s32[1,144]{1,0:T(1,128)S(1)} collective-permute-done((s32[1,144]{1,0:T(1,128)S(1)}, s32[1,144]{1,0:T(1,128)S(1)}, u32[]{:S(2)}, u32[]{:S(2)}) %collective-permute-start.1) | collective-permute-done | bytes 608 | tf_op jit(solution)/shard_map/ppermute | solution.py:217
  12.9 0.0 collective-permute-done.3.edge_ref
  12.9 0.0 collective-permute-done.2.pair_ref
  12.9 0.0 collective-permute-done.flat_ref
  12.9 1.0 %pack.1 = (bf16[136,128]{1,0:T(8,128)(2,1)S(1)}, bf16[400,128]{1,0:T(8,128)(2,1)S(1)}, bf16[264,128]{1,0:T(8,128)(2,1)S(1)}, bf16[264,128]{1,0:T(8,128)(2,1)S(1)...) custom-call(s32[1,128]{1,0:T(1,128)S(1)} %copy-done.2, ...), custom_call_target="tpu_custom_call" | custom-call | flops 10000000 | bytes 1048576 | tf_op jit(solution)/shard_map/pack/pallas_call | solution.py:199
  13.9 5.3 %collective-permute-start.5 = (bf16[264,128]{1,0:T(8,128)(2,1)S(1)}, bf16[264,128]{1,0:T(8,128)(2,1)S(1)}, u32[]{:S(2)}, u32[]{:S(2)}) collective-permute-start(bf16[264,128]{1,0:T(8,128)(2,1)S(1)} %get-tuple-element.31), channel_id=1, source_target_pairs={{0,10},{2,8},{4,14},{6,12},{8,2},{10,0},{12,6},{14,4},{16,26},{18,... | collective-permute-start | bytes 202760 | tf_op jit(solution)/shard_map/ppermute | solution.py:217
  19.2 0.5 %collective-permute-start.6 = (bf16[264,128]{1,0:T(8,128)(2,1)S(1)}, bf16[264,128]{1,0:T(8,128)(2,1)S(1)}, u32[]{:S(2)}, u32[]{:S(2)}) collective-permute-start(bf16[264,128]{1,0:T(8,128)(2,1)S(1)} %get-tuple-element.32), channel_id=1, source_target_pairs={{0,6},{2,4},{4,2},{6,0},{8,14},{10,12},{12,10},{14,8},{16,22},{18,... | collective-permute-start | bytes 202760 | tf_op jit(solution)/shard_map/ppermute | solution.py:217
  19.7 0.0 collective-permute-start.10
  19.7 2.5 %collective-permute-start.4 = (bf16[400,128]{1,0:T(8,128)(2,1)S(1)}, bf16[400,128]{1,0:T(8,128)(2,1)S(1)}, u32[]{:S(2)}, u32[]{:S(2)}) collective-permute-start(bf16[400,128]{1,0:T(8,128)(2,1)S(1)} %get-tuple-element.30), channel_id=1, source_target_pairs={{0,14},{2,12},{4,10},{6,8},{8,6},{10,4},{12,2},{14,0},{16,30},{18,... | collective-permute-start | bytes 307208 | tf_op jit(solution)/shard_map/ppermute | solution.py:217
  22.2 1.4 %collective-permute-done.10.refs_6_ = bf16[136,128]{1,0:T(8,128)(2,1)S(1)} collective-permute-done((bf16[136,128]{1,0:T(8,128)(2,1)S(1)}, bf16[136,128]{1,0:T(8,128)(2,1)S(1)}, u32[]{:S(2)}, u32[]{:S(2)}) %collective-permute-start.10) | collective-permute-done | bytes 34848 | tf_op jit(solution)/shard_map/ppermute | solution.py:217
  23.6 1.6 %collective-permute-start.7 = (bf16[264,128]{1,0:T(8,128)(2,1)S(1)}, bf16[264,128]{1,0:T(8,128)(2,1)S(1)}, u32[]{:S(2)}, u32[]{:S(2)}) collective-permute-start(bf16[264,128]{1,0:T(8,128)(2,1)S(1)} %get-tuple-element.33), channel_id=1, source_target_pairs={{0,12},{2,14},{4,8},{6,10},{8,4},{10,6},{12,0},{14,2},{16,28},{18,... | collective-permute-start | bytes 202760 | tf_op jit(solution)/shard_map/ppermute | solution.py:217
  25.2 0.0 collective-permute-done.5.refs_1_
  25.2 1.9 %collective-permute-start.8 = (bf16[264,128]{1,0:T(8,128)(2,1)S(1)}, bf16[264,128]{1,0:T(8,128)(2,1)S(1)}, u32[]{:S(2)}, u32[]{:S(2)}) collective-permute-start(bf16[264,128]{1,0:T(8,128)(2,1)S(1)} %get-tuple-element.34), channel_id=1, source_target_pairs={{0,8},{2,10},{4,12},{6,14},{8,0},{10,2},{12,4},{14,6},{16,24},{18,... | collective-permute-start | bytes 202760 | tf_op jit(solution)/shard_map/ppermute | solution.py:217
  27.2 0.0 collective-permute-done.6.refs_2_
  27.2 0.7 %collective-permute-start.9 = (bf16[264,128]{1,0:T(8,128)(2,1)S(1)}, bf16[264,128]{1,0:T(8,128)(2,1)S(1)}, u32[]{:S(2)}, u32[]{:S(2)}) collective-permute-start(bf16[264,128]{1,0:T(8,128)(2,1)S(1)} %get-tuple-element.35), channel_id=1, source_target_pairs={{0,4},{2,6},{4,0},{6,2},{8,12},{10,14},{12,8},{14,10},{16,20},{18,... | collective-permute-start | bytes 202760 | tf_op jit(solution)/shard_map/ppermute | solution.py:217
  27.9 1.0 %collective-permute-done.7.refs_3_ = bf16[264,128]{1,0:T(8,128)(2,1)S(1)} collective-permute-done((bf16[264,128]{1,0:T(8,128)(2,1)S(1)}, bf16[264,128]{1,0:T(8,128)(2,1)S(1)}, u32[]{:S(2)}, u32[]{:S(2)}) %collective-permute-start.7) | collective-permute-done | bytes 67616 | tf_op jit(solution)/shard_map/ppermute | solution.py:217
  28.9 1.2 %collective-permute-done.8.refs_4_ = bf16[264,128]{1,0:T(8,128)(2,1)S(1)} collective-permute-done((bf16[264,128]{1,0:T(8,128)(2,1)S(1)}, bf16[264,128]{1,0:T(8,128)(2,1)S(1)}, u32[]{:S(2)}, u32[]{:S(2)}) %collective-permute-start.8) | collective-permute-done | bytes 67616 | tf_op jit(solution)/shard_map/ppermute | solution.py:217
  30.1 1.3 %collective-permute-done.9.refs_5_ = bf16[264,128]{1,0:T(8,128)(2,1)S(1)} collective-permute-done((bf16[264,128]{1,0:T(8,128)(2,1)S(1)}, bf16[264,128]{1,0:T(8,128)(2,1)S(1)}, u32[]{:S(2)}, u32[]{:S(2)}) %collective-permute-start.9) | collective-permute-done | bytes 67616 | tf_op jit(solution)/shard_map/ppermute | solution.py:217
  31.5 0.0 collective-permute-done.4.refs_0_
  31.5 0.0 collective-permute-done.11.refs_10_
  31.5 1.8 %product.1 = f32[256,128]{1,0:T(8,128)S(1)} custom-call(s32[7,16]{1,0:T(8,128)S(1)} %bitcast.12, bf16[136,128]{1,0:T(8,128)(2,1)S(1)} %get-tuple-element.27.self_ref, bf16[264,128]{1,0:T(8,128)(2,1)S(1)} %collective-permute-done.2.pair_ref, bf16[136,128]{1,0:T(8,128)(2,1)S(1)} %collective-permute-done.3.edge_ref, ...), custom_call_target="tpu_custom_call" | custom-call | flops 200000000 | bytes 1048576 | tf_op jit(solution)/shard_map/product/pallas_call | solution.py:199
  33.3 12.5 %all_to_all.5 = f32[16,16,128]{2,1,0:T(8,128)S(1)} all-to-all(f32[16,16,128]{2,1,0:T(8,128)S(1)} %bitcast.6), channel_id=1, replica_groups=mesh['row'=16,'col'=2] {'row'}, dimensions={0} | all-to-all | bytes 262144 | tf_op jit(solution)/shard_map/all_to_all | solution.py:267
  45.8 0.6 %reduce_sum.9 = f32[16,128]{1,0:T(8,128)} reduce(f32[16,16,128]{2,1,0:T(8,128)S(1)} %all_to_all.5, f32[]{:T(128)} %constant.0.clone.1), dimensions={0}, to_apply=%region_0.0 | reduce | flops 30720 | bytes 139268 | tf_op jit(solution)/shard_map/reduce_sum | solution.py:270
  (9 shorter events, 0.0 us)
Async XLA Ops:
  0.0 4.0 %copy-start.2 = (s32[1,128]{1,0:T(1,128)S(1)}, s32[1,128]{1,0:T(1,128)}, u32[]{:S(2)}) copy-start(s32[1,128]{1,0:T(1,128)} %send_ref.3) | copy-start | bytes 1540
  0.0 4.0 %copy-start.3 = (s32[16,1]{0,1:T(1,128)S(1)}, s32[16,1]{0,1:T(1,128)}, u32[]{:S(2)}) copy-start(s32[16,1]{0,1:T(1,128)} %param.9) | copy-start | bytes 196
  0.0 12.9 %collective-permute-start = (bf16[16,4096]{1,0:T(8,128)(2,1)}, bf16[16,4096]{1,0:T(8,128)(2,1)S(1)}, u32[]{:S(2)}, u32[]{:S(2)}) collective-permute-start(bf16[16,4096]{1,0:T(8,128)(2,1)} %bitcast.7), channel_id=1, source_target_pairs={{0,16},{2,18},{4,20},{6,22},{8,24},{10,26},{12,28},{14,30},{16,0},... | collective-permute-start | bytes 393224 | tf_op jit(solution)/shard_map/ppermute | solution.py:217
  4.0 0.9 %copy-start.1 = (bf16[16,1,4096]{2,0,1:T(8,128)(2,1)S(1)}, bf16[16,1,4096]{2,0,1:T(8,128)(2,1)}, u32[]{:S(2)}) copy-start(bf16[16,1,4096]{2,0,1:T(8,128)(2,1)} %param.8) | copy-start | bytes 393220
  6.1 25.4 %collective-permute-start.11 = (bf16[128,1024]{1,0:T(8,128)(2,1)S(1)}, bf16[128,1024]{1,0:T(8,128)(2,1)S(1)}, u32[]{:S(2)}, u32[]{:S(2)}) collective-permute-start(bf16[128,1024]{1,0:T(8,128)(2,1)S(1)} %get-tuple-element.38.refs_9_), channel_id=1, source_target_pairs={{0,1},{1,0},{2,3},{3,2},{4,5},{5,4},{6,7},{7,6},{8,9},{9,8},{10,11... | collective-permute-start | bytes 786440 | tf_op jit(solution)/shard_map/ppermute | solution.py:233
  6.1 6.8 %collective-permute-start.2 = (bf16[264,128]{1,0:T(8,128)(2,1)S(1)}, bf16[264,128]{1,0:T(8,128)(2,1)S(1)}, u32[]{:S(2)}, u32[]{:S(2)}) collective-permute-start(bf16[264,128]{1,0:T(8,128)(2,1)S(1)} %get-tuple-element.22), channel_id=1, source_target_pairs={{0,2},{2,0},{4,6},{6,4},{8,10},{10,8},{12,14},{14,12},{16,18},{18,... | collective-permute-start | bytes 202760 | tf_op jit(solution)/shard_map/ppermute | solution.py:217
  7.7 5.2 %collective-permute-start.3 = (bf16[136,128]{1,0:T(8,128)(2,1)S(1)}, bf16[136,128]{1,0:T(8,128)(2,1)S(1)}, u32[]{:S(2)}, u32[]{:S(2)}) collective-permute-start(bf16[136,128]{1,0:T(8,128)(2,1)S(1)} %get-tuple-element.23), channel_id=1, source_target_pairs={{2,4},{4,2},{6,8},{8,6},{10,12},{12,10},{18,20},{20,18},{22,24},{2... | collective-permute-start | bytes 104456 | tf_op jit(solution)/shard_map/ppermute | solution.py:231
  8.4 4.5 %collective-permute-start.1 = (s32[1,144]{1,0:T(1,128)S(1)}, s32[1,144]{1,0:T(1,128)S(1)}, u32[]{:S(2)}, u32[]{:S(2)}) collective-permute-start(s32[1,144]{1,0:T(1,128)S(1)} %pad_add_fusion), channel_id=1, source_target_pairs={{0,16},{2,18},{4,20},{6,22},{8,24},{10,26},{12,28},{14,30},{16,0},... | collective-permute-start | bytes 1736 | tf_op jit(solution)/shard_map/ppermute | solution.py:217
  9.1 1.2 %copy-start = (bf16[16,7,4096]{2,0,1:T(8,128)(2,1)S(1)}, bf16[16,7,4096]{2,0,1:T(8,128)(2,1)}, u32[]{:S(2)}) copy-start(bf16[16,7,4096]{2,0,1:T(8,128)(2,1)} %param.5) | copy-start | bytes 2752516
  13.9 11.3 %collective-permute-start.5 = (bf16[264,128]{1,0:T(8,128)(2,1)S(1)}, bf16[264,128]{1,0:T(8,128)(2,1)S(1)}, u32[]{:S(2)}, u32[]{:S(2)}) collective-permute-start(bf16[264,128]{1,0:T(8,128)(2,1)S(1)} %get-tuple-element.31), channel_id=1, source_target_pairs={{0,10},{2,8},{4,14},{6,12},{8,2},{10,0},{12,6},{14,4},{16,26},{18,... | collective-permute-start | bytes 202760 | tf_op jit(solution)/shard_map/ppermute | solution.py:217
  19.2 8.0 %collective-permute-start.6 = (bf16[264,128]{1,0:T(8,128)(2,1)S(1)}, bf16[264,128]{1,0:T(8,128)(2,1)S(1)}, u32[]{:S(2)}, u32[]{:S(2)}) collective-permute-start(bf16[264,128]{1,0:T(8,128)(2,1)S(1)} %get-tuple-element.32), channel_id=1, source_target_pairs={{0,6},{2,4},{4,2},{6,0},{8,14},{10,12},{12,10},{14,8},{16,22},{18,... | collective-permute-start | bytes 202760 | tf_op jit(solution)/shard_map/ppermute | solution.py:217
  19.7 3.9 %collective-permute-start.10 = (bf16[136,128]{1,0:T(8,128)(2,1)S(1)}, bf16[136,128]{1,0:T(8,128)(2,1)S(1)}, u32[]{:S(2)}, u32[]{:S(2)}) collective-permute-start(bf16[136,128]{1,0:T(8,128)(2,1)S(1)} %get-tuple-element.36), channel_id=1, source_target_pairs={{0,2},{2,0},{4,6},{6,4},{8,10},{10,8},{12,14},{14,12},{16,18},{18,... | collective-permute-start | bytes 104456 | tf_op jit(solution)/shard_map/ppermute | solution.py:217
  19.7 11.8 %collective-permute-start.4 = (bf16[400,128]{1,0:T(8,128)(2,1)S(1)}, bf16[400,128]{1,0:T(8,128)(2,1)S(1)}, u32[]{:S(2)}, u32[]{:S(2)}) collective-permute-start(bf16[400,128]{1,0:T(8,128)(2,1)S(1)} %get-tuple-element.30), channel_id=1, source_target_pairs={{0,14},{2,12},{4,10},{6,8},{8,6},{10,4},{12,2},{14,0},{16,30},{18,... | collective-permute-start | bytes 307208 | tf_op jit(solution)/shard_map/ppermute | solution.py:217
  23.6 7.8 %copy-start.4 = (s32[16,7]{0,1:T(8,128)S(1)}, s32[16,7]{0,1:T(8,128)}, u32[]{:S(2)}) copy-start(s32[16,7]{0,1:T(8,128)} %param.6) | copy-start | bytes 1348
  23.6 5.3 %collective-permute-start.7 = (bf16[264,128]{1,0:T(8,128)(2,1)S(1)}, bf16[264,128]{1,0:T(8,128)(2,1)S(1)}, u32[]{:S(2)}, u32[]{:S(2)}) collective-permute-start(bf16[264,128]{1,0:T(8,128)(2,1)S(1)} %get-tuple-element.33), channel_id=1, source_target_pairs={{0,12},{2,14},{4,8},{6,10},{8,4},{10,6},{12,0},{14,2},{16,28},{18,... | collective-permute-start | bytes 202760 | tf_op jit(solution)/shard_map/ppermute | solution.py:217
  25.2 4.9 %collective-permute-start.8 = (bf16[264,128]{1,0:T(8,128)(2,1)S(1)}, bf16[264,128]{1,0:T(8,128)(2,1)S(1)}, u32[]{:S(2)}, u32[]{:S(2)}) collective-permute-start(bf16[264,128]{1,0:T(8,128)(2,1)S(1)} %get-tuple-element.34), channel_id=1, source_target_pairs={{0,8},{2,10},{4,12},{6,14},{8,0},{10,2},{12,4},{14,6},{16,24},{18,... | collective-permute-start | bytes 202760 | tf_op jit(solution)/shard_map/ppermute | solution.py:217
  27.2 4.3 %collective-permute-start.9 = (bf16[264,128]{1,0:T(8,128)(2,1)S(1)}, bf16[264,128]{1,0:T(8,128)(2,1)S(1)}, u32[]{:S(2)}, u32[]{:S(2)}) collective-permute-start(bf16[264,128]{1,0:T(8,128)(2,1)S(1)} %get-tuple-element.35), channel_id=1, source_target_pairs={{0,4},{2,6},{4,0},{6,2},{8,12},{10,14},{12,8},{14,10},{16,20},{18,... | collective-permute-start | bytes 202760 | tf_op jit(solution)/shard_map/ppermute | solution.py:217

commit v4 on v3

--- a/solution.py
+++ b/solution.py
@@ -64,30 +64,29 @@
     ref[len(picks) * PACK :, :] = mark.astype(BF16)
 
 
-def beyond(n, me):
-    half = n // 2
-    low = lax.rem(me, half)
-    return me + jnp.where((low == 0) | (low == half - 1), 0, 2 * lax.rem(me, 2) - 1)
-
-
-def own_kernel(n, send_ref, index_ref, flat_ref, own_ref, pair_ref, edge_ref, restrict_ref, scratch):
-    rows = flat_ref.shape[0]
-    me = lax.axis_index("row")
-    turn_rows(flat_ref, lambda r: index_ref[0, r], scratch, own_ref, 0)
-    masks = mask_table(lambda r: index_ref[0, r], rows)
-    own_ref[rows * PACK :, :] = masks.astype(BF16)
-
-    def look(slot):
-        row = send_ref[0, slot]
-        return row, index_ref[0, row]
-
-    fill(edge_ref, own_ref, [look(beyond(n, me) * S + s) for s in range(S2, S)])
-    fill(pair_ref, own_ref, [look(lax.bitwise_xor(me, 1) * S + s) for s in range(S)])
-    pieces = []
-    for r in range(rows):
-        x = own_ref[r * PACK : (r + 1) * PACK, :].astype(jnp.float32)
-        pieces.extend(widen(x, masks[r : r + 1, :]))
-    restrict_ref[...] = jnp.concatenate(pieces, axis=0).T.astype(BF16)
+def prepare_kernel(col_size, *refs):
+    index_refs, refs = refs[:col_size], refs[col_size:]
+    flat_refs, refs = refs[:col_size], refs[col_size:]
+    own_ref, restrict_ref, scratch, table = refs
+    rows = flat_refs[0].shape[0]
+    mine = lax.axis_index("col")
+    for j, (index_ref, flat_ref) in enumerate(zip(index_refs, flat_refs)):
+        panel = lax.rem(mine + col_size - j, col_size)
+        turned = own_ref if j == 0 else table
+
+        def index_of(r, index_ref=index_ref):
+            return index_ref[0, r]
+
+        turn_rows(flat_ref, index_of, scratch, turned, 0)
+        masks = mask_table(index_of, rows)
+        if j == 0:
+            own_ref[rows * PACK :, :] = masks.astype(BF16)
+        pieces = []
+        for r in range(rows):
+            x = turned[r * PACK : (r + 1) * PACK, :].astype(jnp.float32)
+            pieces.extend(widen(x, masks[r : r + 1, :]))
+        wide = jnp.concatenate(pieces, axis=0)
+        restrict_ref[pl.ds(pl.multiple_of(panel * CP * B, LANES), CP * B), :] = wide.T.astype(BF16)
 
 
 def coupling_kernel(a_ref, coupling_ref, scratch):
@@ -110,6 +109,21 @@
         coupling_ref[:, PACK:, lanes] = ordered[:, LANES:].reshape(rows, PACK, LANES)
 
 
+def beside(n, p, q):
+    gap = lax.rem(p - q + n, n)
+    return (gap == 1) | (gap == n - 1)
+
+
+def has_edge(step):
+    return step & (step + 1) == 0
+
+
+def message_order(half):
+    edges = sorted((d for d in range(1, half) if has_edge(d)), reverse=True)
+    rest = sorted((d for d in range(1, half) if not has_edge(d)), key=lambda d: (-d.bit_count(), -(d % 2), d))
+    return rest[: len(rest) // 2] + edges + rest[len(rest) // 2 :]
+
+
 def pack_kernel(n, steps, send_ref, index_ref, far_ref, own_ref, flat_ref, self_ref, *refs):
     rows = flat_ref.shape[0]
     out_refs, (scratch, table) = refs[: len(steps)], refs[len(steps) :]
@@ -126,19 +140,21 @@
         return rows + row, far_ref[0, n * S + row]
 
     for step, ref in zip(steps, out_refs):
-        first = lax.bitwise_xor(me, step) * S
-        picks = [far_row(first + s) for s in range(S2)]
-        if step > 1:
-            picks += [near_row(first + s) for s in range(S2)]
-        if step == n // 2 - 1:
-            picks += [far_row(first + s) for s in range(S2, S)]
+        target = lax.bitwise_xor(me, step)
+        first = target * S
+        picks = [near_row(first + s) for s in range(S2)] + [far_row(first + s) for s in range(S2)]
+        if has_edge(step):
+            near = beside(n, me, target)
+            for s in range(S2, S):
+                pairs = zip(near_row(first + s), far_row(first + s))
+                picks.append(tuple(jnp.where(near, x, y) for x, y in pairs))
         fill(ref, table, picks)
     fill(self_ref, table, [far_row(me * S + s) for s in range(S2)])
 
 
-def product_kernel(n, col_size, steps, code_ref, self_ref, pair_ref, edge_ref, *refs):
+def product_kernel(n, steps, code_ref, self_ref, *refs):
     message_refs, refs = refs[: len(steps)], refs[len(steps) :]
-    own_ref, coupling_ref, *restrict_refs, out_ref, wide, ap = refs
+    own_ref, coupling_ref, restrict_ref, out_ref, wide, ap = refs
     rows = coupling_ref.shape[0]
     span = code_ref.shape[0]
     me = lax.axis_index("row")
@@ -159,16 +175,12 @@
     for r in range(rows):
         place(r, own_ref[r * PACK : (r + 1) * PACK, :], own_ref[rows * PACK + r : rows * PACK + r + 1, :])
     place_slots(self_ref, [lax.bitwise_xor(me, n // 2) * S])
-    near = lax.bitwise_xor(me, 1) * S
-    place_slots(pair_ref, [near, near + S2])
-    place_slots(edge_ref, [beyond(n, me) * S + S2])
     for ref, step in zip(message_refs, steps):
         near = lax.bitwise_xor(me, step)
-        firsts = [lax.bitwise_xor(near, n // 2) * S]
-        if step > 1:
-            firsts.append(near * S)
-        if step == n // 2 - 1:
-            firsts.append(firsts[0] + S2)
+        far = lax.bitwise_xor(near, n // 2)
+        firsts = [near * S, far * S]
+        if has_edge(step):
+            firsts.append(jnp.where(beside(n, me, near), near, far) * S + S2)
         place_slots(ref, firsts)
 
     def row_body(r, carry):
@@ -180,12 +192,7 @@
         return carry
 
     lax.fori_loop(0, rows, row_body, 0, unroll=8)
-    mine = lax.axis_index("col")
-    for j, restrict_ref in enumerate(restrict_refs):
-        first = lax.rem(mine + col_size - j, col_size) * CP * B
-        out_ref[pl.ds(pl.multiple_of(first, LANES), CP * B), :] = jnp.dot(
-            restrict_ref[...], ap[...], preferred_element_type=jnp.float32
-        )
+    out_ref[...] = jnp.dot(restrict_ref[...], ap[...], preferred_element_type=jnp.float32).astype(BF16)
 
 
 def shards(n, col_size, a_tiles, neighbors, send_rows, p_tiles, p_index):
@@ -219,20 +226,19 @@
     unpacked = pltpu.VMEM((rows, PACK, LANES), f32)
     far_flat = swap(flat, half)
     far_ints = swap(jnp.concatenate([send_rows, index], axis=1), half)
-    own, pair, edge, restrict = call(
-        functools.partial(own_kernel, n),
-        [shape(rows * PACK + rows, LANES), message(S), message(S2), shape(CP * B, rows * B)],
-        [unpacked],
-        (send_rows, index, flat),
-        2,
-        "own",
-    )
-    pair = swap(pair, 1)
-    edge = lax.ppermute(edge, "row", [(i, i + 2 * (i % 2) - 1) for i in range(n) if 0 < i % half < half - 1])
-    restricts = [restrict] + [
-        lax.ppermute(restrict, "col", [(i, (i + j) % col_size) for i in range(col_size)])
-        for j in range(1, col_size)
-    ]
+    flats, indices = [flat], [index]
+    for j in range(1, col_size):
+        turn = [(i, (i + j) % col_size) for i in range(col_size)]
+        flats.append(lax.ppermute(flat, "col", turn))
+        indices.append(lax.ppermute(index, "col", turn))
+    own, restrict = call(
+        functools.partial(prepare_kernel, col_size),
+        [shape(rows * PACK + rows, LANES), shape(col_size * CP * B, rows * B)],
+        [unpacked, pltpu.VMEM((rows * PACK, LANES), BF16)],
+        (*indices, *flats),
+        col_size,
+        "prepare",
+    )
     coupling = call(
         coupling_kernel,
         shape(rows, B, pl.cdiv(span, 2) * LANES),
@@ -241,13 +247,11 @@
         0,
         "coupling",
     )
-    far_flat, far_ints, pair, edge, coupling = lax.optimization_barrier(
-        (far_flat, far_ints, pair, edge, coupling)
-    )
-    steps = sorted(range(1, half), key=lambda d: (d == 1, -d.bit_count(), 1 - d % 2, -d))
+    far_flat, far_ints, coupling, own = lax.optimization_barrier((far_flat, far_ints, coupling, own))
+    steps = message_order(half)
     self_part, *out = call(
         functools.partial(pack_kernel, n, steps),
-        [message(S2)] + [message((3 if step == half - 1 else 1 + (step > 1)) * S2) for step in steps],
+        [message(S2)] + [message((3 if has_edge(step) else 2) * S2) for step in steps],
         [unpacked, pltpu.VMEM((2 * rows * PACK, LANES), BF16)],
         (send_rows, index, far_ints, own, far_flat),
         3,
@@ -255,10 +259,10 @@
     )
     messages = [swap(x, step) for x, step in zip(out, steps)]
     partial = call(
-        functools.partial(product_kernel, n, col_size, steps),
-        shape(col_size * CP * B, CP * B, dtype=f32),
+        functools.partial(product_kernel, n, steps),
+        shape(col_size * CP * B, CP * B),
         [pltpu.VMEM(((rows + n * S) * B, LANES), BF16), pltpu.VMEM((rows * B, CP * B), BF16)],
-        (neighbors.T, self_part, pair, edge, *messages, own, coupling, *restricts),
+        (neighbors.T, self_part, *messages, own, coupling, restrict),
         1,
         "product",
         2 * 10**8,
@@ -267,7 +271,7 @@
     parts = lax.all_to_all(
         partial.reshape(n, share, CP * B), "row", split_axis=0, concat_axis=0, tiled=True
     )
-    return jnp.sum(parts, axis=0)
+    return jnp.sum(parts.astype(f32), axis=0)
 
 
 def solution(mesh):

time: 46.6 us -> 41.7 us (0.89)
  starting transfers between devices: 19.6 us -> 14.1 us
  local copies, waits for them, and re-layouts: 2.12 us -> 1.19 us
  waiting for transfers between devices: 5.52 us -> 6.23 us
    ppermute x10 -> x9, starting transfers between devices: 18.9 us -> 13.5 us  [swap(): return lax.ppermute(x, 'row', [(i, i ^ bits) for i in range(n)])]
    unnamed x10, local copies, waits for them, and re-layouts: 2.12 us -> 1.19 us
    ppermute x10 -> x9, waiting for transfers between devices: 5.51 us -> 6.22 us  [swap(): return lax.ppermute(x, 'row', [(i, i ^ bits) for i in range(n)])]
  transfers between devices with their start and end apart: 12 -> 11, of which waited for: 5 -> 3; matrix products, arithmetic and copies ran while one was open for 0% -> 0% of each run, Pallas kernels for 9% -> 8%
where the time goes in v4:
time: 41.7 us; the launch traced here: 41.5 us
  starting transfers between devices  14.1 us (34%)
  blocking collectives  12.9 us (31%)
  Pallas kernels  6.34 us (15%)
  waiting for transfers between devices  6.23 us (15%)
  local copies, waits for them, and re-layouts  1.19 us (3%)
  other arithmetic  0.62 us (1%)
    ppermute x9, starting transfers between devices, swap(): return lax.ppermute(x, 'row', [(i, i ^ bits) for i in range(n)])  13.5 us
    all_to_all x1, blocking collectives, shards(): lax.all_to_all(partial.reshape(n, share, CP * B), 'row', split_axis=0, co...  12.9 us
    pallas_call x4, Pallas kernels, call(): pl.pallas_call(body, out_shape=out_shape, in_specs=[SMEM] * smem + [VMEM]...  6.34 us
    ppermute x9, waiting for transfers between devices, swap(): return lax.ppermute(x, 'row', [(i, i ^ bits) for i in range(n)])  6.22 us
    unnamed x10, local copies, waits for them, and re-layouts  1.19 us
  transfers between devices with their start and end apart: 11, of which 3 were waited for; matrix products, arithmetic and copies ran while one was open for 0% of the time, Pallas kernels for 8%

profile of v4, /device:TPU:0, one launch (start us, length us, event | category | flops | bytes accessed | tf_op | source)
XLA Modules:
  0.0 41.5 jit_solution(11111131142249375218)
XLA Ops:
  0.0 0.5 %collective-permute-start.3 = (bf16[16,4096]{1,0:T(8,128)(2,1)}, bf16[16,4096]{1,0:T(8,128)(2,1)S(1)}, u32[]{:S(2)}, u32[]{:S(2)}) collective-permute-start(bf16[16,4096]{1,0:T(8,128)(2,1)} %bitcast.7), channel_id=1, source_target_pairs={{0,1},{1,0},{2,3},{3,2},{4,5},{5,4},{6,7},{7,6},{8,9},{9,8},{10,11... | collective-permute-start | bytes 393224 | tf_op jit(solution)/shard_map/ppermute | solution.py:232
  0.5 3.7 %collective-permute-start = (bf16[16,4096]{1,0:T(8,128)(2,1)}, bf16[16,4096]{1,0:T(8,128)(2,1)S(1)}, u32[]{:S(2)}, u32[]{:S(2)}) collective-permute-start(bf16[16,4096]{1,0:T(8,128)(2,1)} %bitcast.8), channel_id=1, source_target_pairs={{0,16},{2,18},{4,20},{6,22},{8,24},{10,26},{12,28},{14,30},{16,0},... | collective-permute-start | bytes 393224 | tf_op jit(solution)/shard_map/ppermute | solution.py:224
  4.1 0.0 copy-done.2
  4.1 0.2 collective-permute-start.2
  4.3 0.0 copy-done.4
  4.3 0.5 %collective-permute-start.1 = (s32[1,144]{1,0:T(1,128)S(1)}, s32[1,144]{1,0:T(1,128)S(1)}, u32[]{:S(2)}, u32[]{:S(2)}) collective-permute-start(s32[1,144]{1,0:T(1,128)S(1)} %pad_add_fusion), channel_id=1, source_target_pairs={{0,16},{2,18},{4,20},{6,22},{8,24},{10,26},{12,28},{14,30},{16,0},... | collective-permute-start | bytes 1736 | tf_op jit(solution)/shard_map/ppermute | solution.py:224
  4.8 1.2 %copy-done = bf16[16,7,4096]{2,0,1:T(8,128)(2,1)S(1)} copy-done((bf16[16,7,4096]{2,0,1:T(8,128)(2,1)S(1)}, bf16[16,7,4096]{2,0,1:T(8,128)(2,1)}, u32[]{:S(2)}) %copy-start) | copy-done | bytes 917528
  6.0 2.1 %coupling.1.refs_8_ = bf16[16,64,512]{2,1,0:T(8,128)(2,1)S(1)} custom-call(bf16[7,16,4096]{2,1,0:T(8,128)(2,1)S(1)} %bitcast.5), custom_call_target="tpu_custom_call" | custom-call | flops 10000000 | bytes 1048576 | tf_op jit(solution)/shard_map/coupling/pallas_call | solution.py:206
  8.1 0.0 collective-permute-done.2.refs_1_
  8.1 0.0 collective-permute-done.3.refs_3_
  8.1 0.0 copy-done.1
  8.1 1.4 %prepare.1 = (bf16[528,128]{1,0:T(8,128)(2,1)S(1)}, bf16[256,1024]{1,0:T(8,128)(2,1)S(1)}) custom-call(s32[1,16]{1,0:T(1,128)S(1)} %bitcast.12, s32[1,16]{1,0:T(1,128)S(1)} %collective-permute-done.2.refs_1_, bf16[16,4096]{1,0:T(8,128)(2,1)S(1)} %bitcast.9, bf16[16,4096]{1,0:T(8,128)(2,1)S(1)} %collective-permute-done.3.refs_3_), custom_call_target="tpu_custom_call" | custom-call | flops 10000000 | bytes 1048576 | tf_op jit(solution)/shard_map/prepare/pallas_call | solution.py:206
  9.5 1.8 %collective-permute-done.1.far_ref = s32[1,144]{1,0:T(1,128)S(1)} collective-permute-done((s32[1,144]{1,0:T(1,128)S(1)}, s32[1,144]{1,0:T(1,128)S(1)}, u32[]{:S(2)}, u32[]{:S(2)}) %collective-permute-start.1) | collective-permute-done | bytes 608 | tf_op jit(solution)/shard_map/ppermute | solution.py:224
  11.3 0.0 collective-permute-done.flat_ref
  11.3 1.0 %pack.1 = (bf16[136,128]{1,0:T(8,128)(2,1)S(1)}, bf16[264,128]{1,0:T(8,128)(2,1)S(1)}, bf16[264,128]{1,0:T(8,128)(2,1)S(1)}, bf16[400,128]{1,0:T(8,128)(2,1)S(1)...) custom-call(s32[1,128]{1,0:T(1,128)S(1)} %copy-done.4, ...), custom_call_target="tpu_custom_call" | custom-call | flops 10000000 | bytes 1048576 | tf_op jit(solution)/shard_map/pack/pallas_call | solution.py:206
  12.3 1.8 %collective-permute-start.4 = (bf16[264,128]{1,0:T(8,128)(2,1)S(1)}, bf16[264,128]{1,0:T(8,128)(2,1)S(1)}, u32[]{:S(2)}, u32[]{:S(2)}) collective-permute-start(bf16[264,128]{1,0:T(8,128)(2,1)S(1)} %get-tuple-element.24), channel_id=1, source_target_pairs={{0,10},{2,8},{4,14},{6,12},{8,2},{10,0},{12,6},{14,4},{16,26},{18,... | collective-permute-start | bytes 202760 | tf_op jit(solution)/shard_map/ppermute | solution.py:224
  14.1 2.3 %collective-permute-start.5 = (bf16[264,128]{1,0:T(8,128)(2,1)S(1)}, bf16[264,128]{1,0:T(8,128)(2,1)S(1)}, u32[]{:S(2)}, u32[]{:S(2)}) collective-permute-start(bf16[264,128]{1,0:T(8,128)(2,1)S(1)} %get-tuple-element.25), channel_id=1, source_target_pairs={{0,12},{2,14},{4,8},{6,10},{8,4},{10,6},{12,0},{14,2},{16,28},{18,... | collective-permute-start | bytes 202760 | tf_op jit(solution)/shard_map/ppermute | solution.py:224
  16.4 0.6 %collective-permute-start.6 = (bf16[400,128]{1,0:T(8,128)(2,1)S(1)}, bf16[400,128]{1,0:T(8,128)(2,1)S(1)}, u32[]{:S(2)}, u32[]{:S(2)}) collective-permute-start(bf16[400,128]{1,0:T(8,128)(2,1)S(1)} %get-tuple-element.26), channel_id=1, source_target_pairs={{0,14},{2,12},{4,10},{6,8},{8,6},{10,4},{12,2},{14,0},{16,30},{18,... | collective-permute-start | bytes 307208 | tf_op jit(solution)/shard_map/ppermute | solution.py:224
  17.0 2.4 %collective-permute-start.7 = (bf16[400,128]{1,0:T(8,128)(2,1)S(1)}, bf16[400,128]{1,0:T(8,128)(2,1)S(1)}, u32[]{:S(2)}, u32[]{:S(2)}) collective-permute-start(bf16[400,128]{1,0:T(8,128)(2,1)S(1)} %get-tuple-element.27), channel_id=1, source_target_pairs={{0,6},{2,4},{4,2},{6,0},{8,14},{10,12},{12,10},{14,8},{16,22},{18,... | collective-permute-start | bytes 307208 | tf_op jit(solution)/shard_map/ppermute | solution.py:224
  19.5 0.5 %collective-permute-start.8 = (bf16[400,128]{1,0:T(8,128)(2,1)S(1)}, bf16[400,128]{1,0:T(8,128)(2,1)S(1)}, u32[]{:S(2)}, u32[]{:S(2)}) collective-permute-start(bf16[400,128]{1,0:T(8,128)(2,1)S(1)} %get-tuple-element.28), channel_id=1, source_target_pairs={{0,2},{2,0},{4,6},{6,4},{8,10},{10,8},{12,14},{14,12},{16,18},{18,... | collective-permute-start | bytes 307208 | tf_op jit(solution)/shard_map/ppermute | solution.py:224
  20.0 0.0 collective-permute-done.4.refs_0_
  20.0 0.5 %collective-permute-start.9 = (bf16[264,128]{1,0:T(8,128)(2,1)S(1)}, bf16[264,128]{1,0:T(8,128)(2,1)S(1)}, u32[]{:S(2)}, u32[]{:S(2)}) collective-permute-start(bf16[264,128]{1,0:T(8,128)(2,1)S(1)} %get-tuple-element.29), channel_id=1, source_target_pairs={{0,4},{2,6},{4,0},{6,2},{8,12},{10,14},{12,8},{14,10},{16,20},{18,... | collective-permute-start | bytes 202760 | tf_op jit(solution)/shard_map/ppermute | solution.py:224
  20.5 0.0 collective-permute-done.5.refs_1_
  20.5 1.2 %collective-permute-start.10 = (bf16[264,128]{1,0:T(8,128)(2,1)S(1)}, bf16[264,128]{1,0:T(8,128)(2,1)S(1)}, u32[]{:S(2)}, u32[]{:S(2)}) collective-permute-start(bf16[264,128]{1,0:T(8,128)(2,1)S(1)} %get-tuple-element.30), channel_id=1, source_target_pairs={{0,8},{2,10},{4,12},{6,14},{8,0},{10,2},{12,4},{14,6},{16,24},{18,... | collective-permute-start | bytes 202760 | tf_op jit(solution)/shard_map/ppermute | solution.py:224
  21.8 4.1 %collective-permute-done.9.refs_5_ = bf16[264,128]{1,0:T(8,128)(2,1)S(1)} collective-permute-done((bf16[264,128]{1,0:T(8,128)(2,1)S(1)}, bf16[264,128]{1,0:T(8,128)(2,1)S(1)}, u32[]{:S(2)}, u32[]{:S(2)}) %collective-permute-start.9) | collective-permute-done | bytes 67616 | tf_op jit(solution)/shard_map/ppermute | solution.py:224
  25.8 0.0 collective-permute-done.10.refs_6_
  25.8 0.0 collective-permute-done.6.refs_2_
  25.8 0.0 collective-permute-done.7.refs_3_
  25.8 0.3 collective-permute-done.8.refs_4_
  26.1 1.8 %product.1 = bf16[256,128]{1,0:T(8,128)(2,1)S(1)} custom-call(s32[7,16]{1,0:T(8,128)S(1)} %bitcast.14, bf16[136,128]{1,0:T(8,128)(2,1)S(1)} %get-tuple-element.23.self_ref, bf16[264,128]{1,0:T(8,128)(2,1)S(1)} %collective-permute-done.4.refs_0_, bf16[264,128]{1,0:T(8,128)(2,1)S(1)} %collective-permute-done.5.refs_1_, ...), custom_call_target="tpu_custom_call" | custom-call | flops 200000000 | bytes 1048576 | tf_op jit(solution)/shard_map/product/pallas_call | solution.py:206
  28.0 12.9 %all_to_all.5 = bf16[16,16,128]{2,1,0:T(8,128)(2,1)S(1)} all-to-all(bf16[16,16,128]{2,1,0:T(8,128)(2,1)S(1)} %bitcast.6), channel_id=1, replica_groups=mesh['row'=16,'col'=2] {'row'}, dimensions={0} | all-to-all | bytes 131072 | tf_op jit(solution)/shard_map/all_to_all | solution.py:271
  40.9 0.6 %convert_reduce_fusion = f32[16,128]{1,0:T(8,128)} fusion(bf16[16,16,128]{2,1,0:T(8,128)(2,1)S(1)} %all_to_all.5), kind=kLoop, calls=%fused_computation | loop fusion | flops 63488 | bytes 73728 | tf_op jit(solution)/shard_map/reduce_sum | solution.py:274
  (7 shorter events, 0.0 us)
Async XLA Ops:
  0.0 4.1 %copy-start.2 = (s32[16,1]{0,1:T(1,128)S(1)}, s32[16,1]{0,1:T(1,128)}, u32[]{:S(2)}) copy-start(s32[16,1]{0,1:T(1,128)} %param.9) | copy-start | bytes 196
  0.0 4.3 %copy-start.4 = (s32[1,128]{1,0:T(1,128)S(1)}, s32[1,128]{1,0:T(1,128)}, u32[]{:S(2)}) copy-start(s32[1,128]{1,0:T(1,128)} %send_ref.1) | copy-start | bytes 1540
  0.0 8.1 %collective-permute-start.3 = (bf16[16,4096]{1,0:T(8,128)(2,1)}, bf16[16,4096]{1,0:T(8,128)(2,1)S(1)}, u32[]{:S(2)}, u32[]{:S(2)}) collective-permute-start(bf16[16,4096]{1,0:T(8,128)(2,1)} %bitcast.7), channel_id=1, source_target_pairs={{0,1},{1,0},{2,3},{3,2},{4,5},{5,4},{6,7},{7,6},{8,9},{9,8},{10,11... | collective-permute-start | bytes 393224 | tf_op jit(solution)/shard_map/ppermute | solution.py:232
  0.5 10.9 %collective-permute-start = (bf16[16,4096]{1,0:T(8,128)(2,1)}, bf16[16,4096]{1,0:T(8,128)(2,1)S(1)}, u32[]{:S(2)}, u32[]{:S(2)}) collective-permute-start(bf16[16,4096]{1,0:T(8,128)(2,1)} %bitcast.8), channel_id=1, source_target_pairs={{0,16},{2,18},{4,20},{6,22},{8,24},{10,26},{12,28},{14,30},{16,0},... | collective-permute-start | bytes 393224 | tf_op jit(solution)/shard_map/ppermute | solution.py:224
  4.1 3.9 %collective-permute-start.2 = (s32[1,16]{1,0:T(1,128)S(1)}, s32[1,16]{1,0:T(1,128)S(1)}, u32[]{:S(2)}, u32[]{:S(2)}) collective-permute-start(s32[1,16]{1,0:T(1,128)S(1)} %bitcast.10), channel_id=1, source_target_pairs={{0,1},{1,0},{2,3},{3,2},{4,5},{5,4},{6,7},{7,6},{8,9},{9,8},{10,11... | collective-permute-start | bytes 200 | tf_op jit(solution)/shard_map/ppermute | solution.py:233
  4.3 7.0 %collective-permute-start.1 = (s32[1,144]{1,0:T(1,128)S(1)}, s32[1,144]{1,0:T(1,128)S(1)}, u32[]{:S(2)}, u32[]{:S(2)}) collective-permute-start(s32[1,144]{1,0:T(1,128)S(1)} %pad_add_fusion), channel_id=1, source_target_pairs={{0,16},{2,18},{4,20},{6,22},{8,24},{10,26},{12,28},{14,30},{16,0},... | collective-permute-start | bytes 1736 | tf_op jit(solution)/shard_map/ppermute | solution.py:224
  4.8 1.2 %copy-start = (bf16[16,7,4096]{2,0,1:T(8,128)(2,1)S(1)}, bf16[16,7,4096]{2,0,1:T(8,128)(2,1)}, u32[]{:S(2)}) copy-start(bf16[16,7,4096]{2,0,1:T(8,128)(2,1)} %param.5) | copy-start | bytes 2752516
  6.0 2.1 %copy-start.1 = (bf16[16,1,4096]{2,0,1:T(8,128)(2,1)S(1)}, bf16[16,1,4096]{2,0,1:T(8,128)(2,1)}, u32[]{:S(2)}) copy-start(bf16[16,1,4096]{2,0,1:T(8,128)(2,1)} %param.8) | copy-start | bytes 393220
  12.3 7.7 %collective-permute-start.4 = (bf16[264,128]{1,0:T(8,128)(2,1)S(1)}, bf16[264,128]{1,0:T(8,128)(2,1)S(1)}, u32[]{:S(2)}, u32[]{:S(2)}) collective-permute-start(bf16[264,128]{1,0:T(8,128)(2,1)S(1)} %get-tuple-element.24), channel_id=1, source_target_pairs={{0,10},{2,8},{4,14},{6,12},{8,2},{10,0},{12,6},{14,4},{16,26},{18,... | collective-permute-start | bytes 202760 | tf_op jit(solution)/shard_map/ppermute | solution.py:224
  14.1 6.4 %collective-permute-start.5 = (bf16[264,128]{1,0:T(8,128)(2,1)S(1)}, bf16[264,128]{1,0:T(8,128)(2,1)S(1)}, u32[]{:S(2)}, u32[]{:S(2)}) collective-permute-start(bf16[264,128]{1,0:T(8,128)(2,1)S(1)} %get-tuple-element.25), channel_id=1, source_target_pairs={{0,12},{2,14},{4,8},{6,10},{8,4},{10,6},{12,0},{14,2},{16,28},{18,... | collective-permute-start | bytes 202760 | tf_op jit(solution)/shard_map/ppermute | solution.py:224
  16.4 9.4 %collective-permute-start.6 = (bf16[400,128]{1,0:T(8,128)(2,1)S(1)}, bf16[400,128]{1,0:T(8,128)(2,1)S(1)}, u32[]{:S(2)}, u32[]{:S(2)}) collective-permute-start(bf16[400,128]{1,0:T(8,128)(2,1)S(1)} %get-tuple-element.26), channel_id=1, source_target_pairs={{0,14},{2,12},{4,10},{6,8},{8,6},{10,4},{12,2},{14,0},{16,30},{18,... | collective-permute-start | bytes 307208 | tf_op jit(solution)/shard_map/ppermute | solution.py:224
  17.0 8.8 %collective-permute-start.7 = (bf16[400,128]{1,0:T(8,128)(2,1)S(1)}, bf16[400,128]{1,0:T(8,128)(2,1)S(1)}, u32[]{:S(2)}, u32[]{:S(2)}) collective-permute-start(bf16[400,128]{1,0:T(8,128)(2,1)S(1)} %get-tuple-element.27), channel_id=1, source_target_pairs={{0,6},{2,4},{4,2},{6,0},{8,14},{10,12},{12,10},{14,8},{16,22},{18,... | collective-permute-start | bytes 307208 | tf_op jit(solution)/shard_map/ppermute | solution.py:224
  19.5 6.7 %collective-permute-start.8 = (bf16[400,128]{1,0:T(8,128)(2,1)S(1)}, bf16[400,128]{1,0:T(8,128)(2,1)S(1)}, u32[]{:S(2)}, u32[]{:S(2)}) collective-permute-start(bf16[400,128]{1,0:T(8,128)(2,1)S(1)} %get-tuple-element.28), channel_id=1, source_target_pairs={{0,2},{2,0},{4,6},{6,4},{8,10},{10,8},{12,14},{14,12},{16,18},{18,... | collective-permute-start | bytes 307208 | tf_op jit(solution)/shard_map/ppermute | solution.py:224
  20.0 6.1 %copy-start.3 = (s32[16,7]{0,1:T(8,128)S(1)}, s32[16,7]{0,1:T(8,128)}, u32[]{:S(2)}) copy-start(s32[16,7]{0,1:T(8,128)} %param.6) | copy-start | bytes 1348
  20.0 5.8 %collective-permute-start.9 = (bf16[264,128]{1,0:T(8,128)(2,1)S(1)}, bf16[264,128]{1,0:T(8,128)(2,1)S(1)}, u32[]{:S(2)}, u32[]{:S(2)}) collective-permute-start(bf16[264,128]{1,0:T(8,128)(2,1)S(1)} %get-tuple-element.29), channel_id=1, source_target_pairs={{0,4},{2,6},{4,0},{6,2},{8,12},{10,14},{12,8},{14,10},{16,20},{18,... | collective-permute-start | bytes 202760 | tf_op jit(solution)/shard_map/ppermute | solution.py:224
  20.5 5.3 %collective-permute-start.10 = (bf16[264,128]{1,0:T(8,128)(2,1)S(1)}, bf16[264,128]{1,0:T(8,128)(2,1)S(1)}, u32[]{:S(2)}, u32[]{:S(2)}) collective-permute-start(bf16[264,128]{1,0:T(8,128)(2,1)S(1)} %get-tuple-element.30), channel_id=1, source_target_pairs={{0,8},{2,10},{4,12},{6,14},{8,0},{10,2},{12,4},{14,6},{16,24},{18,... | collective-permute-start | bytes 202760 | tf_op jit(solution)/shard_map/ppermute | solution.py:224

commit v5 on v4

--- a/solution.py
+++ b/solution.py
@@ -64,11 +64,12 @@
     ref[len(picks) * PACK :, :] = mark.astype(BF16)
 
 
-def prepare_kernel(col_size, *refs):
+def prepare_kernel(n, col_size, send_ref, *refs):
     index_refs, refs = refs[:col_size], refs[col_size:]
     flat_refs, refs = refs[:col_size], refs[col_size:]
-    own_ref, restrict_ref, scratch, table = refs
+    own_ref, pair_ref, restrict_ref, scratch, table = refs
     rows = flat_refs[0].shape[0]
+    pair = lax.bitwise_xor(lax.axis_index("row"), 1) * S
     mine = lax.axis_index("col")
     for j, (index_ref, flat_ref) in enumerate(zip(index_refs, flat_refs)):
         panel = lax.rem(mine + col_size - j, col_size)
@@ -81,6 +82,8 @@
         masks = mask_table(index_of, rows)
         if j == 0:
             own_ref[rows * PACK :, :] = masks.astype(BF16)
+            slots = [send_ref[0, pair + s] for s in range(S)]
+            fill(pair_ref, own_ref, [(row, index_of(row)) for row in slots])
         pieces = []
         for r in range(rows):
             x = turned[r * PACK : (r + 1) * PACK, :].astype(jnp.float32)
@@ -109,22 +112,18 @@
         coupling_ref[:, PACK:, lanes] = ordered[:, LANES:].reshape(rows, PACK, LANES)
 
 
-def beside(n, p, q):
-    gap = lax.rem(p - q + n, n)
-    return (gap == 1) | (gap == n - 1)
-
-
-def has_edge(step):
-    return step & (step + 1) == 0
-
-
-def message_order(half):
-    edges = sorted((d for d in range(1, half) if has_edge(d)), reverse=True)
-    rest = sorted((d for d in range(1, half) if not has_edge(d)), key=lambda d: (-d.bit_count(), -(d % 2), d))
-    return rest[: len(rest) // 2] + edges + rest[len(rest) // 2 :]
-
-
-def pack_kernel(n, steps, send_ref, index_ref, far_ref, own_ref, flat_ref, self_ref, *refs):
+def other_neighbour(half, me):
+    low = lax.rem(me, half)
+    odd = lax.rem(me, 2) == 1
+    return me - low + lax.rem(low + jnp.where(odd, 1, half - 1), half)
+
+
+def at_end(half, me):
+    low = lax.rem(me, half)
+    return (low == 0) | (low == half - 1)
+
+
+def pack_kernel(n, steps, send_ref, index_ref, far_ref, own_ref, flat_ref, self_ref, edge_ref, *refs):
     rows = flat_ref.shape[0]
     out_refs, (scratch, table) = refs[: len(steps)], refs[len(steps) :]
     me = lax.axis_index("row")
@@ -140,19 +139,21 @@
         return rows + row, far_ref[0, n * S + row]
 
     for step, ref in zip(steps, out_refs):
-        target = lax.bitwise_xor(me, step)
-        first = target * S
-        picks = [near_row(first + s) for s in range(S2)] + [far_row(first + s) for s in range(S2)]
-        if has_edge(step):
-            near = beside(n, me, target)
-            for s in range(S2, S):
-                pairs = zip(near_row(first + s), far_row(first + s))
-                picks.append(tuple(jnp.where(near, x, y) for x, y in pairs))
+        first = lax.bitwise_xor(me, step) * S
+        picks = [far_row(first + s) for s in range(S2)]
+        if step > 1:
+            picks += [near_row(first + s) for s in range(S2)]
         fill(ref, table, picks)
+    first = other_neighbour(n // 2, me) * S
+    picks = []
+    for s in range(S2, S):
+        pairs = zip(far_row(first + s), near_row(first + s))
+        picks.append(tuple(jnp.where(at_end(n // 2, me), x, y) for x, y in pairs))
+    fill(edge_ref, table, picks)
     fill(self_ref, table, [far_row(me * S + s) for s in range(S2)])
 
 
-def product_kernel(n, steps, code_ref, self_ref, *refs):
+def product_kernel(n, steps, code_ref, self_ref, edge_ref, pair_ref, *refs):
     message_refs, refs = refs[: len(steps)], refs[len(steps) :]
     own_ref, coupling_ref, restrict_ref, out_ref, wide, ap = refs
     rows = coupling_ref.shape[0]
@@ -175,12 +176,15 @@
     for r in range(rows):
         place(r, own_ref[r * PACK : (r + 1) * PACK, :], own_ref[rows * PACK + r : rows * PACK + r + 1, :])
     place_slots(self_ref, [lax.bitwise_xor(me, n // 2) * S])
+    near = lax.bitwise_xor(me, 1) * S
+    place_slots(pair_ref, [near, near + S2])
+    near = other_neighbour(n // 2, me)
+    place_slots(edge_ref, [jnp.where(at_end(n // 2, me), lax.bitwise_xor(near, n // 2), near) * S + S2])
     for ref, step in zip(message_refs, steps):
         near = lax.bitwise_xor(me, step)
-        far = lax.bitwise_xor(near, n // 2)
-        firsts = [near * S, far * S]
-        if has_edge(step):
-            firsts.append(jnp.where(beside(n, me, near), near, far) * S + S2)
+        firsts = [lax.bitwise_xor(near, n // 2) * S]
+        if step > 1:
+            firsts.append(near * S)
         place_slots(ref, firsts)
 
     def row_body(r, carry):
@@ -192,7 +196,7 @@
         return carry
 
     lax.fori_loop(0, rows, row_body, 0, unroll=8)
-    out_ref[...] = jnp.dot(restrict_ref[...], ap[...], preferred_element_type=jnp.float32).astype(BF16)
+    out_ref[...] = jnp.dot(restrict_ref[...], ap[...], preferred_element_type=jnp.float32)
 
 
 def shards(n, col_size, a_tiles, neighbors, send_rows, p_tiles, p_index):
@@ -218,7 +222,7 @@
         return jax.ShapeDtypeStruct(dims, dtype)
 
     def message(slots):
-        return shape(slots * PACK + (8 if slots <= 8 else 16), LANES)
+        return shape(slots * PACK + 8, LANES)
 
     def swap(x, bits):
         return lax.ppermute(x, "row", [(i, i ^ bits) for i in range(n)])
@@ -231,12 +235,12 @@
         turn = [(i, (i + j) % col_size) for i in range(col_size)]
         flats.append(lax.ppermute(flat, "col", turn))
         indices.append(lax.ppermute(index, "col", turn))
-    own, restrict = call(
-        functools.partial(prepare_kernel, col_size),
-        [shape(rows * PACK + rows, LANES), shape(col_size * CP * B, rows * B)],
+    own, pair, restrict = call(
+        functools.partial(prepare_kernel, n, col_size),
+        [shape(rows * PACK + rows, LANES), message(S), shape(col_size * CP * B, rows * B)],
         [unpacked, pltpu.VMEM((rows * PACK, LANES), BF16)],
-        (*indices, *flats),
-        col_size,
+        (send_rows, *indices, *flats),
+        1 + col_size,
         "prepare",
     )
     coupling = call(
@@ -248,21 +252,26 @@
         "coupling",
     )
     far_flat, far_ints, coupling, own = lax.optimization_barrier((far_flat, far_ints, coupling, own))
-    steps = message_order(half)
-    self_part, *out = call(
+    steps = sorted(range(1, half), key=lambda d: (d == 1, -d.bit_count(), 1 - d % 2, -d))
+    self_part, edge, *out = call(
         functools.partial(pack_kernel, n, steps),
-        [message(S2)] + [message((3 if has_edge(step) else 2) * S2) for step in steps],
+        [message(S2)] * 2 + [message((2 if step > 1 else 1) * S2) for step in steps],
         [unpacked, pltpu.VMEM((2 * rows * PACK, LANES), BF16)],
         (send_rows, index, far_ints, own, far_flat),
         3,
         "pack",
     )
+    pair, edge, *out = lax.optimization_barrier((swap(pair, 1), edge, *out))
     messages = [swap(x, step) for x, step in zip(out, steps)]
+    ends = [i % 2 * 2 - 1 for i in range(half)]
+    edge = lax.ppermute(
+        edge, "row", [(g + i, g + (i + ends[i]) % half) for g in (0, half) for i in range(half)]
+    )
     partial = call(
         functools.partial(product_kernel, n, steps),
-        shape(col_size * CP * B, CP * B),
+        shape(col_size * CP * B, CP * B, dtype=f32),
         [pltpu.VMEM(((rows + n * S) * B, LANES), BF16), pltpu.VMEM((rows * B, CP * B), BF16)],
-        (neighbors.T, self_part, *messages, own, coupling, restrict),
+        (neighbors.T, self_part, edge, pair, *messages, own, coupling, restrict),
         1,
         "product",
         2 * 10**8,
@@ -271,7 +280,7 @@
     parts = lax.all_to_all(
         partial.reshape(n, share, CP * B), "row", split_axis=0, concat_axis=0, tiled=True
     )
-    return jnp.sum(parts.astype(f32), axis=0)
+    return jnp.sum(parts, axis=0)
 
 
 def solution(mesh):

time: 41.7 us -> 44.6 us (1.070)
  starting transfers between devices: 14.1 us -> 18.3 us
  waiting for transfers between devices: 6.23 us -> 4.19 us
  local copies, waits for them, and re-layouts: 1.19 us -> 2.1 us
    ppermute x9 -> x10, waiting for transfers between devices: 6.22 us -> 3.22 us  [swap(): return lax.ppermute(x, 'row', [(i, i ^ bits) for i in range(n)])]
    ppermute x9 -> x10, starting transfers between devices: 13.5 us -> 16.4 us  [swap(): return lax.ppermute(x, 'row', [(i, i ^ bits) for i in range(n)])]
    ppermute x0 -> x1, starting transfers between devices: none -> 1.32 us  [shards(): lax.ppermute(edge, 'row', [(g + i, g + (i + ends[i]) % half) for g in (0,...]
    ppermute x1, waiting for transfers between devices: 0.01 us -> 0.96 us  [shards(): indices.append(lax.ppermute(index, 'col', turn))]
    unnamed x10, local copies, waits for them, and re-layouts: 1.19 us -> 2.1 us
  transfers between devices with their start and end apart: 11 -> 13, of which waited for: 3 -> 6; matrix products, arithmetic and copies ran while one was open for 0% -> 0% of each run, Pallas kernels for 8% -> 10%
where the time goes in v5:
time: 44.6 us; the launch traced here: 44.4 us
  starting transfers between devices  18.3 us (41%)
  blocking collectives  12.8 us (29%)
  Pallas kernels  6.3 us (14%)
  waiting for transfers between devices  4.19 us (9%)
  local copies, waits for them, and re-layouts  2.1 us (5%)
  other arithmetic  0.62 us (1%)
    ppermute x10, starting transfers between devices, swap(): return lax.ppermute(x, 'row', [(i, i ^ bits) for i in range(n)])  16.4 us
    all_to_all x1, blocking collectives, shards(): lax.all_to_all(partial.reshape(n, share, CP * B), 'row', split_axis=0, co...  12.8 us
    pallas_call x4, Pallas kernels, call(): pl.pallas_call(body, out_shape=out_shape, in_specs=[SMEM] * smem + [VMEM]...  6.3 us
    ppermute x10, waiting for transfers between devices, swap(): return lax.ppermute(x, 'row', [(i, i ^ bits) for i in range(n)])  3.22 us
    unnamed x10, local copies, waits for them, and re-layouts  2.1 us
    ppermute x1, starting transfers between devices, shards(): lax.ppermute(edge, 'row', [(g + i, g + (i + ends[i]) % half) for g in (0,...  1.32 us
    ppermute x1, waiting for transfers between devices, shards(): indices.append(lax.ppermute(index, 'col', turn))  0.96 us
  transfers between devices with their start and end apart: 13, of which 6 were waited for; matrix products, arithmetic and copies ran while one was open for 0% of the time, Pallas kernels for 10%

profile of v5, /device:TPU:0, one launch (start us, length us, event | category | flops | bytes accessed | tf_op | source)
XLA Modules:
  0.0 44.4 jit_solution(8189393576835869083)
XLA Ops:
  0.0 0.5 %collective-permute-start.3 = (bf16[16,4096]{1,0:T(8,128)(2,1)}, bf16[16,4096]{1,0:T(8,128)(2,1)S(1)}, u32[]{:S(2)}, u32[]{:S(2)}) collective-permute-start(bf16[16,4096]{1,0:T(8,128)(2,1)} %bitcast.7), channel_id=1, source_target_pairs={{0,1},{1,0},{2,3},{3,2},{4,5},{5,4},{6,7},{7,6},{8,9},{9,8},{10,11... | collective-permute-start | bytes 393224 | tf_op jit(solution)/shard_map/ppermute | solution.py:236
  0.5 3.7 %collective-permute-start = (bf16[16,4096]{1,0:T(8,128)(2,1)}, bf16[16,4096]{1,0:T(8,128)(2,1)S(1)}, u32[]{:S(2)}, u32[]{:S(2)}) collective-permute-start(bf16[16,4096]{1,0:T(8,128)(2,1)} %bitcast.8), channel_id=1, source_target_pairs={{0,16},{2,18},{4,20},{6,22},{8,24},{10,26},{12,28},{14,30},{16,0},... | collective-permute-start | bytes 393224 | tf_op jit(solution)/shard_map/ppermute | solution.py:228
  4.1 0.2 collective-permute-start.2
  4.3 1.0 %collective-permute-done.2.refs_1_ = s32[1,16]{1,0:T(1,128)S(1)} collective-permute-done((s32[1,16]{1,0:T(1,128)S(1)}, s32[1,16]{1,0:T(1,128)S(1)}, u32[]{:S(2)}, u32[]{:S(2)}) %collective-permute-start.2) | collective-permute-done | bytes 96 | tf_op jit(solution)/shard_map/ppermute | solution.py:237
  5.3 0.9 %copy-done.1 = bf16[16,1,4096]{2,0,1:T(8,128)(2,1)S(1)} copy-done((bf16[16,1,4096]{2,0,1:T(8,128)(2,1)S(1)}, bf16[16,1,4096]{2,0,1:T(8,128)(2,1)}, u32[]{:S(2)}) %copy-start.1) | copy-done | bytes 131096
  6.2 1.4 %prepare.1 = (bf16[528,128]{1,0:T(8,128)(2,1)S(1)}, bf16[264,128]{1,0:T(8,128)(2,1)S(1)}, bf16[256,1024]{1,0:T(8,128)(2,1)S(1)}) custom-call(s32[1,128]{1,0:T(1,128)S(1)} %copy-done.2, s32[1,16]{1,0:T(1,128)S(1)} %bitcast.11, s32[1,16]{1,0:T(1,128)S(1)} %collective-permute-done.2.refs_1_, bf16[16,4096]{1,0:T(8,128)(2,1)S(1)} %bitcast.9, ...), custom_call_target="tpu_custom_call" | custom-call | flops 10000000 | bytes 1048576 | tf_op jit(solution)/shard_map/prepare/pallas_call | solution.py:210
  7.6 1.6 %collective-permute-start.4 = (bf16[264,128]{1,0:T(8,128)(2,1)S(1)}, bf16[264,128]{1,0:T(8,128)(2,1)S(1)}, u32[]{:S(2)}, u32[]{:S(2)}) collective-permute-start(bf16[264,128]{1,0:T(8,128)(2,1)S(1)} %get-tuple-element.35), channel_id=1, source_target_pairs={{0,2},{2,0},{4,6},{6,4},{8,10},{10,8},{12,14},{14,12},{16,18},{18,... | collective-permute-start | bytes 202760 | tf_op jit(solution)/shard_map/ppermute | solution.py:228
  9.1 0.6 %collective-permute-start.1 = (s32[1,144]{1,0:T(1,128)S(1)}, s32[1,144]{1,0:T(1,128)S(1)}, u32[]{:S(2)}, u32[]{:S(2)}) collective-permute-start(s32[1,144]{1,0:T(1,128)S(1)} %pad_add_fusion), channel_id=1, source_target_pairs={{0,16},{2,18},{4,20},{6,22},{8,24},{10,26},{12,28},{14,30},{16,0},... | collective-permute-start | bytes 1736 | tf_op jit(solution)/shard_map/ppermute | solution.py:228
  9.7 1.2 %copy-done = bf16[16,7,4096]{2,0,1:T(8,128)(2,1)S(1)} copy-done((bf16[16,7,4096]{2,0,1:T(8,128)(2,1)S(1)}, bf16[16,7,4096]{2,0,1:T(8,128)(2,1)}, u32[]{:S(2)}) %copy-start) | copy-done | bytes 917528
  10.9 2.1 %coupling.1.refs_8_ = bf16[16,64,512]{2,1,0:T(8,128)(2,1)S(1)} custom-call(bf16[7,16,4096]{2,1,0:T(8,128)(2,1)S(1)} %bitcast.5), custom_call_target="tpu_custom_call" | custom-call | flops 10000000 | bytes 1048576 | tf_op jit(solution)/shard_map/coupling/pallas_call | solution.py:210
  13.0 0.6 %collective-permute-done.1.far_ref = s32[1,144]{1,0:T(1,128)S(1)} collective-permute-done((s32[1,144]{1,0:T(1,128)S(1)}, s32[1,144]{1,0:T(1,128)S(1)}, u32[]{:S(2)}, u32[]{:S(2)}) %collective-permute-start.1) | collective-permute-done | bytes 608 | tf_op jit(solution)/shard_map/ppermute | solution.py:228
  13.6 1.0 %pack.1 = (bf16[136,128]{1,0:T(8,128)(2,1)S(1)}, bf16[136,128]{1,0:T(8,128)(2,1)S(1)}, bf16[264,128]{1,0:T(8,128)(2,1)S(1)}, bf16[264,128]{1,0:T(8,128)(2,1)S(1)...) custom-call(s32[1,128]{1,0:T(1,128)S(1)} %copy-done.2, ...), custom_call_target="tpu_custom_call" | custom-call | flops 10000000 | bytes 1048576 | tf_op jit(solution)/shard_map/pack/pallas_call | solution.py:210
  14.6 0.0 collective-permute-done.4.pair_ref
  14.6 0.0 copy-start.4
  14.6 2.6 %collective-permute-start.6 = (bf16[264,128]{1,0:T(8,128)(2,1)S(1)}, bf16[264,128]{1,0:T(8,128)(2,1)S(1)}, u32[]{:S(2)}, u32[]{:S(2)}) collective-permute-start(bf16[264,128]{1,0:T(8,128)(2,1)S(1)} %get-tuple-element.46), channel_id=1, source_target_pairs={{0,14},{2,12},{4,10},{6,8},{8,6},{10,4},{12,2},{14,0},{16,30},{18,... | collective-permute-start | bytes 202760 | tf_op jit(solution)/shard_map/ppermute | solution.py:228
  17.2 1.3 %collective-permute-start.5 = (bf16[136,128]{1,0:T(8,128)(2,1)S(1)}, bf16[136,128]{1,0:T(8,128)(2,1)S(1)}, u32[]{:S(2)}, u32[]{:S(2)}) collective-permute-start(bf16[136,128]{1,0:T(8,128)(2,1)S(1)} %get-tuple-element.44), channel_id=1, source_target_pairs={{0,14},{2,4},{4,2},{6,8},{8,6},{10,12},{12,10},{14,0},{16,30},{18,... | collective-permute-start | bytes 104456 | tf_op jit(solution)/shard_map/ppermute | solution.py:267
  18.5 0.6 %collective-permute-start.12 = (bf16[136,128]{1,0:T(8,128)(2,1)S(1)}, bf16[136,128]{1,0:T(8,128)(2,1)S(1)}, u32[]{:S(2)}, u32[]{:S(2)}) collective-permute-start(bf16[136,128]{1,0:T(8,128)(2,1)S(1)} %get-tuple-element.52), channel_id=1, source_target_pairs={{0,2},{2,0},{4,6},{6,4},{8,10},{10,8},{12,14},{14,12},{16,18},{18,... | collective-permute-start | bytes 104456 | tf_op jit(solution)/shard_map/ppermute | solution.py:228
  19.1 2.4 %collective-permute-start.7 = (bf16[264,128]{1,0:T(8,128)(2,1)S(1)}, bf16[264,128]{1,0:T(8,128)(2,1)S(1)}, u32[]{:S(2)}, u32[]{:S(2)}) collective-permute-start(bf16[264,128]{1,0:T(8,128)(2,1)S(1)} %get-tuple-element.47), channel_id=1, source_target_pairs={{0,10},{2,8},{4,14},{6,12},{8,2},{10,0},{12,6},{14,4},{16,26},{18,... | collective-permute-start | bytes 202760 | tf_op jit(solution)/shard_map/ppermute | solution.py:228
  21.5 1.5 %collective-permute-start.8 = (bf16[264,128]{1,0:T(8,128)(2,1)S(1)}, bf16[264,128]{1,0:T(8,128)(2,1)S(1)}, u32[]{:S(2)}, u32[]{:S(2)}) collective-permute-start(bf16[264,128]{1,0:T(8,128)(2,1)S(1)} %get-tuple-element.48), channel_id=1, source_target_pairs={{0,6},{2,4},{4,2},{6,0},{8,14},{10,12},{12,10},{14,8},{16,22},{18,... | collective-permute-start | bytes 202760 | tf_op jit(solution)/shard_map/ppermute | solution.py:228
  23.0 1.2 %collective-permute-start.9 = (bf16[264,128]{1,0:T(8,128)(2,1)S(1)}, bf16[264,128]{1,0:T(8,128)(2,1)S(1)}, u32[]{:S(2)}, u32[]{:S(2)}) collective-permute-start(bf16[264,128]{1,0:T(8,128)(2,1)S(1)} %get-tuple-element.49), channel_id=1, source_target_pairs={{0,12},{2,14},{4,8},{6,10},{8,4},{10,6},{12,0},{14,2},{16,28},{18,... | collective-permute-start | bytes 202760 | tf_op jit(solution)/shard_map/ppermute | solution.py:228
  24.2 0.0 collective-permute-done.12.refs_6_
  24.2 0.7 %collective-permute-start.10 = (bf16[264,128]{1,0:T(8,128)(2,1)S(1)}, bf16[264,128]{1,0:T(8,128)(2,1)S(1)}, u32[]{:S(2)}, u32[]{:S(2)}) collective-permute-start(bf16[264,128]{1,0:T(8,128)(2,1)S(1)} %get-tuple-element.50), channel_id=1, source_target_pairs={{0,8},{2,10},{4,12},{6,14},{8,0},{10,2},{12,4},{14,6},{16,24},{18,... | collective-permute-start | bytes 202760 | tf_op jit(solution)/shard_map/ppermute | solution.py:228
  24.8 0.0 collective-permute-done.6.refs_0_
  24.8 1.7 %collective-permute-start.11 = (bf16[264,128]{1,0:T(8,128)(2,1)S(1)}, bf16[264,128]{1,0:T(8,128)(2,1)S(1)}, u32[]{:S(2)}, u32[]{:S(2)}) collective-permute-start(bf16[264,128]{1,0:T(8,128)(2,1)S(1)} %get-tuple-element.51), channel_id=1, source_target_pairs={{0,4},{2,6},{4,0},{6,2},{8,12},{10,14},{12,8},{14,10},{16,20},{18,... | collective-permute-start | bytes 202760 | tf_op jit(solution)/shard_map/ppermute | solution.py:228
  26.5 0.0 collective-permute-done.7.refs_1_
  26.5 0.3 collective-permute-done.8.refs_2_
  26.9 1.3 %collective-permute-done.9.refs_3_ = bf16[264,128]{1,0:T(8,128)(2,1)S(1)} collective-permute-done((bf16[264,128]{1,0:T(8,128)(2,1)S(1)}, bf16[264,128]{1,0:T(8,128)(2,1)S(1)}, u32[]{:S(2)}, u32[]{:S(2)}) %collective-permute-start.9) | collective-permute-done | bytes 67616 | tf_op jit(solution)/shard_map/ppermute | solution.py:228
  28.2 0.3 collective-permute-done.10.refs_4_
  28.5 0.7 %collective-permute-done.11.refs_5_ = bf16[264,128]{1,0:T(8,128)(2,1)S(1)} collective-permute-done((bf16[264,128]{1,0:T(8,128)(2,1)S(1)}, bf16[264,128]{1,0:T(8,128)(2,1)S(1)}, u32[]{:S(2)}, u32[]{:S(2)}) %collective-permute-start.11) | collective-permute-done | bytes 67616 | tf_op jit(solution)/shard_map/ppermute | solution.py:228
  29.1 1.8 %product.1 = f32[256,128]{1,0:T(8,128)S(1)} custom-call(s32[7,16]{1,0:T(8,128)S(1)} %bitcast.14, bf16[136,128]{1,0:T(8,128)(2,1)S(1)} %get-tuple-element.34.self_ref, bf16[136,128]{1,0:T(8,128)(2,1)S(1)} %collective-permute-done.5.edge_ref, bf16[264,128]{1,0:T(8,128)(2,1)S(1)} %collective-permute-done.4.pair_ref, ...), custom_call_target="tpu_custom_call" | custom-call | flops 200000000 | bytes 1048576 | tf_op jit(solution)/shard_map/product/pallas_call | solution.py:210
  31.0 12.8 %all_to_all.5 = f32[16,16,128]{2,1,0:T(8,128)S(1)} all-to-all(f32[16,16,128]{2,1,0:T(8,128)S(1)} %bitcast.6), channel_id=1, replica_groups=mesh['row'=16,'col'=2] {'row'}, dimensions={0} | all-to-all | bytes 262144 | tf_op jit(solution)/shard_map/all_to_all | solution.py:280
  43.7 0.6 %reduce_sum.9 = f32[16,128]{1,0:T(8,128)} reduce(f32[16,16,128]{2,1,0:T(8,128)S(1)} %all_to_all.5, f32[]{:T(128)} %constant.0.clone.1), dimensions={0}, to_apply=%region_0.0 | reduce | flops 30720 | bytes 139268 | tf_op jit(solution)/shard_map/reduce_sum | solution.py:283
  (11 shorter events, 0.0 us)
Async XLA Ops:
  0.0 4.1 %copy-start.3 = (s32[16,1]{0,1:T(1,128)S(1)}, s32[16,1]{0,1:T(1,128)}, u32[]{:S(2)}) copy-start(s32[16,1]{0,1:T(1,128)} %param.9) | copy-start | bytes 196
  0.0 5.2 %copy-start.2 = (s32[1,128]{1,0:T(1,128)S(1)}, s32[1,128]{1,0:T(1,128)}, u32[]{:S(2)}) copy-start(s32[1,128]{1,0:T(1,128)} %send_ref.3) | copy-start | bytes 1540
  0.0 5.2 %collective-permute-start.3 = (bf16[16,4096]{1,0:T(8,128)(2,1)}, bf16[16,4096]{1,0:T(8,128)(2,1)S(1)}, u32[]{:S(2)}, u32[]{:S(2)}) collective-permute-start(bf16[16,4096]{1,0:T(8,128)(2,1)} %bitcast.7), channel_id=1, source_target_pairs={{0,1},{1,0},{2,3},{3,2},{4,5},{5,4},{6,7},{7,6},{8,9},{9,8},{10,11... | collective-permute-start | bytes 393224 | tf_op jit(solution)/shard_map/ppermute | solution.py:236
  0.5 13.1 %collective-permute-start = (bf16[16,4096]{1,0:T(8,128)(2,1)}, bf16[16,4096]{1,0:T(8,128)(2,1)S(1)}, u32[]{:S(2)}, u32[]{:S(2)}) collective-permute-start(bf16[16,4096]{1,0:T(8,128)(2,1)} %bitcast.8), channel_id=1, source_target_pairs={{0,16},{2,18},{4,20},{6,22},{8,24},{10,26},{12,28},{14,30},{16,0},... | collective-permute-start | bytes 393224 | tf_op jit(solution)/shard_map/ppermute | solution.py:228
  4.1 1.1 %collective-permute-start.2 = (s32[1,16]{1,0:T(1,128)S(1)}, s32[1,16]{1,0:T(1,128)S(1)}, u32[]{:S(2)}, u32[]{:S(2)}) collective-permute-start(s32[1,16]{1,0:T(1,128)S(1)} %bitcast.10), channel_id=1, source_target_pairs={{0,1},{1,0},{2,3},{3,2},{4,5},{5,4},{6,7},{7,6},{8,9},{9,8},{10,11... | collective-permute-start | bytes 200 | tf_op jit(solution)/shard_map/ppermute | solution.py:237
  5.2 0.9 %copy-start.1 = (bf16[16,1,4096]{2,0,1:T(8,128)(2,1)S(1)}, bf16[16,1,4096]{2,0,1:T(8,128)(2,1)}, u32[]{:S(2)}) copy-start(bf16[16,1,4096]{2,0,1:T(8,128)(2,1)} %param.8) | copy-start | bytes 393220
  7.6 7.0 %collective-permute-start.4 = (bf16[264,128]{1,0:T(8,128)(2,1)S(1)}, bf16[264,128]{1,0:T(8,128)(2,1)S(1)}, u32[]{:S(2)}, u32[]{:S(2)}) collective-permute-start(bf16[264,128]{1,0:T(8,128)(2,1)S(1)} %get-tuple-element.35), channel_id=1, source_target_pairs={{0,2},{2,0},{4,6},{6,4},{8,10},{10,8},{12,14},{14,12},{16,18},{18,... | collective-permute-start | bytes 202760 | tf_op jit(solution)/shard_map/ppermute | solution.py:228
  9.1 4.5 %collective-permute-start.1 = (s32[1,144]{1,0:T(1,128)S(1)}, s32[1,144]{1,0:T(1,128)S(1)}, u32[]{:S(2)}, u32[]{:S(2)}) collective-permute-start(s32[1,144]{1,0:T(1,128)S(1)} %pad_add_fusion), channel_id=1, source_target_pairs={{0,16},{2,18},{4,20},{6,22},{8,24},{10,26},{12,28},{14,30},{16,0},... | collective-permute-start | bytes 1736 | tf_op jit(solution)/shard_map/ppermute | solution.py:228
  9.7 1.2 %copy-start = (bf16[16,7,4096]{2,0,1:T(8,128)(2,1)S(1)}, bf16[16,7,4096]{2,0,1:T(8,128)(2,1)}, u32[]{:S(2)}) copy-start(bf16[16,7,4096]{2,0,1:T(8,128)(2,1)} %param.5) | copy-start | bytes 2752516
  14.6 14.5 %copy-start.4 = (s32[16,7]{0,1:T(8,128)S(1)}, s32[16,7]{0,1:T(8,128)}, u32[]{:S(2)}) copy-start(s32[16,7]{0,1:T(8,128)} %param.6) | copy-start | bytes 1348
  14.6 10.2 %collective-permute-start.6 = (bf16[264,128]{1,0:T(8,128)(2,1)S(1)}, bf16[264,128]{1,0:T(8,128)(2,1)S(1)}, u32[]{:S(2)}, u32[]{:S(2)}) collective-permute-start(bf16[264,128]{1,0:T(8,128)(2,1)S(1)} %get-tuple-element.46), channel_id=1, source_target_pairs={{0,14},{2,12},{4,10},{6,8},{8,6},{10,4},{12,2},{14,0},{16,30},{18,... | collective-permute-start | bytes 202760 | tf_op jit(solution)/shard_map/ppermute | solution.py:228
  17.2 5.9 %collective-permute-start.5 = (bf16[136,128]{1,0:T(8,128)(2,1)S(1)}, bf16[136,128]{1,0:T(8,128)(2,1)S(1)}, u32[]{:S(2)}, u32[]{:S(2)}) collective-permute-start(bf16[136,128]{1,0:T(8,128)(2,1)S(1)} %get-tuple-element.44), channel_id=1, source_target_pairs={{0,14},{2,4},{4,2},{6,8},{8,6},{10,12},{12,10},{14,0},{16,30},{18,... | collective-permute-start | bytes 104456 | tf_op jit(solution)/shard_map/ppermute | solution.py:267
  18.5 5.7 %collective-permute-start.12 = (bf16[136,128]{1,0:T(8,128)(2,1)S(1)}, bf16[136,128]{1,0:T(8,128)(2,1)S(1)}, u32[]{:S(2)}, u32[]{:S(2)}) collective-permute-start(bf16[136,128]{1,0:T(8,128)(2,1)S(1)} %get-tuple-element.52), channel_id=1, source_target_pairs={{0,2},{2,0},{4,6},{6,4},{8,10},{10,8},{12,14},{14,12},{16,18},{18,... | collective-permute-start | bytes 104456 | tf_op jit(solution)/shard_map/ppermute | solution.py:228
  19.1 7.4 %collective-permute-start.7 = (bf16[264,128]{1,0:T(8,128)(2,1)S(1)}, bf16[264,128]{1,0:T(8,128)(2,1)S(1)}, u32[]{:S(2)}, u32[]{:S(2)}) collective-permute-start(bf16[264,128]{1,0:T(8,128)(2,1)S(1)} %get-tuple-element.47), channel_id=1, source_target_pairs={{0,10},{2,8},{4,14},{6,12},{8,2},{10,0},{12,6},{14,4},{16,26},{18,... | collective-permute-start | bytes 202760 | tf_op jit(solution)/shard_map/ppermute | solution.py:228
  21.5 5.3 %collective-permute-start.8 = (bf16[264,128]{1,0:T(8,128)(2,1)S(1)}, bf16[264,128]{1,0:T(8,128)(2,1)S(1)}, u32[]{:S(2)}, u32[]{:S(2)}) collective-permute-start(bf16[264,128]{1,0:T(8,128)(2,1)S(1)} %get-tuple-element.48), channel_id=1, source_target_pairs={{0,6},{2,4},{4,2},{6,0},{8,14},{10,12},{12,10},{14,8},{16,22},{18,... | collective-permute-start | bytes 202760 | tf_op jit(solution)/shard_map/ppermute | solution.py:228
  23.0 5.2 %collective-permute-start.9 = (bf16[264,128]{1,0:T(8,128)(2,1)S(1)}, bf16[264,128]{1,0:T(8,128)(2,1)S(1)}, u32[]{:S(2)}, u32[]{:S(2)}) collective-permute-start(bf16[264,128]{1,0:T(8,128)(2,1)S(1)} %get-tuple-element.49), channel_id=1, source_target_pairs={{0,12},{2,14},{4,8},{6,10},{8,4},{10,6},{12,0},{14,2},{16,28},{18,... | collective-permute-start | bytes 202760 | tf_op jit(solution)/shard_map/ppermute | solution.py:228
  24.2 4.3 %collective-permute-start.10 = (bf16[264,128]{1,0:T(8,128)(2,1)S(1)}, bf16[264,128]{1,0:T(8,128)(2,1)S(1)}, u32[]{:S(2)}, u32[]{:S(2)}) collective-permute-start(bf16[264,128]{1,0:T(8,128)(2,1)S(1)} %get-tuple-element.50), channel_id=1, source_target_pairs={{0,8},{2,10},{4,12},{6,14},{8,0},{10,2},{12,4},{14,6},{16,24},{18,... | collective-permute-start | bytes 202760 | tf_op jit(solution)/shard_map/ppermute | solution.py:228
  24.8 4.3 %collective-permute-start.11 = (bf16[264,128]{1,0:T(8,128)(2,1)S(1)}, bf16[264,128]{1,0:T(8,128)(2,1)S(1)}, u32[]{:S(2)}, u32[]{:S(2)}) collective-permute-start(bf16[264,128]{1,0:T(8,128)(2,1)S(1)} %get-tuple-element.51), channel_id=1, source_target_pairs={{0,4},{2,6},{4,0},{6,2},{8,12},{10,14},{12,8},{14,10},{16,20},{18,... | collective-permute-start | bytes 202760 | tf_op jit(solution)/shard_map/ppermute | solution.py:228

commit v6 on v4

--- a/solution.py
+++ b/solution.py
@@ -16,6 +16,7 @@
 BF16 = jnp.bfloat16
 VMEM = pl.BlockSpec(memory_space=pltpu.VMEM)
 SMEM = pl.BlockSpec(memory_space=pltpu.SMEM)
+HBM = pl.BlockSpec(memory_space=pl.ANY)
 PARAMS = pltpu.CompilerParams(vmem_limit_bytes=40 * 2**20)
 
 
@@ -28,9 +29,8 @@
     return jnp.concatenate([x[:, B:], x[:, :B]], axis=1)
 
 
-def turn_rows(flat, index_of, scratch, out, base):
+def turn_rows(index_of, scratch, out, base):
     rows = scratch.shape[0]
-    unpack_rows(flat, scratch)
     for r in range(rows):
         x = scratch[r]
         x = jnp.where(index_of(r) == 0, x, swap_halves(x))
@@ -77,7 +77,8 @@
         def index_of(r, index_ref=index_ref):
             return index_ref[0, r]
 
-        turn_rows(flat_ref, index_of, scratch, turned, 0)
+        unpack_rows(flat_ref, scratch)
+        turn_rows(index_of, scratch, turned, 0)
         masks = mask_table(index_of, rows)
         if j == 0:
             own_ref[rows * PACK :, :] = masks.astype(BF16)
@@ -124,12 +125,23 @@
     return rest[: len(rest) // 2] + edges + rest[len(rest) // 2 :]
 
 
-def pack_kernel(n, steps, send_ref, index_ref, far_ref, own_ref, flat_ref, self_ref, *refs):
+def fetch(sources, targets, sems):
+    copies = [pltpu.make_async_copy(x, y, sems.at[i]) for i, (x, y) in enumerate(zip(sources, targets))]
+    for copy in copies:
+        copy.start()
+    return copies
+
+
+def pack_kernel(n, steps, send_hbm, index_hbm, far_hbm, own_ref, flat_ref, self_ref, *refs):
     rows = flat_ref.shape[0]
-    out_refs, (scratch, table) = refs[: len(steps)], refs[len(steps) :]
+    out_refs, (scratch, table, send_ref, index_ref, far_ref, sems) = refs[: len(steps)], refs[len(steps) :]
+    copies = fetch((send_hbm, index_hbm, far_hbm), (send_ref, index_ref, far_ref), sems)
     me = lax.axis_index("row")
-    turn_rows(flat_ref, lambda r: far_ref[0, n * S + r], scratch, table, rows * PACK)
+    unpack_rows(flat_ref, scratch)
     table[: rows * PACK, :] = own_ref[: rows * PACK, :]
+    for copy in copies:
+        copy.wait()
+    turn_rows(lambda r: far_ref[0, n * S + r], scratch, table, rows * PACK)
 
     def near_row(slot):
         row = send_ref[0, slot]
@@ -152,9 +164,10 @@
     fill(self_ref, table, [far_row(me * S + s) for s in range(S2)])
 
 
-def product_kernel(n, steps, code_ref, self_ref, *refs):
+def product_kernel(n, steps, code_hbm, self_ref, *refs):
     message_refs, refs = refs[: len(steps)], refs[len(steps) :]
-    own_ref, coupling_ref, restrict_ref, out_ref, wide, ap = refs
+    own_ref, coupling_ref, restrict_ref, out_ref, wide, ap, code_ref, sems = refs
+    (copy,) = fetch((code_hbm,), (code_ref,), sems)
     rows = coupling_ref.shape[0]
     span = code_ref.shape[0]
     me = lax.axis_index("row")
@@ -183,6 +196,8 @@
             firsts.append(jnp.where(beside(n, me, near), near, far) * S + S2)
         place_slots(ref, firsts)
 
+    copy.wait()
+
     def row_body(r, carry):
         picked = jnp.concatenate(
             [wide[pl.ds(pl.multiple_of(code_ref[k, r] * B, B), B), :] for k in range(span)], axis=0
@@ -192,7 +207,7 @@
         return carry
 
     lax.fori_loop(0, rows, row_body, 0, unroll=8)
-    out_ref[...] = jnp.dot(restrict_ref[...], ap[...], preferred_element_type=jnp.float32).astype(BF16)
+    out_ref[...] = jnp.dot(restrict_ref[...], ap[...], preferred_element_type=jnp.float32)
 
 
 def shards(n, col_size, a_tiles, neighbors, send_rows, p_tiles, p_index):
@@ -202,15 +217,15 @@
     flat = p_tiles[:, 0, :]
     index = p_index.T
 
-    def call(body, out_shape, scratch_shapes, operands, smem, name, flops=10**7):
+    def call(body, out_shape, scratch_shapes, operands, smem, name, hbm=0):
         return pl.pallas_call(
             body,
             out_shape=out_shape,
-            in_specs=[SMEM] * smem + [VMEM] * (len(operands) - smem),
+            in_specs=[SMEM] * smem + [HBM] * hbm + [VMEM] * (len(operands) - smem - hbm),
             out_specs=jax.tree.map(lambda _: VMEM, out_shape),
             scratch_shapes=scratch_shapes,
             compiler_params=PARAMS,
-            cost_estimate=pl.CostEstimate(flops=flops, bytes_accessed=2**20, transcendentals=0),
+            cost_estimate=pl.CostEstimate(flops=10**7, bytes_accessed=2**20, transcendentals=0),
             name=name,
         )(*operands)
 
@@ -252,26 +267,34 @@
     self_part, *out = call(
         functools.partial(pack_kernel, n, steps),
         [message(S2)] + [message((3 if has_edge(step) else 2) * S2) for step in steps],
-        [unpacked, pltpu.VMEM((2 * rows * PACK, LANES), BF16)],
+        [unpacked, pltpu.VMEM((2 * rows * PACK, LANES), BF16)]
+        + [pltpu.SMEM(x.shape, x.dtype) for x in (send_rows, index, far_ints)]
+        + [pltpu.SemaphoreType.DMA((3,))],
         (send_rows, index, far_ints, own, far_flat),
+        0,
+        "pack",
         3,
-        "pack",
     )
     messages = [swap(x, step) for x, step in zip(out, steps)]
     partial = call(
         functools.partial(product_kernel, n, steps),
-        shape(col_size * CP * B, CP * B),
-        [pltpu.VMEM(((rows + n * S) * B, LANES), BF16), pltpu.VMEM((rows * B, CP * B), BF16)],
+        shape(col_size * CP * B, CP * B, dtype=f32),
+        [
+            pltpu.VMEM(((rows + n * S) * B, LANES), BF16),
+            pltpu.VMEM((rows * B, CP * B), BF16),
+            pltpu.SMEM((span, rows), jnp.int32),
+            pltpu.SemaphoreType.DMA((1,)),
+        ],
         (neighbors.T, self_part, *messages, own, coupling, restrict),
+        0,
+        "product",
         1,
-        "product",
-        2 * 10**8,
     )
     share = col_size * CP * B // n
     parts = lax.all_to_all(
         partial.reshape(n, share, CP * B), "row", split_axis=0, concat_axis=0, tiled=True
     )
-    return jnp.sum(parts.astype(f32), axis=0)
+    return jnp.sum(parts, axis=0)
 
 
 def solution(mesh):

time: 41.7 us -> 41.9 us (level)
  no operation moved by 1% of the time
where the time goes in v6:
time: 41.9 us; the launch traced here: 41.7 us
  starting transfers between devices  14.1 us (34%)
  blocking collectives  13.2 us (32%)
  Pallas kernels  6.26 us (15%)
  waiting for transfers between devices  6.23 us (15%)
  local copies, waits for them, and re-layouts  1.19 us (3%)
  other arithmetic  0.62 us (1%)
    ppermute x9, starting transfers between devices, swap(): return lax.ppermute(x, 'row', [(i, i ^ bits) for i in range(n)])  13.5 us
    all_to_all x1, blocking collectives, shards(): lax.all_to_all(partial.reshape(n, share, CP * B), 'row', split_axis=0, co...  13.2 us
    pallas_call x4, Pallas kernels, call(): pl.pallas_call(body, out_shape=out_shape, in_specs=[SMEM] * smem + [HBM]...  6.26 us
    ppermute x9, waiting for transfers between devices, swap(): return lax.ppermute(x, 'row', [(i, i ^ bits) for i in range(n)])  6.22 us
    unnamed x10, local copies, waits for them, and re-layouts  1.19 us
  transfers between devices with their start and end apart: 11, of which 3 were waited for; matrix products, arithmetic and copies ran while one was open for 0% of the time, Pallas kernels for 8%

profile of v6, /device:TPU:0, one launch (start us, length us, event | category | flops | bytes accessed | tf_op | source)
XLA Modules:
  0.0 41.7 jit_solution(16510691774564338634)
XLA Ops:
  0.0 0.5 %collective-permute-start.3 = (bf16[16,4096]{1,0:T(8,128)(2,1)}, bf16[16,4096]{1,0:T(8,128)(2,1)S(1)}, u32[]{:S(2)}, u32[]{:S(2)}) collective-permute-start(bf16[16,4096]{1,0:T(8,128)(2,1)} %bitcast.7), channel_id=1, source_target_pairs={{0,1},{1,0},{2,3},{3,2},{4,5},{5,4},{6,7},{7,6},{8,9},{9,8},{10,11... | collective-permute-start | bytes 393224 | tf_op jit(solution)/shard_map/ppermute | solution.py:247
  0.5 3.7 %collective-permute-start = (bf16[16,4096]{1,0:T(8,128)(2,1)}, bf16[16,4096]{1,0:T(8,128)(2,1)S(1)}, u32[]{:S(2)}, u32[]{:S(2)}) collective-permute-start(bf16[16,4096]{1,0:T(8,128)(2,1)} %bitcast.8), channel_id=1, source_target_pairs={{0,16},{2,18},{4,20},{6,22},{8,24},{10,26},{12,28},{14,30},{16,0},... | collective-permute-start | bytes 393224 | tf_op jit(solution)/shard_map/ppermute | solution.py:239
  4.1 0.0 copy-done.2
  4.1 0.2 collective-permute-start.2
  4.3 0.0 copy-done.4
  4.3 0.5 %collective-permute-start.1 = (s32[1,144]{1,0:T(1,128)S(1)}, s32[1,144]{1,0:T(1,128)S(1)}, u32[]{:S(2)}, u32[]{:S(2)}) collective-permute-start(s32[1,144]{1,0:T(1,128)S(1)} %pad_add_fusion), channel_id=1, source_target_pairs={{0,16},{2,18},{4,20},{6,22},{8,24},{10,26},{12,28},{14,30},{16,0},... | collective-permute-start | bytes 1736 | tf_op jit(solution)/shard_map/ppermute | solution.py:239
  4.8 1.2 %copy-done = bf16[16,7,4096]{2,0,1:T(8,128)(2,1)S(1)} copy-done((bf16[16,7,4096]{2,0,1:T(8,128)(2,1)S(1)}, bf16[16,7,4096]{2,0,1:T(8,128)(2,1)}, u32[]{:S(2)}) %copy-start) | copy-done | bytes 917528
  6.0 2.1 %coupling.1.refs_8_ = bf16[16,64,512]{2,1,0:T(8,128)(2,1)S(1)} custom-call(bf16[7,16,4096]{2,1,0:T(8,128)(2,1)S(1)} %bitcast.5), custom_call_target="tpu_custom_call" | custom-call | flops 10000000 | bytes 1048576 | tf_op jit(solution)/shard_map/coupling/pallas_call | solution.py:221
  8.1 0.0 collective-permute-done.2.refs_1_
  8.1 0.0 collective-permute-done.3.refs_3_
  8.1 1.4 %prepare.1 = (bf16[528,128]{1,0:T(8,128)(2,1)S(1)}, bf16[256,1024]{1,0:T(8,128)(2,1)S(1)}) custom-call(s32[1,16]{1,0:T(1,128)S(1)} %bitcast.12, s32[1,16]{1,0:T(1,128)S(1)} %collective-permute-done.2.refs_1_, bf16[16,4096]{1,0:T(8,128)(2,1)S(1)} %bitcast.9, bf16[16,4096]{1,0:T(8,128)(2,1)S(1)} %collective-permute-done.3.refs_3_), custom_call_target="tpu_custom_call" | custom-call | flops 10000000 | bytes 1048576 | tf_op jit(solution)/shard_map/prepare/pallas_call | solution.py:221
  9.5 1.8 %collective-permute-done.1.far_hbm = s32[1,144]{1,0:T(1,128)S(1)} collective-permute-done((s32[1,144]{1,0:T(1,128)S(1)}, s32[1,144]{1,0:T(1,128)S(1)}, u32[]{:S(2)}, u32[]{:S(2)}) %collective-permute-start.1) | collective-permute-done | bytes 608 | tf_op jit(solution)/shard_map/ppermute | solution.py:239
  11.3 0.0 collective-permute-done.flat_ref
  11.3 0.9 %pack.1 = (bf16[136,128]{1,0:T(8,128)(2,1)S(1)}, bf16[264,128]{1,0:T(8,128)(2,1)S(1)}, bf16[264,128]{1,0:T(8,128)(2,1)S(1)}, bf16[400,128]{1,0:T(8,128)(2,1)S(1)...) custom-call(s32[1,128]{1,0:T(1,128)S(1)} %copy-done.4, ...), custom_call_target="tpu_custom_call" | custom-call | flops 10000000 | bytes 1048576 | tf_op jit(solution)/shard_map/pack/pallas_call | solution.py:221
  12.3 1.8 %collective-permute-start.4 = (bf16[264,128]{1,0:T(8,128)(2,1)S(1)}, bf16[264,128]{1,0:T(8,128)(2,1)S(1)}, u32[]{:S(2)}, u32[]{:S(2)}) collective-permute-start(bf16[264,128]{1,0:T(8,128)(2,1)S(1)} %get-tuple-element.24), channel_id=1, source_target_pairs={{0,10},{2,8},{4,14},{6,12},{8,2},{10,0},{12,6},{14,4},{16,26},{18,... | collective-permute-start | bytes 202760 | tf_op jit(solution)/shard_map/ppermute | solution.py:239
  14.0 2.3 %collective-permute-start.5 = (bf16[264,128]{1,0:T(8,128)(2,1)S(1)}, bf16[264,128]{1,0:T(8,128)(2,1)S(1)}, u32[]{:S(2)}, u32[]{:S(2)}) collective-permute-start(bf16[264,128]{1,0:T(8,128)(2,1)S(1)} %get-tuple-element.25), channel_id=1, source_target_pairs={{0,12},{2,14},{4,8},{6,10},{8,4},{10,6},{12,0},{14,2},{16,28},{18,... | collective-permute-start | bytes 202760 | tf_op jit(solution)/shard_map/ppermute | solution.py:239
  16.3 0.6 %collective-permute-start.6 = (bf16[400,128]{1,0:T(8,128)(2,1)S(1)}, bf16[400,128]{1,0:T(8,128)(2,1)S(1)}, u32[]{:S(2)}, u32[]{:S(2)}) collective-permute-start(bf16[400,128]{1,0:T(8,128)(2,1)S(1)} %get-tuple-element.26), channel_id=1, source_target_pairs={{0,14},{2,12},{4,10},{6,8},{8,6},{10,4},{12,2},{14,0},{16,30},{18,... | collective-permute-start | bytes 307208 | tf_op jit(solution)/shard_map/ppermute | solution.py:239
  16.9 2.4 %collective-permute-start.7 = (bf16[400,128]{1,0:T(8,128)(2,1)S(1)}, bf16[400,128]{1,0:T(8,128)(2,1)S(1)}, u32[]{:S(2)}, u32[]{:S(2)}) collective-permute-start(bf16[400,128]{1,0:T(8,128)(2,1)S(1)} %get-tuple-element.27), channel_id=1, source_target_pairs={{0,6},{2,4},{4,2},{6,0},{8,14},{10,12},{12,10},{14,8},{16,22},{18,... | collective-permute-start | bytes 307208 | tf_op jit(solution)/shard_map/ppermute | solution.py:239
  19.4 0.5 %collective-permute-start.8 = (bf16[400,128]{1,0:T(8,128)(2,1)S(1)}, bf16[400,128]{1,0:T(8,128)(2,1)S(1)}, u32[]{:S(2)}, u32[]{:S(2)}) collective-permute-start(bf16[400,128]{1,0:T(8,128)(2,1)S(1)} %get-tuple-element.28), channel_id=1, source_target_pairs={{0,2},{2,0},{4,6},{6,4},{8,10},{10,8},{12,14},{14,12},{16,18},{18,... | collective-permute-start | bytes 307208 | tf_op jit(solution)/shard_map/ppermute | solution.py:239
  19.9 0.0 collective-permute-done.4.refs_0_
  19.9 0.5 %collective-permute-start.9 = (bf16[264,128]{1,0:T(8,128)(2,1)S(1)}, bf16[264,128]{1,0:T(8,128)(2,1)S(1)}, u32[]{:S(2)}, u32[]{:S(2)}) collective-permute-start(bf16[264,128]{1,0:T(8,128)(2,1)S(1)} %get-tuple-element.29), channel_id=1, source_target_pairs={{0,4},{2,6},{4,0},{6,2},{8,12},{10,14},{12,8},{14,10},{16,20},{18,... | collective-permute-start | bytes 202760 | tf_op jit(solution)/shard_map/ppermute | solution.py:239
  20.4 0.0 collective-permute-done.5.refs_1_
  20.5 1.2 %collective-permute-start.10 = (bf16[264,128]{1,0:T(8,128)(2,1)S(1)}, bf16[264,128]{1,0:T(8,128)(2,1)S(1)}, u32[]{:S(2)}, u32[]{:S(2)}) collective-permute-start(bf16[264,128]{1,0:T(8,128)(2,1)S(1)} %get-tuple-element.30), channel_id=1, source_target_pairs={{0,8},{2,10},{4,12},{6,14},{8,0},{10,2},{12,4},{14,6},{16,24},{18,... | collective-permute-start | bytes 202760 | tf_op jit(solution)/shard_map/ppermute | solution.py:239
  21.7 4.1 %collective-permute-done.9.refs_5_ = bf16[264,128]{1,0:T(8,128)(2,1)S(1)} collective-permute-done((bf16[264,128]{1,0:T(8,128)(2,1)S(1)}, bf16[264,128]{1,0:T(8,128)(2,1)S(1)}, u32[]{:S(2)}, u32[]{:S(2)}) %collective-permute-start.9) | collective-permute-done | bytes 67616 | tf_op jit(solution)/shard_map/ppermute | solution.py:239
  25.7 0.0 collective-permute-done.10.refs_6_
  25.7 0.0 collective-permute-done.6.refs_2_
  25.7 0.0 collective-permute-done.7.refs_3_
  25.8 0.3 collective-permute-done.8.refs_4_
  26.0 0.0 copy-done.3
  26.0 1.8 %product.1 = f32[256,128]{1,0:T(8,128)S(1)} custom-call(s32[7,16]{1,0:T(8,128)S(1)} %bitcast.14, bf16[136,128]{1,0:T(8,128)(2,1)S(1)} %get-tuple-element.23.self_ref, bf16[264,128]{1,0:T(8,128)(2,1)S(1)} %collective-permute-done.4.refs_0_, bf16[264,128]{1,0:T(8,128)(2,1)S(1)} %collective-permute-done.5.refs_1_, ...), custom_call_target="tpu_custom_call" | custom-call | flops 10000000 | bytes 1048576 | tf_op jit(solution)/shard_map/product/pallas_call | solution.py:221
  27.9 13.2 %all_to_all.5 = f32[16,16,128]{2,1,0:T(8,128)S(1)} all-to-all(f32[16,16,128]{2,1,0:T(8,128)S(1)} %bitcast.6), channel_id=1, replica_groups=mesh['row'=16,'col'=2] {'row'}, dimensions={0} | all-to-all | bytes 262144 | tf_op jit(solution)/shard_map/all_to_all | solution.py:294
  41.1 0.6 %reduce_sum.9 = f32[16,128]{1,0:T(8,128)} reduce(f32[16,16,128]{2,1,0:T(8,128)S(1)} %all_to_all.5, f32[]{:T(128)} %constant.0.clone.1), dimensions={0}, to_apply=%region_0.0 | reduce | flops 30720 | bytes 139268 | tf_op jit(solution)/shard_map/reduce_sum | solution.py:297
  (7 shorter events, 0.0 us)
Async XLA Ops:
  0.0 4.1 %copy-start.2 = (s32[16,1]{0,1:T(1,128)S(1)}, s32[16,1]{0,1:T(1,128)}, u32[]{:S(2)}) copy-start(s32[16,1]{0,1:T(1,128)} %param.9) | copy-start | bytes 196
  0.0 4.3 %copy-start.4 = (s32[1,128]{1,0:T(1,128)S(1)}, s32[1,128]{1,0:T(1,128)}, u32[]{:S(2)}) copy-start(s32[1,128]{1,0:T(1,128)} %send_hbm.1) | copy-start | bytes 1540
  0.0 8.1 %collective-permute-start.3 = (bf16[16,4096]{1,0:T(8,128)(2,1)}, bf16[16,4096]{1,0:T(8,128)(2,1)S(1)}, u32[]{:S(2)}, u32[]{:S(2)}) collective-permute-start(bf16[16,4096]{1,0:T(8,128)(2,1)} %bitcast.7), channel_id=1, source_target_pairs={{0,1},{1,0},{2,3},{3,2},{4,5},{5,4},{6,7},{7,6},{8,9},{9,8},{10,11... | collective-permute-start | bytes 393224 | tf_op jit(solution)/shard_map/ppermute | solution.py:247
  0.5 10.9 %collective-permute-start = (bf16[16,4096]{1,0:T(8,128)(2,1)}, bf16[16,4096]{1,0:T(8,128)(2,1)S(1)}, u32[]{:S(2)}, u32[]{:S(2)}) collective-permute-start(bf16[16,4096]{1,0:T(8,128)(2,1)} %bitcast.8), channel_id=1, source_target_pairs={{0,16},{2,18},{4,20},{6,22},{8,24},{10,26},{12,28},{14,30},{16,0},... | collective-permute-start | bytes 393224 | tf_op jit(solution)/shard_map/ppermute | solution.py:239
  4.1 3.9 %collective-permute-start.2 = (s32[1,16]{1,0:T(1,128)S(1)}, s32[1,16]{1,0:T(1,128)S(1)}, u32[]{:S(2)}, u32[]{:S(2)}) collective-permute-start(s32[1,16]{1,0:T(1,128)S(1)} %bitcast.10), channel_id=1, source_target_pairs={{0,1},{1,0},{2,3},{3,2},{4,5},{5,4},{6,7},{7,6},{8,9},{9,8},{10,11... | collective-permute-start | bytes 200 | tf_op jit(solution)/shard_map/ppermute | solution.py:248
  4.3 7.0 %collective-permute-start.1 = (s32[1,144]{1,0:T(1,128)S(1)}, s32[1,144]{1,0:T(1,128)S(1)}, u32[]{:S(2)}, u32[]{:S(2)}) collective-permute-start(s32[1,144]{1,0:T(1,128)S(1)} %pad_add_fusion), channel_id=1, source_target_pairs={{0,16},{2,18},{4,20},{6,22},{8,24},{10,26},{12,28},{14,30},{16,0},... | collective-permute-start | bytes 1736 | tf_op jit(solution)/shard_map/ppermute | solution.py:239
  4.8 1.2 %copy-start = (bf16[16,7,4096]{2,0,1:T(8,128)(2,1)S(1)}, bf16[16,7,4096]{2,0,1:T(8,128)(2,1)}, u32[]{:S(2)}) copy-start(bf16[16,7,4096]{2,0,1:T(8,128)(2,1)} %param.5) | copy-start | bytes 2752516
  6.0 2.1 %copy-start.1 = (bf16[16,1,4096]{2,0,1:T(8,128)(2,1)S(1)}, bf16[16,1,4096]{2,0,1:T(8,128)(2,1)}, u32[]{:S(2)}) copy-start(bf16[16,1,4096]{2,0,1:T(8,128)(2,1)} %param.8) | copy-start | bytes 393220
  12.3 7.7 %collective-permute-start.4 = (bf16[264,128]{1,0:T(8,128)(2,1)S(1)}, bf16[264,128]{1,0:T(8,128)(2,1)S(1)}, u32[]{:S(2)}, u32[]{:S(2)}) collective-permute-start(bf16[264,128]{1,0:T(8,128)(2,1)S(1)} %get-tuple-element.24), channel_id=1, source_target_pairs={{0,10},{2,8},{4,14},{6,12},{8,2},{10,0},{12,6},{14,4},{16,26},{18,... | collective-permute-start | bytes 202760 | tf_op jit(solution)/shard_map/ppermute | solution.py:239
  14.0 6.4 %collective-permute-start.5 = (bf16[264,128]{1,0:T(8,128)(2,1)S(1)}, bf16[264,128]{1,0:T(8,128)(2,1)S(1)}, u32[]{:S(2)}, u32[]{:S(2)}) collective-permute-start(bf16[264,128]{1,0:T(8,128)(2,1)S(1)} %get-tuple-element.25), channel_id=1, source_target_pairs={{0,12},{2,14},{4,8},{6,10},{8,4},{10,6},{12,0},{14,2},{16,28},{18,... | collective-permute-start | bytes 202760 | tf_op jit(solution)/shard_map/ppermute | solution.py:239
  16.3 9.4 %collective-permute-start.6 = (bf16[400,128]{1,0:T(8,128)(2,1)S(1)}, bf16[400,128]{1,0:T(8,128)(2,1)S(1)}, u32[]{:S(2)}, u32[]{:S(2)}) collective-permute-start(bf16[400,128]{1,0:T(8,128)(2,1)S(1)} %get-tuple-element.26), channel_id=1, source_target_pairs={{0,14},{2,12},{4,10},{6,8},{8,6},{10,4},{12,2},{14,0},{16,30},{18,... | collective-permute-start | bytes 307208 | tf_op jit(solution)/shard_map/ppermute | solution.py:239
  16.9 8.8 %collective-permute-start.7 = (bf16[400,128]{1,0:T(8,128)(2,1)S(1)}, bf16[400,128]{1,0:T(8,128)(2,1)S(1)}, u32[]{:S(2)}, u32[]{:S(2)}) collective-permute-start(bf16[400,128]{1,0:T(8,128)(2,1)S(1)} %get-tuple-element.27), channel_id=1, source_target_pairs={{0,6},{2,4},{4,2},{6,0},{8,14},{10,12},{12,10},{14,8},{16,22},{18,... | collective-permute-start | bytes 307208 | tf_op jit(solution)/shard_map/ppermute | solution.py:239
  19.4 6.7 %collective-permute-start.8 = (bf16[400,128]{1,0:T(8,128)(2,1)S(1)}, bf16[400,128]{1,0:T(8,128)(2,1)S(1)}, u32[]{:S(2)}, u32[]{:S(2)}) collective-permute-start(bf16[400,128]{1,0:T(8,128)(2,1)S(1)} %get-tuple-element.28), channel_id=1, source_target_pairs={{0,2},{2,0},{4,6},{6,4},{8,10},{10,8},{12,14},{14,12},{16,18},{18,... | collective-permute-start | bytes 307208 | tf_op jit(solution)/shard_map/ppermute | solution.py:239
  19.9 6.1 %copy-start.3 = (s32[16,7]{0,1:T(8,128)S(1)}, s32[16,7]{0,1:T(8,128)}, u32[]{:S(2)}) copy-start(s32[16,7]{0,1:T(8,128)} %param.6) | copy-start | bytes 1348
  19.9 5.8 %collective-permute-start.9 = (bf16[264,128]{1,0:T(8,128)(2,1)S(1)}, bf16[264,128]{1,0:T(8,128)(2,1)S(1)}, u32[]{:S(2)}, u32[]{:S(2)}) collective-permute-start(bf16[264,128]{1,0:T(8,128)(2,1)S(1)} %get-tuple-element.29), channel_id=1, source_target_pairs={{0,4},{2,6},{4,0},{6,2},{8,12},{10,14},{12,8},{14,10},{16,20},{18,... | collective-permute-start | bytes 202760 | tf_op jit(solution)/shard_map/ppermute | solution.py:239
  20.5 5.3 %collective-permute-start.10 = (bf16[264,128]{1,0:T(8,128)(2,1)S(1)}, bf16[264,128]{1,0:T(8,128)(2,1)S(1)}, u32[]{:S(2)}, u32[]{:S(2)}) collective-permute-start(bf16[264,128]{1,0:T(8,128)(2,1)S(1)} %get-tuple-element.30), channel_id=1, source_target_pairs={{0,8},{2,10},{4,12},{6,14},{8,0},{10,2},{12,4},{14,6},{16,24},{18,... | collective-permute-start | bytes 202760 | tf_op jit(solution)/shard_map/ppermute | solution.py:239

commit v7 on v2

--- a/solution.py
+++ b/solution.py
@@ -64,11 +64,13 @@
     ref[(*block, pl.ds(len(picks) * PACK, marks), slice(None))] = mark.astype(BF16)
 
 
-def own_kernel(n, send_ref, index_ref, flat_ref, own_ref, near_ref, left_ref, right_ref, scratch):
+def alternating(n):
+    return [i // 2 + i % 2 * (n // 2) for i in range(n)]
+
+
+def own_kernel(n, send_ref, index_ref, flat_ref, own_ref, out_ref, left_ref, right_ref, scratch):
     rows = flat_ref.shape[0]
-    half = n // 2
     me = lax.axis_index("row")
-    base = me - lax.rem(me, half)
     turn_rows(flat_ref, lambda r: index_ref[0, r], scratch, own_ref, 0)
     own_ref[rows * PACK :, :] = mask_table(lambda r: index_ref[0, r], rows).astype(BF16)
 
@@ -76,25 +78,11 @@
         row = send_ref[0, slot]
         return row, index_ref[0, row]
 
-    for j in range(half):
-        fill(near_ref, (j,), own_ref, [look((base + j) * S + s) for s in range(S2)], 8)
+    for j, target in enumerate(alternating(n)):
+        fill(out_ref, (j,), own_ref, [look(target * S + s) for s in range(S2)], 8)
     for ref, step in ((left_ref, n - 1), (right_ref, 1)):
         first = lax.rem(me + step, n) * S
         fill(ref, (), own_ref, [look(first + s) for s in range(S2, S)], 8)
-
-
-def far_kernel(n, far_ref, flat_ref, out_ref, scratch, table):
-    half = n // 2
-    me = lax.axis_index("row")
-    base = me - lax.rem(me, half)
-    turn_rows(flat_ref, lambda r: far_ref[0, n * S + r], scratch, table, 0)
-
-    def look(slot):
-        row = far_ref[0, slot]
-        return row, far_ref[0, n * S + row]
-
-    for j in range(half):
-        fill(out_ref, (j,), table, [look((base + j) * S + s) for s in range(S2)], 8)
 
 
 def coupling_kernel(a_ref, coupling_ref, scratch):
@@ -132,13 +120,11 @@
 
 
 def product_kernel(
-    n, code_ref, near_ref, far_ref, left_ref, right_ref, own_ref, coupling_ref, restrict_ref, out_ref, wide, ap
+    n, code_ref, ghost_ref, left_ref, right_ref, own_ref, coupling_ref, restrict_ref, out_ref, wide, ap
 ):
-    half = n // 2
     rows = coupling_ref.shape[0]
     span = code_ref.shape[0]
     me = lax.axis_index("row")
-    base = me - lax.rem(me, half)
 
     def place(slot, tile, mask):
         even, odd = widen(tile, mask)
@@ -153,9 +139,8 @@
 
     for r in range(rows):
         place(r, own_ref[r * PACK : (r + 1) * PACK, :], own_ref[rows * PACK + r : rows * PACK + r + 1, :])
-    for j in range(half):
-        place_slots((base + j) * S, near_ref, (j,))
-        place_slots(lax.rem(base + half + j, n) * S, far_ref, (j,))
+    for j, source in enumerate(alternating(n)):
+        place_slots(source * S, ghost_ref, (j,))
     for ref, step in ((left_ref, n - 1), (right_ref, 1)):
         place_slots(lax.rem(me + step, n) * S + S2, ref, ())
 
@@ -168,13 +153,14 @@
         return carry
 
     lax.fori_loop(0, rows, row_body, 0, unroll=8)
-    out_ref[...] = jnp.dot(restrict_ref[...], ap[...], preferred_element_type=jnp.float32)
+    coarse = jnp.dot(restrict_ref[...], ap[...], preferred_element_type=jnp.float32)
+    share = out_ref.shape[0] // n
+    for j, target in enumerate(alternating(n)):
+        out_ref[j * share : (j + 1) * share, :] = coarse[target * share : (target + 1) * share]
 
 
 def shards(n, col_size, a_tiles, neighbors, send_rows, p_tiles, p_index):
     rows, span = a_tiles.shape[0], a_tiles.shape[1]
-    half = n // 2
-    halves = [list(range(half)), list(range(half, n))]
     flat = p_tiles[:, 0, :]
     index = p_index.T
     f32 = jnp.float32
@@ -195,17 +181,17 @@
         return jax.ShapeDtypeStruct(dims, dtype)
 
     def exchange(x):
-        return lax.all_to_all(x, "row", split_axis=0, concat_axis=0, tiled=True, axis_index_groups=halves)
+        return lax.all_to_all(
+            x, "row", split_axis=0, concat_axis=0, tiled=True, axis_index_groups=[alternating(n)]
+        )
 
     def ring(x, step):
         return lax.ppermute(x, "row", [(i, (i + step) % n) for i in range(n)])
 
     unpacked = pltpu.VMEM((rows, PACK, LANES), f32)
-    far_flat = ring(flat, half)
-    far_ints = ring(jnp.concatenate([send_rows, index], axis=1), half)
     edge = shape(S2 * PACK + 8, LANES)
-    blocks = shape(half, S2 * PACK + 8, LANES)
-    own, near, left, right = call(
+    blocks = shape(n, S2 * PACK + 8, LANES)
+    own, out, left, right = call(
         functools.partial(own_kernel, n),
         [shape(rows * PACK + rows, LANES), blocks, edge, edge],
         [unpacked],
@@ -213,25 +199,13 @@
         2,
         "own",
     )
-    near = exchange(near)
+    out, own, left, right, a_tiles = lax.optimization_barrier((out, own, left, right, a_tiles))
+    ghosts = exchange(out)
     from_right, from_left = ring(left, n - 1), ring(right, 1)
     panels = [own] + [
         lax.ppermute(own, "col", [(i, (i + j) % col_size) for i in range(col_size)])
         for j in range(1, col_size)
     ]
-    far = call(
-        functools.partial(far_kernel, n),
-        blocks,
-        [unpacked, pltpu.VMEM((rows * PACK, LANES), BF16)],
-        (far_ints, far_flat),
-        1,
-        "far",
-        10**13,
-    )
-    far, near, from_left, from_right, a_tiles = lax.optimization_barrier(
-        (far, near, from_left, from_right, a_tiles)
-    )
-    far = exchange(far)
     coupling = call(
         coupling_kernel,
         shape(rows, B, pl.cdiv(span, 2) * LANES),
@@ -254,15 +228,12 @@
         functools.partial(product_kernel, n),
         shape(col_size * CP * B, CP * B, dtype=f32),
         [pltpu.VMEM(((rows + n * S) * B, LANES), BF16), pltpu.VMEM((rows * B, CP * B), BF16)],
-        (neighbors.T, near, far, from_left, from_right, own, coupling, restrict),
+        (neighbors.T, ghosts, from_left, from_right, own, coupling, restrict),
         1,
         "product",
         2 * 10**8,
     )
-    share = col_size * CP * B // n
-    parts = lax.all_to_all(
-        partial.reshape(n, share, CP * B), "row", split_axis=0, concat_axis=0, tiled=True
-    )
+    parts = exchange(partial.reshape(n, col_size * CP * B // n, CP * B))
     return jnp.sum(parts, axis=0)
 
 

time: 46.6 us -> 42 us (0.901)
  starting transfers between devices: 18.5 us -> 14 us
  waiting for transfers between devices: 6.17 us -> 8.41 us
  Pallas kernels: 7.88 us -> 6.02 us
  blocking collectives: 12 us -> 11 us
  local copies, waits for them, and re-layouts: 0.92 us -> 1.58 us
    ppermute x4 -> x2, waiting for transfers between devices: 2.05 us -> 7.52 us  [ring(): return lax.ppermute(x, 'row', [(i, (i + step) % n) for i in range(n)])]
    ppermute x4 -> x2, starting transfers between devices: 10.3 us -> 5.67 us  [ring(): return lax.ppermute(x, 'row', [(i, (i + step) % n) for i in range(n)])]
    all_to_all x2 -> x1, waiting for transfers between devices: 2.78 us -> 0.9 us  [exchange(): lax.all_to_all(x, 'row', split_axis=0, concat_axis=0, tiled=True, axis_in...]
    pallas_call x5 -> x4, Pallas kernels: 7.88 us -> 6.02 us  [call(): pl.pallas_call(body, out_shape=out_shape, in_specs=[SMEM] * smem + [VMEM]...]
    ppermute x1, waiting for transfers between devices: 1.34 us -> 0.01 us  [shards(): lax.ppermute(own, 'col', [(i, (i + j) % col_size) for i in range(col_size)])]
    all_to_all x1, blocking collectives: 12 us -> 11 us  [exchange(): lax.all_to_all(x, 'row', split_axis=0, concat_axis=0, tiled=True, axis_in...]
    unnamed x10, local copies, waits for them, and re-layouts: 0.92 us -> 1.58 us
    all_to_all x2 -> x1, starting transfers between devices: 8.15 us -> 8.31 us  [exchange(): lax.all_to_all(x, 'row', split_axis=0, concat_axis=0, tiled=True, axis_in...]
  transfers between devices with their start and end apart: 7 -> 4, of which waited for: 3 -> 2; matrix products, arithmetic and copies ran while one was open for 0% -> 0% of each run, Pallas kernels for 12% -> 6%
where the time goes in v7:
time: 42 us; the launch traced here: 41.7 us
  starting transfers between devices  14 us (33%)
  blocking collectives  11 us (26%)
  waiting for transfers between devices  8.41 us (20%)
  Pallas kernels  6.02 us (14%)
  local copies, waits for them, and re-layouts  1.58 us (4%)
  other arithmetic  0.62 us (1%)
    all_to_all x1, blocking collectives, exchange(): lax.all_to_all(x, 'row', split_axis=0, concat_axis=0, tiled=True, axis_in...  11 us
    all_to_all x1, starting transfers between devices, exchange(): lax.all_to_all(x, 'row', split_axis=0, concat_axis=0, tiled=True, axis_in...  8.31 us
    ppermute x2, waiting for transfers between devices, ring(): return lax.ppermute(x, 'row', [(i, (i + step) % n) for i in range(n)])  7.52 us
    pallas_call x4, Pallas kernels, call(): pl.pallas_call(body, out_shape=out_shape, in_specs=[SMEM] * smem + [VMEM]...  6.02 us
    ppermute x2, starting transfers between devices, ring(): return lax.ppermute(x, 'row', [(i, (i + step) % n) for i in range(n)])  5.67 us
    unnamed x10, local copies, waits for them, and re-layouts  1.58 us
    all_to_all x1, waiting for transfers between devices, exchange(): lax.all_to_all(x, 'row', split_axis=0, concat_axis=0, tiled=True, axis_in...  0.9 us
  transfers between devices with their start and end apart: 4, of which 2 were waited for; matrix products, arithmetic and copies ran while one was open for 0% of the time, Pallas kernels for 6%

profile of v7, /device:TPU:0, one launch (start us, length us, event | category | flops | bytes accessed | tf_op | source)
XLA Modules:
  0.0 41.7 jit_solution(11494984144973750143)
XLA Ops:
  0.0 0.0 copy-start.2
  0.0 0.0 copy-start.3
  0.0 0.7 %copy-done.2 = s32[1,128]{1,0:T(1,128)S(1)} copy-done((s32[1,128]{1,0:T(1,128)S(1)}, s32[1,128]{1,0:T(1,128)}, u32[]{:S(2)}) %copy-start.2) | copy-done | bytes 536
  0.7 0.0 copy-done.3
  0.7 0.0 copy-start
  0.7 0.9 %copy-done = bf16[16,1,4096]{2,0,1:T(8,128)(2,1)S(1)} copy-done((bf16[16,1,4096]{2,0,1:T(8,128)(2,1)S(1)}, bf16[16,1,4096]{2,0,1:T(8,128)(2,1)}, u32[]{:S(2)}) %copy-start) | copy-done | bytes 131096
  1.6 0.0 copy-start.4
  1.6 1.8 %own.1 = (bf16[528,128]{1,0:T(8,128)(2,1)S(1)}, bf16[16,136,128]{2,1,0:T(8,128)(2,1)}, bf16[136,128]{1,0:T(8,128)(2,1)S(1)}, bf16[136,128]{1,0:T(8,128)(2,1)S(1)}) custom-call(s32[1,128]{1,0:T(1,128)S(1)} %copy-done.2, s32[1,16]{1,0:T(1,128)S(1)} %bitcast.8, bf16[16,4096]{1,0:T(8,128)(2,1)S(1)} %bitcast.6), custom_call_target="tpu_custom_call" | custom-call | flops 10000000 | bytes 1048576 | tf_op jit(solution)/shard_map/own/pallas_call | solution.py:169
  3.4 8.3 %all-to-all-start = ((bf16[16,136,128]{2,1,0:T(8,128)(2,1)}), bf16[16,136,128]{2,1,0:T(8,128)(2,1)S(1)}, u32[]{:S(2)}, u32[]{:S(2)}) async-start(bf16[16,136,128]{2,1,0:T(8,128)(2,1)} %get-tuple-element.18), calls=%async_computation | async-start | bytes 1114112 | tf_op jit(solution)/shard_map/all_to_all | solution.py:184
  11.7 1.9 %collective-permute-start = (bf16[136,128]{1,0:T(8,128)(2,1)S(1)}, bf16[136,128]{1,0:T(8,128)(2,1)S(1)}, u32[]{:S(2)}, u32[]{:S(2)}) collective-permute-start(bf16[136,128]{1,0:T(8,128)(2,1)S(1)} %get-tuple-element.19), channel_id=1, source_target_pairs={{0,2},{2,4},{4,6},{6,8},{8,10},{10,12},{12,14},{14,16},{16,18},{18... | collective-permute-start | bytes 104456 | tf_op jit(solution)/shard_map/ppermute | solution.py:189
  13.6 3.7 %collective-permute-start.1 = (bf16[136,128]{1,0:T(8,128)(2,1)S(1)}, bf16[136,128]{1,0:T(8,128)(2,1)S(1)}, u32[]{:S(2)}, u32[]{:S(2)}) collective-permute-start(bf16[136,128]{1,0:T(8,128)(2,1)S(1)} %get-tuple-element.20), channel_id=1, source_target_pairs={{0,30},{2,0},{4,2},{6,4},{8,6},{10,8},{12,10},{14,12},{16,14},{18,... | collective-permute-start | bytes 104456 | tf_op jit(solution)/shard_map/ppermute | solution.py:189
  17.4 0.0 collective-permute-start.2
  17.4 0.0 copy-done.4
  17.4 2.1 %coupling.1.coupling_ref = bf16[16,64,512]{2,1,0:T(8,128)(2,1)S(1)} custom-call(bf16[7,16,4096]{2,1,0:T(8,128)(2,1)S(1)} %bitcast.9), custom_call_target="tpu_custom_call" | custom-call | flops 2000000000 | bytes 1048576 | tf_op jit(solution)/shard_map/coupling/pallas_call | solution.py:169
  19.5 0.0 collective-permute-done.2.refs_1_
  19.5 0.0 copy-start.1
  19.5 0.3 restrict.1.restrict_ref
  19.8 7.5 %collective-permute-done.left_ref = bf16[136,128]{1,0:T(8,128)(2,1)S(1)} collective-permute-done((bf16[136,128]{1,0:T(8,128)(2,1)S(1)}, bf16[136,128]{1,0:T(8,128)(2,1)S(1)}, u32[]{:S(2)}, u32[]{:S(2)}) %collective-permute-start) | collective-permute-done | bytes 34848 | tf_op jit(solution)/shard_map/ppermute | solution.py:189
  27.3 0.0 collective-permute-done.1.right_ref
  27.3 0.9 %all-to-all-done.ghost_ref = bf16[16,136,128]{2,1,0:T(8,128)(2,1)S(1)} async-done(((bf16[16,136,128]{2,1,0:T(8,128)(2,1)}), bf16[16,136,128]{2,1,0:T(8,128)(2,1)S(1)}, u32[]{:S(2)}, u32[]{:S(2)}) %all-to-all-start) | async-done | bytes 557088 | tf_op jit(solution)/shard_map/all_to_all | solution.py:184
  28.2 0.0 copy-done.1
  28.2 1.8 %product.1 = f32[256,128]{1,0:T(8,128)S(1)} custom-call(s32[7,16]{1,0:T(8,128)S(1)} %bitcast.7, bf16[16,136,128]{2,1,0:T(8,128)(2,1)S(1)} %all-to-all-done.ghost_ref, bf16[136,128]{1,0:T(8,128)(2,1)S(1)} %collective-permute-done.left_ref, bf16[136,128]{1,0:T(8,128)(2,1)S(1)} %collective-permute-done.1.right_ref, ...), custom_call_target="tpu_custom_call" | custom-call | flops 200000000 | bytes 1048576 | tf_op jit(solution)/shard_map/product/pallas_call | solution.py:169
  30.0 11.0 %all_to_all.10 = f32[16,16,128]{2,1,0:T(8,128)S(1)} all-to-all(f32[16,16,128]{2,1,0:T(8,128)S(1)} %bitcast.5), channel_id=1, replica_groups={{0,16,2,18,4,20,6,22,8,24,10,26,12,28,14,30},{1,17,3,19,5,21,7,23,9,25,..., dimensions={0} | all-to-all | bytes 262144 | tf_op jit(solution)/shard_map/all_to_all | solution.py:184
  41.1 0.6 %reduce_sum.9 = f32[16,128]{1,0:T(8,128)} reduce(f32[16,16,128]{2,1,0:T(8,128)S(1)} %all_to_all.10, f32[]{:T(128)} %constant.0.clone.1), dimensions={0}, to_apply=%region_0.0 | reduce | flops 30720 | bytes 139268 | tf_op jit(solution)/shard_map/reduce_sum | solution.py:237
Async XLA Ops:
  0.0 0.7 %copy-start.2 = (s32[1,128]{1,0:T(1,128)S(1)}, s32[1,128]{1,0:T(1,128)}, u32[]{:S(2)}) copy-start(s32[1,128]{1,0:T(1,128)} %send_ref.1) | copy-start | bytes 1540
  0.0 0.7 %copy-start.3 = (s32[16,1]{0,1:T(1,128)S(1)}, s32[16,1]{0,1:T(1,128)}, u32[]{:S(2)}) copy-start(s32[16,1]{0,1:T(1,128)} %param.9) | copy-start | bytes 196
  0.7 0.9 %copy-start = (bf16[16,1,4096]{2,0,1:T(8,128)(2,1)S(1)}, bf16[16,1,4096]{2,0,1:T(8,128)(2,1)}, u32[]{:S(2)}) copy-start(bf16[16,1,4096]{2,0,1:T(8,128)(2,1)} %param.8) | copy-start | bytes 393220
  1.6 15.8 %copy-start.4 = (bf16[16,7,4096]{2,0,1:T(8,128)(2,1)S(1)}, bf16[16,7,4096]{2,0,1:T(8,128)(2,1)}, u32[]{:S(2)}) copy-start(bf16[16,7,4096]{2,0,1:T(8,128)(2,1)} %param.5) | copy-start | bytes 2752516
  3.4 24.8 %all-to-all-start = ((bf16[16,136,128]{2,1,0:T(8,128)(2,1)}), bf16[16,136,128]{2,1,0:T(8,128)(2,1)S(1)}, u32[]{:S(2)}, u32[]{:S(2)}) async-start(bf16[16,136,128]{2,1,0:T(8,128)(2,1)} %get-tuple-element.18), calls=%async_computation | async-start | bytes 1114112 | tf_op jit(solution)/shard_map/all_to_all | solution.py:184
  11.7 15.6 %collective-permute-start = (bf16[136,128]{1,0:T(8,128)(2,1)S(1)}, bf16[136,128]{1,0:T(8,128)(2,1)S(1)}, u32[]{:S(2)}, u32[]{:S(2)}) collective-permute-start(bf16[136,128]{1,0:T(8,128)(2,1)S(1)} %get-tuple-element.19), channel_id=1, source_target_pairs={{0,2},{2,4},{4,6},{6,8},{8,10},{10,12},{12,14},{14,16},{16,18},{18... | collective-permute-start | bytes 104456 | tf_op jit(solution)/shard_map/ppermute | solution.py:189
  13.6 13.7 %collective-permute-start.1 = (bf16[136,128]{1,0:T(8,128)(2,1)S(1)}, bf16[136,128]{1,0:T(8,128)(2,1)S(1)}, u32[]{:S(2)}, u32[]{:S(2)}) collective-permute-start(bf16[136,128]{1,0:T(8,128)(2,1)S(1)} %get-tuple-element.20), channel_id=1, source_target_pairs={{0,30},{2,0},{4,2},{6,4},{8,6},{10,8},{12,10},{14,12},{16,14},{18,... | collective-permute-start | bytes 104456 | tf_op jit(solution)/shard_map/ppermute | solution.py:189
  17.4 2.1 %collective-permute-start.2 = (bf16[528,128]{1,0:T(8,128)(2,1)S(1)}, bf16[528,128]{1,0:T(8,128)(2,1)S(1)}, u32[]{:S(2)}, u32[]{:S(2)}) collective-permute-start(bf16[528,128]{1,0:T(8,128)(2,1)S(1)} %get-tuple-element.21.refs_0_.own_ref), channel_id=1, source_target_pairs={{0,1},{1,0},{2,3},{3,2},{4,5},{5,4},{6,7},{7,6},{8,9},{9,8},{10,11... | collective-permute-start | bytes 405512 | tf_op jit(solution)/shard_map/ppermute | solution.py:206
  19.5 8.7 %copy-start.1 = (s32[16,7]{0,1:T(8,128)S(1)}, s32[16,7]{0,1:T(8,128)}, u32[]{:S(2)}) copy-start(s32[16,7]{0,1:T(8,128)} %param.6) | copy-start | bytes 1348

commit v8 on v7

--- a/solution.py
+++ b/solution.py
@@ -16,6 +16,8 @@
 BF16 = jnp.bfloat16
 VMEM = pl.BlockSpec(memory_space=pltpu.VMEM)
 SMEM = pl.BlockSpec(memory_space=pltpu.SMEM)
+HBM = pl.BlockSpec(memory_space=pl.ANY)
+WHOLE = 60 * 2**20
 PARAMS = pltpu.CompilerParams(vmem_limit_bytes=40 * 2**20)
 
 
@@ -28,9 +30,8 @@
     return jnp.concatenate([x[:, B:], x[:, :B]], axis=1)
 
 
-def turn_rows(flat, index_of, scratch, out, base):
+def turn_rows(index_of, scratch, out, base):
     rows = scratch.shape[0]
-    unpack_rows(flat, scratch)
     for r in range(rows):
         x = scratch[r]
         x = jnp.where(index_of(r) == 0, x, swap_halves(x))
@@ -68,21 +69,36 @@
     return [i // 2 + i % 2 * (n // 2) for i in range(n)]
 
 
-def own_kernel(n, send_ref, index_ref, flat_ref, own_ref, out_ref, left_ref, right_ref, scratch):
+def own_kernel(n, send_hbm, index_hbm, flat_hbm, out_hbm, own_hbm, left_hbm, right_hbm, *refs):
+    send_ref, index_ref, flat_ref, scratch, own_ref, blocks, in_sems, out_sems = refs
     rows = flat_ref.shape[0]
     me = lax.axis_index("row")
-    turn_rows(flat_ref, lambda r: index_ref[0, r], scratch, own_ref, 0)
+    pairs = ((flat_hbm, flat_ref), (send_hbm, send_ref), (index_hbm, index_ref))
+    arriving = [pltpu.make_async_copy(x, y, in_sems.at[i]) for i, (x, y) in enumerate(pairs)]
+    for copy in arriving:
+        copy.start()
+    arriving[0].wait()
+    unpack_rows(flat_ref, scratch)
+    arriving[1].wait()
+    arriving[2].wait()
+    turn_rows(lambda r: index_ref[0, r], scratch, own_ref, 0)
     own_ref[rows * PACK :, :] = mask_table(lambda r: index_ref[0, r], rows).astype(BF16)
+    leaving = [pltpu.make_async_copy(own_ref, own_hbm, out_sems.at[n + 2])]
+    leaving[0].start()
 
     def look(slot):
         row = send_ref[0, slot]
         return row, index_ref[0, row]
 
-    for j, target in enumerate(alternating(n)):
-        fill(out_ref, (j,), own_ref, [look(target * S + s) for s in range(S2)], 8)
-    for ref, step in ((left_ref, n - 1), (right_ref, 1)):
-        first = lax.rem(me + step, n) * S
-        fill(ref, (), own_ref, [look(first + s) for s in range(S2, S)], 8)
+    targets = [(target * S, out_hbm.at[j]) for j, target in enumerate(alternating(n))]
+    targets.append((lax.rem(me + n - 1, n) * S + S2, left_hbm))
+    targets.append((lax.rem(me + 1, n) * S + S2, right_hbm))
+    for j, (first, out) in enumerate(targets):
+        fill(blocks, (j,), own_ref, [look(first + s) for s in range(S2)], 8)
+        leaving.append(pltpu.make_async_copy(blocks.at[j], out, out_sems.at[j]))
+        leaving[-1].start()
+    for copy in leaving:
+        copy.wait()
 
 
 def coupling_kernel(a_ref, coupling_ref, scratch):
@@ -191,14 +207,25 @@
     unpacked = pltpu.VMEM((rows, PACK, LANES), f32)
     edge = shape(S2 * PACK + 8, LANES)
     blocks = shape(n, S2 * PACK + 8, LANES)
-    own, out, left, right = call(
+    out, own, left, right = pl.pallas_call(
         functools.partial(own_kernel, n),
-        [shape(rows * PACK + rows, LANES), blocks, edge, edge],
-        [unpacked],
-        (send_rows, index, flat),
-        2,
-        "own",
-    )
+        out_shape=(blocks, shape(rows * PACK + rows, LANES), edge, edge),
+        in_specs=[HBM] * 3,
+        out_specs=(HBM,) * 4,
+        scratch_shapes=[
+            pltpu.SMEM(send_rows.shape, jnp.int32),
+            pltpu.SMEM(index.shape, jnp.int32),
+            pltpu.VMEM(flat.shape, BF16),
+            unpacked,
+            pltpu.VMEM((rows * PACK + rows, LANES), BF16),
+            pltpu.VMEM((n + 2, *edge.shape), BF16),
+            pltpu.SemaphoreType.DMA((3,)),
+            pltpu.SemaphoreType.DMA((n + 3,)),
+        ],
+        compiler_params=pltpu.CompilerParams(vmem_limit_bytes=WHOLE),
+        cost_estimate=pl.CostEstimate(flops=10**7, bytes_accessed=2**20, transcendentals=0),
+        name="own",
+    )(send_rows, index, flat)
     out, own, left, right, a_tiles = lax.optimization_barrier((out, own, left, right, a_tiles))
     ghosts = exchange(out)
     from_right, from_left = ring(left, n - 1), ring(right, 1)

time: 42 us -> 41.2 us (0.981)
  local copies, waits for them, and re-layouts: 1.58 us -> 0.02 us
  Pallas kernels: 6.02 us -> 6.64 us
    pallas_call x0 -> x1, Pallas kernels: none -> 2.39 us  [shards(): pl.pallas_call(functools.partial(own_kernel, n), out_shape=(blocks, shape...]
    pallas_call x4 -> x3, Pallas kernels: 6.02 us -> 4.25 us  [call(): pl.pallas_call(body, out_shape=out_shape, in_specs=[SMEM] * smem + [VMEM]...]
    unnamed x10, local copies, waits for them, and re-layouts: 1.58 us -> 0.02 us
where the time goes in v8:
time: 41.2 us; the launch traced here: 40.9 us
  starting transfers between devices  14.1 us (34%)
  blocking collectives  11 us (27%)
  waiting for transfers between devices  8.4 us (20%)
  Pallas kernels  6.64 us (16%)
  other arithmetic  0.62 us (2%)
    all_to_all x1, blocking collectives, exchange(): lax.all_to_all(x, 'row', split_axis=0, concat_axis=0, tiled=True, axis_in...  11 us
    all_to_all x1, starting transfers between devices, exchange(): lax.all_to_all(x, 'row', split_axis=0, concat_axis=0, tiled=True, axis_in...  8.46 us
    ppermute x2, waiting for transfers between devices, ring(): return lax.ppermute(x, 'row', [(i, (i + step) % n) for i in range(n)])  7.5 us
    ppermute x2, starting transfers between devices, ring(): return lax.ppermute(x, 'row', [(i, (i + step) % n) for i in range(n)])  5.67 us
    pallas_call x3, Pallas kernels, call(): pl.pallas_call(body, out_shape=out_shape, in_specs=[SMEM] * smem + [VMEM]...  4.25 us
    pallas_call x1, Pallas kernels, shards(): pl.pallas_call(functools.partial(own_kernel, n), out_shape=(blocks, shape...  2.39 us
    all_to_all x1, waiting for transfers between devices, exchange(): lax.all_to_all(x, 'row', split_axis=0, concat_axis=0, tiled=True, axis_in...  0.9 us
  transfers between devices with their start and end apart: 4, of which 2 were waited for; matrix products, arithmetic and copies ran while one was open for 0% of the time, Pallas kernels for 6%

profile of v8, /device:TPU:0, one launch (start us, length us, event | category | flops | bytes accessed | tf_op | source)
XLA Modules:
  0.0 40.9 jit_solution(8855726952214253111)
XLA Ops:
  0.0 0.0 copy-start.2
  0.0 2.4 %own.1 = (bf16[16,136,128]{2,1,0:T(8,128)(2,1)}, bf16[528,128]{1,0:T(8,128)(2,1)}, bf16[136,128]{1,0:T(8,128)(2,1)}, bf16[136,128]{1,0:T(8,128)(2,1)}) custom-call(s32[1,128]{1,0:T(1,128)} %send_hbm.1, s32[1,16]{1,0:T(1,128)} %bitcast.9, bf16[16,4096]{1,0:T(8,128)(2,1)} %bitcast.8), custom_call_target="tpu_custom_call" | custom-call | flops 10000000 | bytes 1048576 | tf_op jit(solution)/shard_map/own/pallas_call | solution.py:210
  2.4 0.0 copy-start.4
  2.4 0.0 copy-start.3
  2.4 0.0 copy-start
  2.4 8.5 %all-to-all-start = ((bf16[16,136,128]{2,1,0:T(8,128)(2,1)}), bf16[16,136,128]{2,1,0:T(8,128)(2,1)S(1)}, u32[]{:S(2)}, u32[]{:S(2)}) async-start(bf16[16,136,128]{2,1,0:T(8,128)(2,1)} %get-tuple-element.18), calls=%async_computation | async-start | bytes 1114112 | tf_op jit(solution)/shard_map/all_to_all | solution.py:200
  10.9 0.0 copy-done.4
  10.9 2.0 %collective-permute-start = (bf16[136,128]{1,0:T(8,128)(2,1)S(1)}, bf16[136,128]{1,0:T(8,128)(2,1)S(1)}, u32[]{:S(2)}, u32[]{:S(2)}) collective-permute-start(bf16[136,128]{1,0:T(8,128)(2,1)S(1)} %copy-done.4), channel_id=1, source_target_pairs={{0,2},{2,4},{4,6},{6,8},{8,10},{10,12},{12,14},{14,16},{16,18},{18... | collective-permute-start | bytes 104456 | tf_op jit(solution)/shard_map/ppermute | solution.py:205
  12.9 0.0 copy-done.3
  12.9 3.7 %collective-permute-start.1 = (bf16[136,128]{1,0:T(8,128)(2,1)S(1)}, bf16[136,128]{1,0:T(8,128)(2,1)S(1)}, u32[]{:S(2)}, u32[]{:S(2)}) collective-permute-start(bf16[136,128]{1,0:T(8,128)(2,1)S(1)} %copy-done.3), channel_id=1, source_target_pairs={{0,30},{2,0},{4,2},{6,4},{8,6},{10,8},{12,10},{14,12},{16,14},{18,... | collective-permute-start | bytes 104456 | tf_op jit(solution)/shard_map/ppermute | solution.py:205
  16.6 0.0 copy-done
  16.6 0.0 collective-permute-start.2
  16.6 0.0 copy-done.2
  16.6 2.1 %coupling.1.coupling_ref = bf16[16,64,512]{2,1,0:T(8,128)(2,1)S(1)} custom-call(bf16[7,16,4096]{2,1,0:T(8,128)(2,1)S(1)} %bitcast.7), custom_call_target="tpu_custom_call" | custom-call | flops 2000000000 | bytes 1048576 | tf_op jit(solution)/shard_map/coupling/pallas_call | solution.py:185
  18.7 0.0 collective-permute-done.2.refs_1_
  18.7 0.0 copy-start.1
  18.7 0.3 restrict.1.restrict_ref
  19.0 7.5 %collective-permute-done.left_ref = bf16[136,128]{1,0:T(8,128)(2,1)S(1)} collective-permute-done((bf16[136,128]{1,0:T(8,128)(2,1)S(1)}, bf16[136,128]{1,0:T(8,128)(2,1)S(1)}, u32[]{:S(2)}, u32[]{:S(2)}) %collective-permute-start) | collective-permute-done | bytes 34848 | tf_op jit(solution)/shard_map/ppermute | solution.py:205
  26.5 0.0 collective-permute-done.1.right_ref
  26.5 0.9 %all-to-all-done.ghost_ref = bf16[16,136,128]{2,1,0:T(8,128)(2,1)S(1)} async-done(((bf16[16,136,128]{2,1,0:T(8,128)(2,1)}), bf16[16,136,128]{2,1,0:T(8,128)(2,1)S(1)}, u32[]{:S(2)}, u32[]{:S(2)}) %all-to-all-start) | async-done | bytes 557088 | tf_op jit(solution)/shard_map/all_to_all | solution.py:200
  27.4 0.0 copy-done.1
  27.4 1.8 %product.1 = f32[256,128]{1,0:T(8,128)S(1)} custom-call(s32[7,16]{1,0:T(8,128)S(1)} %bitcast.6, bf16[16,136,128]{2,1,0:T(8,128)(2,1)S(1)} %all-to-all-done.ghost_ref, bf16[136,128]{1,0:T(8,128)(2,1)S(1)} %collective-permute-done.left_ref, bf16[136,128]{1,0:T(8,128)(2,1)S(1)} %collective-permute-done.1.right_ref, bf16[528,128]{1,0:T(8,128)(2,1)S(1)} %copy-done, ...), custom_call_target="tpu_custom_call" | custom-call | flops 200000000 | bytes 1048576 | tf_op jit(solution)/shard_map/product/pallas_call | solution.py:185
  29.3 11.0 %all_to_all.10 = f32[16,16,128]{2,1,0:T(8,128)S(1)} all-to-all(f32[16,16,128]{2,1,0:T(8,128)S(1)} %bitcast.5), channel_id=1, replica_groups={{0,16,2,18,4,20,6,22,8,24,10,26,12,28,14,30},{1,17,3,19,5,21,7,23,9,25,..., dimensions={0} | all-to-all | bytes 262144 | tf_op jit(solution)/shard_map/all_to_all | solution.py:200
  40.3 0.6 %reduce_sum.9 = f32[16,128]{1,0:T(8,128)} reduce(f32[16,16,128]{2,1,0:T(8,128)S(1)} %all_to_all.10, f32[]{:T(128)} %constant.0.clone.1), dimensions={0}, to_apply=%region_0.0 | reduce | flops 30720 | bytes 139268 | tf_op jit(solution)/shard_map/reduce_sum | solution.py:264
Async XLA Ops:
  0.0 16.6 %copy-start.2 = (bf16[16,7,4096]{2,0,1:T(8,128)(2,1)S(1)}, bf16[16,7,4096]{2,0,1:T(8,128)(2,1)}, u32[]{:S(2)}) copy-start(bf16[16,7,4096]{2,0,1:T(8,128)(2,1)} %param.5) | copy-start | bytes 2752516
  2.4 8.5 %copy-start.4 = (bf16[136,128]{1,0:T(8,128)(2,1)S(1)}, bf16[136,128]{1,0:T(8,128)(2,1)}, u32[]{:S(2)}) copy-start(bf16[136,128]{1,0:T(8,128)(2,1)} %get-tuple-element.19) | copy-start | bytes 104452
  2.4 10.5 %copy-start.3 = (bf16[136,128]{1,0:T(8,128)(2,1)S(1)}, bf16[136,128]{1,0:T(8,128)(2,1)}, u32[]{:S(2)}) copy-start(bf16[136,128]{1,0:T(8,128)(2,1)} %get-tuple-element.20) | copy-start | bytes 104452
  2.4 14.2 %copy-start = (bf16[528,128]{1,0:T(8,128)(2,1)S(1)}, bf16[528,128]{1,0:T(8,128)(2,1)}, u32[]{:S(2)}) copy-start(bf16[528,128]{1,0:T(8,128)(2,1)} %get-tuple-element.21.refs_0_.own_ref) | copy-start | bytes 405508
  2.4 25.0 %all-to-all-start = ((bf16[16,136,128]{2,1,0:T(8,128)(2,1)}), bf16[16,136,128]{2,1,0:T(8,128)(2,1)S(1)}, u32[]{:S(2)}, u32[]{:S(2)}) async-start(bf16[16,136,128]{2,1,0:T(8,128)(2,1)} %get-tuple-element.18), calls=%async_computation | async-start | bytes 1114112 | tf_op jit(solution)/shard_map/all_to_all | solution.py:200
  10.9 15.6 %collective-permute-start = (bf16[136,128]{1,0:T(8,128)(2,1)S(1)}, bf16[136,128]{1,0:T(8,128)(2,1)S(1)}, u32[]{:S(2)}, u32[]{:S(2)}) collective-permute-start(bf16[136,128]{1,0:T(8,128)(2,1)S(1)} %copy-done.4), channel_id=1, source_target_pairs={{0,2},{2,4},{4,6},{6,8},{8,10},{10,12},{12,14},{14,16},{16,18},{18... | collective-permute-start | bytes 104456 | tf_op jit(solution)/shard_map/ppermute | solution.py:205
  12.9 13.6 %collective-permute-start.1 = (bf16[136,128]{1,0:T(8,128)(2,1)S(1)}, bf16[136,128]{1,0:T(8,128)(2,1)S(1)}, u32[]{:S(2)}, u32[]{:S(2)}) collective-permute-start(bf16[136,128]{1,0:T(8,128)(2,1)S(1)} %copy-done.3), channel_id=1, source_target_pairs={{0,30},{2,0},{4,2},{6,4},{8,6},{10,8},{12,10},{14,12},{16,14},{18,... | collective-permute-start | bytes 104456 | tf_op jit(solution)/shard_map/ppermute | solution.py:205
  16.6 2.1 %collective-permute-start.2 = (bf16[528,128]{1,0:T(8,128)(2,1)S(1)}, bf16[528,128]{1,0:T(8,128)(2,1)S(1)}, u32[]{:S(2)}, u32[]{:S(2)}) collective-permute-start(bf16[528,128]{1,0:T(8,128)(2,1)S(1)} %copy-done), channel_id=1, source_target_pairs={{0,1},{1,0},{2,3},{3,2},{4,5},{5,4},{6,7},{7,6},{8,9},{9,8},{10,11... | collective-permute-start | bytes 405512 | tf_op jit(solution)/shard_map/ppermute | solution.py:233
  18.7 8.7 %copy-start.1 = (s32[16,7]{0,1:T(8,128)S(1)}, s32[16,7]{0,1:T(8,128)}, u32[]{:S(2)}) copy-start(s32[16,7]{0,1:T(8,128)} %param.6) | copy-start | bytes 1348

commit v9 on v8

--- a/solution.py
+++ b/solution.py
@@ -66,7 +66,7 @@
 
 
 def alternating(n):
-    return [i // 2 + i % 2 * (n // 2) for i in range(n)]
+    return [i // 4 + i % 2 * (n // 2) + i // 2 % 2 * (n // 4) for i in range(n)]
 
 
 def own_kernel(n, send_hbm, index_hbm, flat_hbm, out_hbm, own_hbm, left_hbm, right_hbm, *refs):

time: 41.2 us -> 41.2 us (level)
  blocking collectives: 11 us -> 12 us
  waiting for transfers between devices: 8.4 us -> 7.44 us
    all_to_all x1, blocking collectives: 11 us -> 12 us  [exchange(): lax.all_to_all(x, 'row', split_axis=0, concat_axis=0, tiled=True, axis_in...]
    all_to_all x1, waiting for transfers between devices: 0.9 us -> 0.01 us  [exchange(): lax.all_to_all(x, 'row', split_axis=0, concat_axis=0, tiled=True, axis_in...]
  transfers between devices with their start and end apart: 4 -> 4, of which waited for: 2 -> 1; matrix products, arithmetic and copies ran while one was open for 0% -> 0% of each run, Pallas kernels for 6% -> 6%
where the time goes in v9:
time: 41.2 us; the launch traced here: 40.9 us
  starting transfers between devices  14.1 us (34%)
  blocking collectives  12 us (29%)
  waiting for transfers between devices  7.44 us (18%)
  Pallas kernels  6.64 us (16%)
  other arithmetic  0.62 us (2%)
    all_to_all x1, blocking collectives, exchange(): lax.all_to_all(x, 'row', split_axis=0, concat_axis=0, tiled=True, axis_in...  12 us
    all_to_all x1, starting transfers between devices, exchange(): lax.all_to_all(x, 'row', split_axis=0, concat_axis=0, tiled=True, axis_in...  8.46 us
    ppermute x2, waiting for transfers between devices, ring(): return lax.ppermute(x, 'row', [(i, (i + step) % n) for i in range(n)])  7.44 us
    ppermute x2, starting transfers between devices, ring(): return lax.ppermute(x, 'row', [(i, (i + step) % n) for i in range(n)])  5.67 us
    pallas_call x3, Pallas kernels, call(): pl.pallas_call(body, out_shape=out_shape, in_specs=[SMEM] * smem + [VMEM]...  4.25 us
    pallas_call x1, Pallas kernels, shards(): pl.pallas_call(functools.partial(own_kernel, n), out_shape=(blocks, shape...  2.39 us
  transfers between devices with their start and end apart: 4, of which 1 were waited for; matrix products, arithmetic and copies ran while one was open for 0% of the time, Pallas kernels for 6%

profile of v9, /device:TPU:0, one launch (start us, length us, event | category | flops | bytes accessed | tf_op | source)
XLA Modules:
  0.0 40.9 jit_solution(7447435952423621751)
XLA Ops:
  0.0 0.0 copy-start.2
  0.0 2.4 %own.1 = (bf16[16,136,128]{2,1,0:T(8,128)(2,1)}, bf16[528,128]{1,0:T(8,128)(2,1)}, bf16[136,128]{1,0:T(8,128)(2,1)}, bf16[136,128]{1,0:T(8,128)(2,1)}) custom-call(s32[1,128]{1,0:T(1,128)} %send_hbm.1, s32[1,16]{1,0:T(1,128)} %bitcast.9, bf16[16,4096]{1,0:T(8,128)(2,1)} %bitcast.8), custom_call_target="tpu_custom_call" | custom-call | flops 10000000 | bytes 1048576 | tf_op jit(solution)/shard_map/own/pallas_call | solution.py:210
  2.4 0.0 copy-start.4
  2.4 0.0 copy-start.3
  2.4 0.0 copy-start
  2.4 8.5 %all-to-all-start = ((bf16[16,136,128]{2,1,0:T(8,128)(2,1)}), bf16[16,136,128]{2,1,0:T(8,128)(2,1)S(1)}, u32[]{:S(2)}, u32[]{:S(2)}) async-start(bf16[16,136,128]{2,1,0:T(8,128)(2,1)} %get-tuple-element.18), calls=%async_computation | async-start | bytes 1114112 | tf_op jit(solution)/shard_map/all_to_all | solution.py:200
  10.9 0.0 copy-done.4
  10.9 2.0 %collective-permute-start = (bf16[136,128]{1,0:T(8,128)(2,1)S(1)}, bf16[136,128]{1,0:T(8,128)(2,1)S(1)}, u32[]{:S(2)}, u32[]{:S(2)}) collective-permute-start(bf16[136,128]{1,0:T(8,128)(2,1)S(1)} %copy-done.4), channel_id=1, source_target_pairs={{0,2},{2,4},{4,6},{6,8},{8,10},{10,12},{12,14},{14,16},{16,18},{18... | collective-permute-start | bytes 104456 | tf_op jit(solution)/shard_map/ppermute | solution.py:205
  12.9 0.0 copy-done.3
  12.9 3.7 %collective-permute-start.1 = (bf16[136,128]{1,0:T(8,128)(2,1)S(1)}, bf16[136,128]{1,0:T(8,128)(2,1)S(1)}, u32[]{:S(2)}, u32[]{:S(2)}) collective-permute-start(bf16[136,128]{1,0:T(8,128)(2,1)S(1)} %copy-done.3), channel_id=1, source_target_pairs={{0,30},{2,0},{4,2},{6,4},{8,6},{10,8},{12,10},{14,12},{16,14},{18,... | collective-permute-start | bytes 104456 | tf_op jit(solution)/shard_map/ppermute | solution.py:205
  16.6 0.0 copy-done
  16.6 0.0 collective-permute-start.2
  16.6 0.0 copy-done.2
  16.6 2.1 %coupling.1.coupling_ref = bf16[16,64,512]{2,1,0:T(8,128)(2,1)S(1)} custom-call(bf16[7,16,4096]{2,1,0:T(8,128)(2,1)S(1)} %bitcast.7), custom_call_target="tpu_custom_call" | custom-call | flops 2000000000 | bytes 1048576 | tf_op jit(solution)/shard_map/coupling/pallas_call | solution.py:185
  18.7 0.0 collective-permute-done.2.refs_1_
  18.7 0.0 copy-start.1
  18.7 0.3 restrict.1.restrict_ref
  19.0 7.4 %collective-permute-done.left_ref = bf16[136,128]{1,0:T(8,128)(2,1)S(1)} collective-permute-done((bf16[136,128]{1,0:T(8,128)(2,1)S(1)}, bf16[136,128]{1,0:T(8,128)(2,1)S(1)}, u32[]{:S(2)}, u32[]{:S(2)}) %collective-permute-start) | collective-permute-done | bytes 34848 | tf_op jit(solution)/shard_map/ppermute | solution.py:205
  26.5 0.0 collective-permute-done.1.right_ref
  26.5 0.0 all-to-all-done.ghost_ref
  26.5 0.0 copy-done.1
  26.5 1.8 %product.1 = f32[256,128]{1,0:T(8,128)S(1)} custom-call(s32[7,16]{1,0:T(8,128)S(1)} %bitcast.6, bf16[16,136,128]{2,1,0:T(8,128)(2,1)S(1)} %all-to-all-done.ghost_ref, bf16[136,128]{1,0:T(8,128)(2,1)S(1)} %collective-permute-done.left_ref, bf16[136,128]{1,0:T(8,128)(2,1)S(1)} %collective-permute-done.1.right_ref, bf16[528,128]{1,0:T(8,128)(2,1)S(1)} %copy-done, ...), custom_call_target="tpu_custom_call" | custom-call | flops 200000000 | bytes 1048576 | tf_op jit(solution)/shard_map/product/pallas_call | solution.py:185
  28.3 12.0 %all_to_all.10 = f32[16,16,128]{2,1,0:T(8,128)S(1)} all-to-all(f32[16,16,128]{2,1,0:T(8,128)S(1)} %bitcast.5), channel_id=1, replica_groups={{0,16,8,24,2,18,10,26,4,20,12,28,6,22,14,30},{1,17,9,25,3,19,11,27,5,21..., dimensions={0} | all-to-all | bytes 262144 | tf_op jit(solution)/shard_map/all_to_all | solution.py:200
  40.3 0.6 %reduce_sum.9 = f32[16,128]{1,0:T(8,128)} reduce(f32[16,16,128]{2,1,0:T(8,128)S(1)} %all_to_all.10, f32[]{:T(128)} %constant.0.clone.1), dimensions={0}, to_apply=%region_0.0 | reduce | flops 30720 | bytes 139268 | tf_op jit(solution)/shard_map/reduce_sum | solution.py:264
Async XLA Ops:
  0.0 16.6 %copy-start.2 = (bf16[16,7,4096]{2,0,1:T(8,128)(2,1)S(1)}, bf16[16,7,4096]{2,0,1:T(8,128)(2,1)}, u32[]{:S(2)}) copy-start(bf16[16,7,4096]{2,0,1:T(8,128)(2,1)} %param.5) | copy-start | bytes 2752516
  2.4 8.5 %copy-start.4 = (bf16[136,128]{1,0:T(8,128)(2,1)S(1)}, bf16[136,128]{1,0:T(8,128)(2,1)}, u32[]{:S(2)}) copy-start(bf16[136,128]{1,0:T(8,128)(2,1)} %get-tuple-element.19) | copy-start | bytes 104452
  2.4 10.5 %copy-start.3 = (bf16[136,128]{1,0:T(8,128)(2,1)S(1)}, bf16[136,128]{1,0:T(8,128)(2,1)}, u32[]{:S(2)}) copy-start(bf16[136,128]{1,0:T(8,128)(2,1)} %get-tuple-element.20) | copy-start | bytes 104452
  2.4 14.2 %copy-start = (bf16[528,128]{1,0:T(8,128)(2,1)S(1)}, bf16[528,128]{1,0:T(8,128)(2,1)}, u32[]{:S(2)}) copy-start(bf16[528,128]{1,0:T(8,128)(2,1)} %get-tuple-element.21.refs_0_.own_ref) | copy-start | bytes 405508
  2.4 24.0 %all-to-all-start = ((bf16[16,136,128]{2,1,0:T(8,128)(2,1)}), bf16[16,136,128]{2,1,0:T(8,128)(2,1)S(1)}, u32[]{:S(2)}, u32[]{:S(2)}) async-start(bf16[16,136,128]{2,1,0:T(8,128)(2,1)} %get-tuple-element.18), calls=%async_computation | async-start | bytes 1114112 | tf_op jit(solution)/shard_map/all_to_all | solution.py:200
  10.9 15.5 %collective-permute-start = (bf16[136,128]{1,0:T(8,128)(2,1)S(1)}, bf16[136,128]{1,0:T(8,128)(2,1)S(1)}, u32[]{:S(2)}, u32[]{:S(2)}) collective-permute-start(bf16[136,128]{1,0:T(8,128)(2,1)S(1)} %copy-done.4), channel_id=1, source_target_pairs={{0,2},{2,4},{4,6},{6,8},{8,10},{10,12},{12,14},{14,16},{16,18},{18... | collective-permute-start | bytes 104456 | tf_op jit(solution)/shard_map/ppermute | solution.py:205
  12.9 13.6 %collective-permute-start.1 = (bf16[136,128]{1,0:T(8,128)(2,1)S(1)}, bf16[136,128]{1,0:T(8,128)(2,1)S(1)}, u32[]{:S(2)}, u32[]{:S(2)}) collective-permute-start(bf16[136,128]{1,0:T(8,128)(2,1)S(1)} %copy-done.3), channel_id=1, source_target_pairs={{0,30},{2,0},{4,2},{6,4},{8,6},{10,8},{12,10},{14,12},{16,14},{18,... | collective-permute-start | bytes 104456 | tf_op jit(solution)/shard_map/ppermute | solution.py:205
  16.6 2.1 %collective-permute-start.2 = (bf16[528,128]{1,0:T(8,128)(2,1)S(1)}, bf16[528,128]{1,0:T(8,128)(2,1)S(1)}, u32[]{:S(2)}, u32[]{:S(2)}) collective-permute-start(bf16[528,128]{1,0:T(8,128)(2,1)S(1)} %copy-done), channel_id=1, source_target_pairs={{0,1},{1,0},{2,3},{3,2},{4,5},{5,4},{6,7},{7,6},{8,9},{9,8},{10,11... | collective-permute-start | bytes 405512 | tf_op jit(solution)/shard_map/ppermute | solution.py:233
  18.7 7.8 %copy-start.1 = (s32[16,7]{0,1:T(8,128)S(1)}, s32[16,7]{0,1:T(8,128)}, u32[]{:S(2)}) copy-start(s32[16,7]{0,1:T(8,128)} %param.6) | copy-start | bytes 1348

commit v10 on v9

--- a/solution.py
+++ b/solution.py
@@ -160,15 +160,22 @@
     for ref, step in ((left_ref, n - 1), (right_ref, 1)):
         place_slots(lax.rem(me + step, n) * S + S2, ref, ())
 
-    def row_body(r, carry):
-        picked = jnp.concatenate(
-            [wide[pl.ds(pl.multiple_of(code_ref[k, r] * B, B), B), :] for k in range(span)], axis=0
-        )
-        block = jnp.dot(coupling_ref[r, :, : span * B], picked, preferred_element_type=jnp.float32)
-        ap[pl.ds(pl.multiple_of(r * B, B), B), :] = block.astype(BF16)
+    def pair_body(i, carry):
+        pair = (2 * i, 2 * i + 1)
+        picked = [
+            jnp.concatenate(
+                [wide[pl.ds(pl.multiple_of(code_ref[k, r] * B, B), B), :] for k in range(span)], axis=0
+            )
+            for r in pair
+        ]
+        both = coupling_ref[pl.ds(2 * i, 2), :, : span * B].reshape(2 * B, span * B)
+        block = jnp.dot(both, jnp.concatenate(picked, axis=1), preferred_element_type=jnp.float32)
+        for h, r in enumerate(pair):
+            own = block[h * B : (h + 1) * B, h * LANES : (h + 1) * LANES]
+            ap[pl.ds(pl.multiple_of(r * B, B), B), :] = own.astype(BF16)
         return carry
 
-    lax.fori_loop(0, rows, row_body, 0, unroll=8)
+    lax.fori_loop(0, rows // 2, pair_body, 0, unroll=8)
     coarse = jnp.dot(restrict_ref[...], ap[...], preferred_element_type=jnp.float32)
     share = out_ref.shape[0] // n
     for j, target in enumerate(alternating(n)):

time: 41.2 us -> 40.9 us (level)
  no operation moved by 1% of the time
where the time goes in v10:
time: 40.9 us; the launch traced here: 40.7 us
  starting transfers between devices  14.1 us (34%)
  blocking collectives  12 us (29%)
  waiting for transfers between devices  7.44 us (18%)
  Pallas kernels  6.4 us (16%)
  other arithmetic  0.62 us (2%)
    all_to_all x1, blocking collectives, exchange(): lax.all_to_all(x, 'row', split_axis=0, concat_axis=0, tiled=True, axis_in...  12 us
    all_to_all x1, starting transfers between devices, exchange(): lax.all_to_all(x, 'row', split_axis=0, concat_axis=0, tiled=True, axis_in...  8.46 us
    ppermute x2, waiting for transfers between devices, ring(): return lax.ppermute(x, 'row', [(i, (i + step) % n) for i in range(n)])  7.44 us
    ppermute x2, starting transfers between devices, ring(): return lax.ppermute(x, 'row', [(i, (i + step) % n) for i in range(n)])  5.67 us
    pallas_call x3, Pallas kernels, call(): pl.pallas_call(body, out_shape=out_shape, in_specs=[SMEM] * smem + [VMEM]...  4 us
    pallas_call x1, Pallas kernels, shards(): pl.pallas_call(functools.partial(own_kernel, n), out_shape=(blocks, shape...  2.39 us
  transfers between devices with their start and end apart: 4, of which 1 were waited for; matrix products, arithmetic and copies ran while one was open for 0% of the time, Pallas kernels for 6%

profile of v10, /device:TPU:0, one launch (start us, length us, event | category | flops | bytes accessed | tf_op | source)
XLA Modules:
  0.0 40.7 jit_solution(7841607097581386347)
XLA Ops:
  0.0 0.0 copy-start.2
  0.0 2.4 %own.1 = (bf16[16,136,128]{2,1,0:T(8,128)(2,1)}, bf16[528,128]{1,0:T(8,128)(2,1)}, bf16[136,128]{1,0:T(8,128)(2,1)}, bf16[136,128]{1,0:T(8,128)(2,1)}) custom-call(s32[1,128]{1,0:T(1,128)} %send_hbm.1, s32[1,16]{1,0:T(1,128)} %bitcast.9, bf16[16,4096]{1,0:T(8,128)(2,1)} %bitcast.8), custom_call_target="tpu_custom_call" | custom-call | flops 10000000 | bytes 1048576 | tf_op jit(solution)/shard_map/own/pallas_call | solution.py:217
  2.4 0.0 copy-start.4
  2.4 0.0 copy-start.3
  2.4 0.0 copy-start
  2.4 8.5 %all-to-all-start = ((bf16[16,136,128]{2,1,0:T(8,128)(2,1)}), bf16[16,136,128]{2,1,0:T(8,128)(2,1)S(1)}, u32[]{:S(2)}, u32[]{:S(2)}) async-start(bf16[16,136,128]{2,1,0:T(8,128)(2,1)} %get-tuple-element.18), calls=%async_computation | async-start | bytes 1114112 | tf_op jit(solution)/shard_map/all_to_all | solution.py:207
  10.9 0.0 copy-done.4
  10.9 2.0 %collective-permute-start = (bf16[136,128]{1,0:T(8,128)(2,1)S(1)}, bf16[136,128]{1,0:T(8,128)(2,1)S(1)}, u32[]{:S(2)}, u32[]{:S(2)}) collective-permute-start(bf16[136,128]{1,0:T(8,128)(2,1)S(1)} %copy-done.4), channel_id=1, source_target_pairs={{0,2},{2,4},{4,6},{6,8},{8,10},{10,12},{12,14},{14,16},{16,18},{18... | collective-permute-start | bytes 104456 | tf_op jit(solution)/shard_map/ppermute | solution.py:212
  12.9 0.0 copy-done.3
  12.9 3.7 %collective-permute-start.1 = (bf16[136,128]{1,0:T(8,128)(2,1)S(1)}, bf16[136,128]{1,0:T(8,128)(2,1)S(1)}, u32[]{:S(2)}, u32[]{:S(2)}) collective-permute-start(bf16[136,128]{1,0:T(8,128)(2,1)S(1)} %copy-done.3), channel_id=1, source_target_pairs={{0,30},{2,0},{4,2},{6,4},{8,6},{10,8},{12,10},{14,12},{16,14},{18,... | collective-permute-start | bytes 104456 | tf_op jit(solution)/shard_map/ppermute | solution.py:212
  16.6 0.0 copy-done
  16.6 0.0 collective-permute-start.2
  16.6 0.0 copy-done.2
  16.6 2.1 %coupling.1.coupling_ref = bf16[16,64,512]{2,1,0:T(8,128)(2,1)S(1)} custom-call(bf16[7,16,4096]{2,1,0:T(8,128)(2,1)S(1)} %bitcast.7), custom_call_target="tpu_custom_call" | custom-call | flops 2000000000 | bytes 1048576 | tf_op jit(solution)/shard_map/coupling/pallas_call | solution.py:192
  18.7 0.0 collective-permute-done.2.refs_1_
  18.7 0.0 copy-start.1
  18.7 0.3 restrict.1.restrict_ref
  19.0 7.4 %collective-permute-done.left_ref = bf16[136,128]{1,0:T(8,128)(2,1)S(1)} collective-permute-done((bf16[136,128]{1,0:T(8,128)(2,1)S(1)}, bf16[136,128]{1,0:T(8,128)(2,1)S(1)}, u32[]{:S(2)}, u32[]{:S(2)}) %collective-permute-start) | collective-permute-done | bytes 34848 | tf_op jit(solution)/shard_map/ppermute | solution.py:212
  26.5 0.0 collective-permute-done.1.right_ref
  26.5 0.0 all-to-all-done.ghost_ref
  26.5 0.0 copy-done.1
  26.5 1.6 %product.1 = f32[256,128]{1,0:T(8,128)S(1)} custom-call(s32[7,16]{1,0:T(8,128)S(1)} %bitcast.6, bf16[16,136,128]{2,1,0:T(8,128)(2,1)S(1)} %all-to-all-done.ghost_ref, bf16[136,128]{1,0:T(8,128)(2,1)S(1)} %collective-permute-done.left_ref, bf16[136,128]{1,0:T(8,128)(2,1)S(1)} %collective-permute-done.1.right_ref, bf16[528,128]{1,0:T(8,128)(2,1)S(1)} %copy-done, ...), custom_call_target="tpu_custom_call" | custom-call | flops 200000000 | bytes 1048576 | tf_op jit(solution)/shard_map/product/pallas_call | solution.py:192
  28.1 12.0 %all_to_all.10 = f32[16,16,128]{2,1,0:T(8,128)S(1)} all-to-all(f32[16,16,128]{2,1,0:T(8,128)S(1)} %bitcast.5), channel_id=1, replica_groups={{0,16,8,24,2,18,10,26,4,20,12,28,6,22,14,30},{1,17,9,25,3,19,11,27,5,21..., dimensions={0} | all-to-all | bytes 262144 | tf_op jit(solution)/shard_map/all_to_all | solution.py:207
  40.0 0.6 %reduce_sum.9 = f32[16,128]{1,0:T(8,128)} reduce(f32[16,16,128]{2,1,0:T(8,128)S(1)} %all_to_all.10, f32[]{:T(128)} %constant.0.clone.1), dimensions={0}, to_apply=%region_0.0 | reduce | flops 30720 | bytes 139268 | tf_op jit(solution)/shard_map/reduce_sum | solution.py:271
Async XLA Ops:
  0.0 16.6 %copy-start.2 = (bf16[16,7,4096]{2,0,1:T(8,128)(2,1)S(1)}, bf16[16,7,4096]{2,0,1:T(8,128)(2,1)}, u32[]{:S(2)}) copy-start(bf16[16,7,4096]{2,0,1:T(8,128)(2,1)} %param.5) | copy-start | bytes 2752516
  2.4 8.5 %copy-start.4 = (bf16[136,128]{1,0:T(8,128)(2,1)S(1)}, bf16[136,128]{1,0:T(8,128)(2,1)}, u32[]{:S(2)}) copy-start(bf16[136,128]{1,0:T(8,128)(2,1)} %get-tuple-element.19) | copy-start | bytes 104452
  2.4 10.5 %copy-start.3 = (bf16[136,128]{1,0:T(8,128)(2,1)S(1)}, bf16[136,128]{1,0:T(8,128)(2,1)}, u32[]{:S(2)}) copy-start(bf16[136,128]{1,0:T(8,128)(2,1)} %get-tuple-element.20) | copy-start | bytes 104452
  2.4 14.2 %copy-start = (bf16[528,128]{1,0:T(8,128)(2,1)S(1)}, bf16[528,128]{1,0:T(8,128)(2,1)}, u32[]{:S(2)}) copy-start(bf16[528,128]{1,0:T(8,128)(2,1)} %get-tuple-element.21.refs_0_.own_ref) | copy-start | bytes 405508
  2.4 24.0 %all-to-all-start = ((bf16[16,136,128]{2,1,0:T(8,128)(2,1)}), bf16[16,136,128]{2,1,0:T(8,128)(2,1)S(1)}, u32[]{:S(2)}, u32[]{:S(2)}) async-start(bf16[16,136,128]{2,1,0:T(8,128)(2,1)} %get-tuple-element.18), calls=%async_computation | async-start | bytes 1114112 | tf_op jit(solution)/shard_map/all_to_all | solution.py:207
  10.9 15.5 %collective-permute-start = (bf16[136,128]{1,0:T(8,128)(2,1)S(1)}, bf16[136,128]{1,0:T(8,128)(2,1)S(1)}, u32[]{:S(2)}, u32[]{:S(2)}) collective-permute-start(bf16[136,128]{1,0:T(8,128)(2,1)S(1)} %copy-done.4), channel_id=1, source_target_pairs={{0,2},{2,4},{4,6},{6,8},{8,10},{10,12},{12,14},{14,16},{16,18},{18... | collective-permute-start | bytes 104456 | tf_op jit(solution)/shard_map/ppermute | solution.py:212
  12.9 13.6 %collective-permute-start.1 = (bf16[136,128]{1,0:T(8,128)(2,1)S(1)}, bf16[136,128]{1,0:T(8,128)(2,1)S(1)}, u32[]{:S(2)}, u32[]{:S(2)}) collective-permute-start(bf16[136,128]{1,0:T(8,128)(2,1)S(1)} %copy-done.3), channel_id=1, source_target_pairs={{0,30},{2,0},{4,2},{6,4},{8,6},{10,8},{12,10},{14,12},{16,14},{18,... | collective-permute-start | bytes 104456 | tf_op jit(solution)/shard_map/ppermute | solution.py:212
  16.6 2.1 %collective-permute-start.2 = (bf16[528,128]{1,0:T(8,128)(2,1)S(1)}, bf16[528,128]{1,0:T(8,128)(2,1)S(1)}, u32[]{:S(2)}, u32[]{:S(2)}) collective-permute-start(bf16[528,128]{1,0:T(8,128)(2,1)S(1)} %copy-done), channel_id=1, source_target_pairs={{0,1},{1,0},{2,3},{3,2},{4,5},{5,4},{6,7},{7,6},{8,9},{9,8},{10,11... | collective-permute-start | bytes 405512 | tf_op jit(solution)/shard_map/ppermute | solution.py:240
  18.7 7.8 %copy-start.1 = (s32[16,7]{0,1:T(8,128)S(1)}, s32[16,7]{0,1:T(8,128)}, u32[]{:S(2)}) copy-start(s32[16,7]{0,1:T(8,128)} %param.6) | copy-start | bytes 1348

commit v11 on v10

--- a/solution.py
+++ b/solution.py
@@ -55,16 +55,6 @@
     return table
 
 
-def fill(ref, block, table, picks, marks):
-    sub = lax.broadcasted_iota(jnp.int32, (marks, LANES), 0)
-    mark = jnp.zeros((marks, LANES), jnp.float32)
-    for s, (row, index) in enumerate(picks):
-        tile = table[pl.ds(pl.multiple_of(row * PACK, PACK), PACK), :]
-        ref[(*block, pl.ds(s * PACK, PACK), slice(None))] = tile
-        mark = jnp.where(sub == s, mask_row(index, (marks, LANES)), mark)
-    ref[(*block, pl.ds(len(picks) * PACK, marks), slice(None))] = mark.astype(BF16)
-
-
 def alternating(n):
     return [i // 4 + i % 2 * (n // 2) + i // 2 % 2 * (n // 4) for i in range(n)]
 
@@ -77,24 +67,28 @@
     arriving = [pltpu.make_async_copy(x, y, in_sems.at[i]) for i, (x, y) in enumerate(pairs)]
     for copy in arriving:
         copy.start()
-    arriving[0].wait()
-    unpack_rows(flat_ref, scratch)
     arriving[1].wait()
     arriving[2].wait()
-    turn_rows(lambda r: index_ref[0, r], scratch, own_ref, 0)
-    own_ref[rows * PACK :, :] = mask_table(lambda r: index_ref[0, r], rows).astype(BF16)
-    leaving = [pltpu.make_async_copy(own_ref, own_hbm, out_sems.at[n + 2])]
-    leaving[0].start()
-
-    def look(slot):
-        row = send_ref[0, slot]
-        return row, index_ref[0, row]
-
     targets = [(target * S, out_hbm.at[j]) for j, target in enumerate(alternating(n))]
     targets.append((lax.rem(me + n - 1, n) * S + S2, left_hbm))
     targets.append((lax.rem(me + 1, n) * S + S2, right_hbm))
-    for j, (first, out) in enumerate(targets):
-        fill(blocks, (j,), own_ref, [look(first + s) for s in range(S2)], 8)
+    picks = [[send_ref[0, first + s] for s in range(S2)] for first, _ in targets]
+    sub = lax.broadcasted_iota(jnp.int32, (8, LANES), 0)
+    for j, picked in enumerate(picks):
+        mark = jnp.zeros((8, LANES), jnp.float32)
+        for s, row in enumerate(picked):
+            mark = jnp.where(sub == s, mask_row(index_ref[0, row], (8, LANES)), mark)
+        blocks[j, S2 * PACK :, :] = mark.astype(BF16)
+    own_ref[rows * PACK :, :] = mask_table(lambda r: index_ref[0, r], rows).astype(BF16)
+    arriving[0].wait()
+    unpack_rows(flat_ref, scratch)
+    turn_rows(lambda r: index_ref[0, r], scratch, own_ref, 0)
+    leaving = [pltpu.make_async_copy(own_ref, own_hbm, out_sems.at[n + 2])]
+    leaving[0].start()
+    for j, (picked, (_, out)) in enumerate(zip(picks, targets)):
+        for s, row in enumerate(picked):
+            tile = own_ref[pl.ds(pl.multiple_of(row * PACK, PACK), PACK), :]
+            blocks[j, s * PACK : (s + 1) * PACK, :] = tile
         leaving.append(pltpu.make_async_copy(blocks.at[j], out, out_sems.at[j]))
         leaving[-1].start()
     for copy in leaving:

time: 40.9 us -> 40.9 us (level)
  no operation moved by 1% of the time
where the time goes in v11:
time: 40.9 us; the launch traced here: 40.6 us
  starting transfers between devices  14.1 us (34%)
  blocking collectives  12 us (29%)
  waiting for transfers between devices  7.44 us (18%)
  Pallas kernels  6.39 us (16%)
  other arithmetic  0.62 us (2%)
    all_to_all x1, blocking collectives, exchange(): lax.all_to_all(x, 'row', split_axis=0, concat_axis=0, tiled=True, axis_in...  12 us
    all_to_all x1, starting transfers between devices, exchange(): lax.all_to_all(x, 'row', split_axis=0, concat_axis=0, tiled=True, axis_in...  8.46 us
    ppermute x2, waiting for transfers between devices, ring(): return lax.ppermute(x, 'row', [(i, (i + step) % n) for i in range(n)])  7.44 us
    ppermute x2, starting transfers between devices, ring(): return lax.ppermute(x, 'row', [(i, (i + step) % n) for i in range(n)])  5.67 us
    pallas_call x3, Pallas kernels, call(): pl.pallas_call(body, out_shape=out_shape, in_specs=[SMEM] * smem + [VMEM]...  4 us
    pallas_call x1, Pallas kernels, shards(): pl.pallas_call(functools.partial(own_kernel, n), out_shape=(blocks, shape...  2.39 us
  transfers between devices with their start and end apart: 4, of which 1 were waited for; matrix products, arithmetic and copies ran while one was open for 0% of the time, Pallas kernels for 6%

profile of v11, /device:TPU:0, one launch (start us, length us, event | category | flops | bytes accessed | tf_op | source)
XLA Modules:
  0.0 40.6 jit_solution(11773361963939785929)
XLA Ops:
  0.0 0.0 copy-start.2
  0.0 2.4 %own.1 = (bf16[16,136,128]{2,1,0:T(8,128)(2,1)}, bf16[528,128]{1,0:T(8,128)(2,1)}, bf16[136,128]{1,0:T(8,128)(2,1)}, bf16[136,128]{1,0:T(8,128)(2,1)}) custom-call(s32[1,128]{1,0:T(1,128)} %send_hbm.1, s32[1,16]{1,0:T(1,128)} %bitcast.9, bf16[16,4096]{1,0:T(8,128)(2,1)} %bitcast.8), custom_call_target="tpu_custom_call" | custom-call | flops 10000000 | bytes 1048576 | tf_op jit(solution)/shard_map/own/pallas_call | solution.py:211
  2.4 0.0 copy-start.4
  2.4 0.0 copy-start.3
  2.4 0.0 copy-start
  2.4 8.5 %all-to-all-start = ((bf16[16,136,128]{2,1,0:T(8,128)(2,1)}), bf16[16,136,128]{2,1,0:T(8,128)(2,1)S(1)}, u32[]{:S(2)}, u32[]{:S(2)}) async-start(bf16[16,136,128]{2,1,0:T(8,128)(2,1)} %get-tuple-element.18), calls=%async_computation | async-start | bytes 1114112 | tf_op jit(solution)/shard_map/all_to_all | solution.py:201
  10.9 0.0 copy-done.4
  10.9 2.0 %collective-permute-start = (bf16[136,128]{1,0:T(8,128)(2,1)S(1)}, bf16[136,128]{1,0:T(8,128)(2,1)S(1)}, u32[]{:S(2)}, u32[]{:S(2)}) collective-permute-start(bf16[136,128]{1,0:T(8,128)(2,1)S(1)} %copy-done.4), channel_id=1, source_target_pairs={{0,2},{2,4},{4,6},{6,8},{8,10},{10,12},{12,14},{14,16},{16,18},{18... | collective-permute-start | bytes 104456 | tf_op jit(solution)/shard_map/ppermute | solution.py:206
  12.9 0.0 copy-done.3
  12.9 3.7 %collective-permute-start.1 = (bf16[136,128]{1,0:T(8,128)(2,1)S(1)}, bf16[136,128]{1,0:T(8,128)(2,1)S(1)}, u32[]{:S(2)}, u32[]{:S(2)}) collective-permute-start(bf16[136,128]{1,0:T(8,128)(2,1)S(1)} %copy-done.3), channel_id=1, source_target_pairs={{0,30},{2,0},{4,2},{6,4},{8,6},{10,8},{12,10},{14,12},{16,14},{18,... | collective-permute-start | bytes 104456 | tf_op jit(solution)/shard_map/ppermute | solution.py:206
  16.6 0.0 copy-done
  16.6 0.0 collective-permute-start.2
  16.6 0.0 copy-done.2
  16.6 2.1 %coupling.1.coupling_ref = bf16[16,64,512]{2,1,0:T(8,128)(2,1)S(1)} custom-call(bf16[7,16,4096]{2,1,0:T(8,128)(2,1)S(1)} %bitcast.7), custom_call_target="tpu_custom_call" | custom-call | flops 2000000000 | bytes 1048576 | tf_op jit(solution)/shard_map/coupling/pallas_call | solution.py:186
  18.7 0.0 collective-permute-done.2.refs_1_
  18.7 0.0 copy-start.1
  18.7 0.3 restrict.1.restrict_ref
  19.0 7.4 %collective-permute-done.left_ref = bf16[136,128]{1,0:T(8,128)(2,1)S(1)} collective-permute-done((bf16[136,128]{1,0:T(8,128)(2,1)S(1)}, bf16[136,128]{1,0:T(8,128)(2,1)S(1)}, u32[]{:S(2)}, u32[]{:S(2)}) %collective-permute-start) | collective-permute-done | bytes 34848 | tf_op jit(solution)/shard_map/ppermute | solution.py:206
  26.4 0.0 collective-permute-done.1.right_ref
  26.5 0.0 all-to-all-done.ghost_ref
  26.5 0.0 copy-done.1
  26.5 1.6 %product.1 = f32[256,128]{1,0:T(8,128)S(1)} custom-call(s32[7,16]{1,0:T(8,128)S(1)} %bitcast.6, bf16[16,136,128]{2,1,0:T(8,128)(2,1)S(1)} %all-to-all-done.ghost_ref, bf16[136,128]{1,0:T(8,128)(2,1)S(1)} %collective-permute-done.left_ref, bf16[136,128]{1,0:T(8,128)(2,1)S(1)} %collective-permute-done.1.right_ref, bf16[528,128]{1,0:T(8,128)(2,1)S(1)} %copy-done, ...), custom_call_target="tpu_custom_call" | custom-call | flops 200000000 | bytes 1048576 | tf_op jit(solution)/shard_map/product/pallas_call | solution.py:186
  28.1 12.0 %all_to_all.10 = f32[16,16,128]{2,1,0:T(8,128)S(1)} all-to-all(f32[16,16,128]{2,1,0:T(8,128)S(1)} %bitcast.5), channel_id=1, replica_groups={{0,16,8,24,2,18,10,26,4,20,12,28,6,22,14,30},{1,17,9,25,3,19,11,27,5,21..., dimensions={0} | all-to-all | bytes 262144 | tf_op jit(solution)/shard_map/all_to_all | solution.py:201
  40.0 0.6 %reduce_sum.9 = f32[16,128]{1,0:T(8,128)} reduce(f32[16,16,128]{2,1,0:T(8,128)S(1)} %all_to_all.10, f32[]{:T(128)} %constant.0.clone.1), dimensions={0}, to_apply=%region_0.0 | reduce | flops 30720 | bytes 139268 | tf_op jit(solution)/shard_map/reduce_sum | solution.py:265
Async XLA Ops:
  0.0 16.6 %copy-start.2 = (bf16[16,7,4096]{2,0,1:T(8,128)(2,1)S(1)}, bf16[16,7,4096]{2,0,1:T(8,128)(2,1)}, u32[]{:S(2)}) copy-start(bf16[16,7,4096]{2,0,1:T(8,128)(2,1)} %param.5) | copy-start | bytes 2752516
  2.4 8.5 %copy-start.4 = (bf16[136,128]{1,0:T(8,128)(2,1)S(1)}, bf16[136,128]{1,0:T(8,128)(2,1)}, u32[]{:S(2)}) copy-start(bf16[136,128]{1,0:T(8,128)(2,1)} %get-tuple-element.19) | copy-start | bytes 104452
  2.4 10.5 %copy-start.3 = (bf16[136,128]{1,0:T(8,128)(2,1)S(1)}, bf16[136,128]{1,0:T(8,128)(2,1)}, u32[]{:S(2)}) copy-start(bf16[136,128]{1,0:T(8,128)(2,1)} %get-tuple-element.20) | copy-start | bytes 104452
  2.4 14.2 %copy-start = (bf16[528,128]{1,0:T(8,128)(2,1)S(1)}, bf16[528,128]{1,0:T(8,128)(2,1)}, u32[]{:S(2)}) copy-start(bf16[528,128]{1,0:T(8,128)(2,1)} %get-tuple-element.21.refs_0_.own_ref) | copy-start | bytes 405508
  2.4 24.0 %all-to-all-start = ((bf16[16,136,128]{2,1,0:T(8,128)(2,1)}), bf16[16,136,128]{2,1,0:T(8,128)(2,1)S(1)}, u32[]{:S(2)}, u32[]{:S(2)}) async-start(bf16[16,136,128]{2,1,0:T(8,128)(2,1)} %get-tuple-element.18), calls=%async_computation | async-start | bytes 1114112 | tf_op jit(solution)/shard_map/all_to_all | solution.py:201
  10.9 15.5 %collective-permute-start = (bf16[136,128]{1,0:T(8,128)(2,1)S(1)}, bf16[136,128]{1,0:T(8,128)(2,1)S(1)}, u32[]{:S(2)}, u32[]{:S(2)}) collective-permute-start(bf16[136,128]{1,0:T(8,128)(2,1)S(1)} %copy-done.4), channel_id=1, source_target_pairs={{0,2},{2,4},{4,6},{6,8},{8,10},{10,12},{12,14},{14,16},{16,18},{18... | collective-permute-start | bytes 104456 | tf_op jit(solution)/shard_map/ppermute | solution.py:206
  12.9 13.6 %collective-permute-start.1 = (bf16[136,128]{1,0:T(8,128)(2,1)S(1)}, bf16[136,128]{1,0:T(8,128)(2,1)S(1)}, u32[]{:S(2)}, u32[]{:S(2)}) collective-permute-start(bf16[136,128]{1,0:T(8,128)(2,1)S(1)} %copy-done.3), channel_id=1, source_target_pairs={{0,30},{2,0},{4,2},{6,4},{8,6},{10,8},{12,10},{14,12},{16,14},{18,... | collective-permute-start | bytes 104456 | tf_op jit(solution)/shard_map/ppermute | solution.py:206
  16.6 2.1 %collective-permute-start.2 = (bf16[528,128]{1,0:T(8,128)(2,1)S(1)}, bf16[528,128]{1,0:T(8,128)(2,1)S(1)}, u32[]{:S(2)}, u32[]{:S(2)}) collective-permute-start(bf16[528,128]{1,0:T(8,128)(2,1)S(1)} %copy-done), channel_id=1, source_target_pairs={{0,1},{1,0},{2,3},{3,2},{4,5},{5,4},{6,7},{7,6},{8,9},{9,8},{10,11... | collective-permute-start | bytes 405512 | tf_op jit(solution)/shard_map/ppermute | solution.py:234
  18.7 7.8 %copy-start.1 = (s32[16,7]{0,1:T(8,128)S(1)}, s32[16,7]{0,1:T(8,128)}, u32[]{:S(2)}) copy-start(s32[16,7]{0,1:T(8,128)} %param.6) | copy-start | bytes 1348

commit v12 on v10

--- a/solution.py
+++ b/solution.py
@@ -69,36 +69,29 @@
     return [i // 4 + i % 2 * (n // 2) + i // 2 % 2 * (n // 4) for i in range(n)]
 
 
-def own_kernel(n, send_hbm, index_hbm, flat_hbm, out_hbm, own_hbm, left_hbm, right_hbm, *refs):
-    send_ref, index_ref, flat_ref, scratch, own_ref, blocks, in_sems, out_sems = refs
+def own_kernel(n, send_hbm, index_hbm, flat_hbm, out_ref, own_ref, left_ref, right_ref, *refs):
+    send_ref, index_ref, flat_ref, scratch, sems = refs
     rows = flat_ref.shape[0]
     me = lax.axis_index("row")
     pairs = ((flat_hbm, flat_ref), (send_hbm, send_ref), (index_hbm, index_ref))
-    arriving = [pltpu.make_async_copy(x, y, in_sems.at[i]) for i, (x, y) in enumerate(pairs)]
-    for copy in arriving:
+    copies = [pltpu.make_async_copy(x, y, sems.at[i]) for i, (x, y) in enumerate(pairs)]
+    for copy in copies:
         copy.start()
-    arriving[0].wait()
+    for copy in copies:
+        copy.wait()
     unpack_rows(flat_ref, scratch)
-    arriving[1].wait()
-    arriving[2].wait()
     turn_rows(lambda r: index_ref[0, r], scratch, own_ref, 0)
     own_ref[rows * PACK :, :] = mask_table(lambda r: index_ref[0, r], rows).astype(BF16)
-    leaving = [pltpu.make_async_copy(own_ref, own_hbm, out_sems.at[n + 2])]
-    leaving[0].start()
 
     def look(slot):
         row = send_ref[0, slot]
         return row, index_ref[0, row]
 
-    targets = [(target * S, out_hbm.at[j]) for j, target in enumerate(alternating(n))]
-    targets.append((lax.rem(me + n - 1, n) * S + S2, left_hbm))
-    targets.append((lax.rem(me + 1, n) * S + S2, right_hbm))
-    for j, (first, out) in enumerate(targets):
-        fill(blocks, (j,), own_ref, [look(first + s) for s in range(S2)], 8)
-        leaving.append(pltpu.make_async_copy(blocks.at[j], out, out_sems.at[j]))
-        leaving[-1].start()
-    for copy in leaving:
-        copy.wait()
+    for j, target in enumerate(alternating(n)):
+        fill(out_ref, (j,), own_ref, [look(target * S + s) for s in range(S2)], 8)
+    for ref, step in ((left_ref, n - 1), (right_ref, 1)):
+        first = lax.rem(me + step, n) * S
+        fill(ref, (), own_ref, [look(first + s) for s in range(S2, S)], 8)
 
 
 def coupling_kernel(a_ref, coupling_ref, scratch):
@@ -218,16 +211,13 @@
         functools.partial(own_kernel, n),
         out_shape=(blocks, shape(rows * PACK + rows, LANES), edge, edge),
         in_specs=[HBM] * 3,
-        out_specs=(HBM,) * 4,
+        out_specs=(VMEM,) * 4,
         scratch_shapes=[
             pltpu.SMEM(send_rows.shape, jnp.int32),
             pltpu.SMEM(index.shape, jnp.int32),
             pltpu.VMEM(flat.shape, BF16),
             unpacked,
-            pltpu.VMEM((rows * PACK + rows, LANES), BF16),
-            pltpu.VMEM((n + 2, *edge.shape), BF16),
             pltpu.SemaphoreType.DMA((3,)),
-            pltpu.SemaphoreType.DMA((n + 3,)),
         ],
         compiler_params=pltpu.CompilerParams(vmem_limit_bytes=WHOLE),
         cost_estimate=pl.CostEstimate(flops=10**7, bytes_accessed=2**20, transcendentals=0),

time: 40.9 us -> 40.8 us (level)
  no operation moved by 1% of the time
where the time goes in v12:
time: 40.8 us; the launch traced here: 40.6 us
  starting transfers between devices  14.1 us (35%)
  blocking collectives  12 us (29%)
  waiting for transfers between devices  7.44 us (18%)
  Pallas kernels  6.31 us (15%)
  other arithmetic  0.62 us (2%)
    all_to_all x1, blocking collectives, exchange(): lax.all_to_all(x, 'row', split_axis=0, concat_axis=0, tiled=True, axis_in...  12 us
    all_to_all x1, starting transfers between devices, exchange(): lax.all_to_all(x, 'row', split_axis=0, concat_axis=0, tiled=True, axis_in...  8.46 us
    ppermute x2, waiting for transfers between devices, ring(): return lax.ppermute(x, 'row', [(i, (i + step) % n) for i in range(n)])  7.44 us
    ppermute x2, starting transfers between devices, ring(): return lax.ppermute(x, 'row', [(i, (i + step) % n) for i in range(n)])  5.67 us
    pallas_call x3, Pallas kernels, call(): pl.pallas_call(body, out_shape=out_shape, in_specs=[SMEM] * smem + [VMEM]...  4 us
    pallas_call x1, Pallas kernels, shards(): pl.pallas_call(functools.partial(own_kernel, n), out_shape=(blocks, shape...  2.3 us
  transfers between devices with their start and end apart: 4, of which 1 were waited for; matrix products, arithmetic and copies ran while one was open for 0% of the time, Pallas kernels for 6%

profile of v12, /device:TPU:0, one launch (start us, length us, event | category | flops | bytes accessed | tf_op | source)
XLA Modules:
  0.0 40.6 jit_solution(4474179906894029361)
XLA Ops:
  0.0 0.0 copy-start.2
  0.0 2.3 %own.1 = (bf16[16,136,128]{2,1,0:T(8,128)(2,1)}, bf16[528,128]{1,0:T(8,128)(2,1)}, bf16[136,128]{1,0:T(8,128)(2,1)}, bf16[136,128]{1,0:T(8,128)(2,1)}) custom-call(s32[1,128]{1,0:T(1,128)} %send_hbm.1, s32[1,16]{1,0:T(1,128)} %bitcast.9, bf16[16,4096]{1,0:T(8,128)(2,1)} %bitcast.8), custom_call_target="tpu_custom_call" | custom-call | flops 10000000 | bytes 1048576 | tf_op jit(solution)/shard_map/own/pallas_call | solution.py:210
  2.3 0.0 copy-start.4
  2.3 0.0 copy-start.3
  2.3 0.0 copy-start
  2.3 8.5 %all-to-all-start = ((bf16[16,136,128]{2,1,0:T(8,128)(2,1)}), bf16[16,136,128]{2,1,0:T(8,128)(2,1)S(1)}, u32[]{:S(2)}, u32[]{:S(2)}) async-start(bf16[16,136,128]{2,1,0:T(8,128)(2,1)} %get-tuple-element.18), calls=%async_computation | async-start | bytes 1114112 | tf_op jit(solution)/shard_map/all_to_all | solution.py:200
  10.8 0.0 copy-done.4
  10.8 2.0 %collective-permute-start = (bf16[136,128]{1,0:T(8,128)(2,1)S(1)}, bf16[136,128]{1,0:T(8,128)(2,1)S(1)}, u32[]{:S(2)}, u32[]{:S(2)}) collective-permute-start(bf16[136,128]{1,0:T(8,128)(2,1)S(1)} %copy-done.4), channel_id=1, source_target_pairs={{0,2},{2,4},{4,6},{6,8},{8,10},{10,12},{12,14},{14,16},{16,18},{18... | collective-permute-start | bytes 104456 | tf_op jit(solution)/shard_map/ppermute | solution.py:205
  12.8 0.0 copy-done.3
  12.8 3.7 %collective-permute-start.1 = (bf16[136,128]{1,0:T(8,128)(2,1)S(1)}, bf16[136,128]{1,0:T(8,128)(2,1)S(1)}, u32[]{:S(2)}, u32[]{:S(2)}) collective-permute-start(bf16[136,128]{1,0:T(8,128)(2,1)S(1)} %copy-done.3), channel_id=1, source_target_pairs={{0,30},{2,0},{4,2},{6,4},{8,6},{10,8},{12,10},{14,12},{16,14},{18,... | collective-permute-start | bytes 104456 | tf_op jit(solution)/shard_map/ppermute | solution.py:205
  16.5 0.0 copy-done
  16.5 0.0 collective-permute-start.2
  16.5 0.0 copy-done.2
  16.5 2.1 %coupling.1.coupling_ref = bf16[16,64,512]{2,1,0:T(8,128)(2,1)S(1)} custom-call(bf16[7,16,4096]{2,1,0:T(8,128)(2,1)S(1)} %bitcast.7), custom_call_target="tpu_custom_call" | custom-call | flops 2000000000 | bytes 1048576 | tf_op jit(solution)/shard_map/coupling/pallas_call | solution.py:185
  18.6 0.0 collective-permute-done.2.refs_1_
  18.6 0.0 copy-start.1
  18.6 0.3 restrict.1.restrict_ref
  18.9 7.4 %collective-permute-done.left_ref = bf16[136,128]{1,0:T(8,128)(2,1)S(1)} collective-permute-done((bf16[136,128]{1,0:T(8,128)(2,1)S(1)}, bf16[136,128]{1,0:T(8,128)(2,1)S(1)}, u32[]{:S(2)}, u32[]{:S(2)}) %collective-permute-start) | collective-permute-done | bytes 34848 | tf_op jit(solution)/shard_map/ppermute | solution.py:205
  26.4 0.0 collective-permute-done.1.right_ref
  26.4 0.0 all-to-all-done.ghost_ref
  26.4 0.0 copy-done.1
  26.4 1.6 %product.1 = f32[256,128]{1,0:T(8,128)S(1)} custom-call(s32[7,16]{1,0:T(8,128)S(1)} %bitcast.6, bf16[16,136,128]{2,1,0:T(8,128)(2,1)S(1)} %all-to-all-done.ghost_ref, bf16[136,128]{1,0:T(8,128)(2,1)S(1)} %collective-permute-done.left_ref, bf16[136,128]{1,0:T(8,128)(2,1)S(1)} %collective-permute-done.1.right_ref, bf16[528,128]{1,0:T(8,128)(2,1)S(1)} %copy-done, ...), custom_call_target="tpu_custom_call" | custom-call | flops 200000000 | bytes 1048576 | tf_op jit(solution)/shard_map/product/pallas_call | solution.py:185
  28.0 12.0 %all_to_all.10 = f32[16,16,128]{2,1,0:T(8,128)S(1)} all-to-all(f32[16,16,128]{2,1,0:T(8,128)S(1)} %bitcast.5), channel_id=1, replica_groups={{0,16,8,24,2,18,10,26,4,20,12,28,6,22,14,30},{1,17,9,25,3,19,11,27,5,21..., dimensions={0} | all-to-all | bytes 262144 | tf_op jit(solution)/shard_map/all_to_all | solution.py:200
  39.9 0.6 %reduce_sum.9 = f32[16,128]{1,0:T(8,128)} reduce(f32[16,16,128]{2,1,0:T(8,128)S(1)} %all_to_all.10, f32[]{:T(128)} %constant.0.clone.1), dimensions={0}, to_apply=%region_0.0 | reduce | flops 30720 | bytes 139268 | tf_op jit(solution)/shard_map/reduce_sum | solution.py:261
Async XLA Ops:
  0.0 16.5 %copy-start.2 = (bf16[16,7,4096]{2,0,1:T(8,128)(2,1)S(1)}, bf16[16,7,4096]{2,0,1:T(8,128)(2,1)}, u32[]{:S(2)}) copy-start(bf16[16,7,4096]{2,0,1:T(8,128)(2,1)} %param.5) | copy-start | bytes 2752516
  2.3 8.5 %copy-start.4 = (bf16[136,128]{1,0:T(8,128)(2,1)S(1)}, bf16[136,128]{1,0:T(8,128)(2,1)}, u32[]{:S(2)}) copy-start(bf16[136,128]{1,0:T(8,128)(2,1)} %get-tuple-element.19) | copy-start | bytes 104452
  2.3 10.5 %copy-start.3 = (bf16[136,128]{1,0:T(8,128)(2,1)S(1)}, bf16[136,128]{1,0:T(8,128)(2,1)}, u32[]{:S(2)}) copy-start(bf16[136,128]{1,0:T(8,128)(2,1)} %get-tuple-element.20) | copy-start | bytes 104452
  2.3 14.2 %copy-start = (bf16[528,128]{1,0:T(8,128)(2,1)S(1)}, bf16[528,128]{1,0:T(8,128)(2,1)}, u32[]{:S(2)}) copy-start(bf16[528,128]{1,0:T(8,128)(2,1)} %get-tuple-element.21.refs_0_.own_ref) | copy-start | bytes 405508
  2.3 24.0 %all-to-all-start = ((bf16[16,136,128]{2,1,0:T(8,128)(2,1)}), bf16[16,136,128]{2,1,0:T(8,128)(2,1)S(1)}, u32[]{:S(2)}, u32[]{:S(2)}) async-start(bf16[16,136,128]{2,1,0:T(8,128)(2,1)} %get-tuple-element.18), calls=%async_computation | async-start | bytes 1114112 | tf_op jit(solution)/shard_map/all_to_all | solution.py:200
  10.8 15.5 %collective-permute-start = (bf16[136,128]{1,0:T(8,128)(2,1)S(1)}, bf16[136,128]{1,0:T(8,128)(2,1)S(1)}, u32[]{:S(2)}, u32[]{:S(2)}) collective-permute-start(bf16[136,128]{1,0:T(8,128)(2,1)S(1)} %copy-done.4), channel_id=1, source_target_pairs={{0,2},{2,4},{4,6},{6,8},{8,10},{10,12},{12,14},{14,16},{16,18},{18... | collective-permute-start | bytes 104456 | tf_op jit(solution)/shard_map/ppermute | solution.py:205
  12.8 13.6 %collective-permute-start.1 = (bf16[136,128]{1,0:T(8,128)(2,1)S(1)}, bf16[136,128]{1,0:T(8,128)(2,1)S(1)}, u32[]{:S(2)}, u32[]{:S(2)}) collective-permute-start(bf16[136,128]{1,0:T(8,128)(2,1)S(1)} %copy-done.3), channel_id=1, source_target_pairs={{0,30},{2,0},{4,2},{6,4},{8,6},{10,8},{12,10},{14,12},{16,14},{18,... | collective-permute-start | bytes 104456 | tf_op jit(solution)/shard_map/ppermute | solution.py:205
  16.5 2.1 %collective-permute-start.2 = (bf16[528,128]{1,0:T(8,128)(2,1)S(1)}, bf16[528,128]{1,0:T(8,128)(2,1)S(1)}, u32[]{:S(2)}, u32[]{:S(2)}) collective-permute-start(bf16[528,128]{1,0:T(8,128)(2,1)S(1)} %copy-done), channel_id=1, source_target_pairs={{0,1},{1,0},{2,3},{3,2},{4,5},{5,4},{6,7},{7,6},{8,9},{9,8},{10,11... | collective-permute-start | bytes 405512 | tf_op jit(solution)/shard_map/ppermute | solution.py:230
  18.6 7.8 %copy-start.1 = (s32[16,7]{0,1:T(8,128)S(1)}, s32[16,7]{0,1:T(8,128)}, u32[]{:S(2)}) copy-start(s32[16,7]{0,1:T(8,128)} %param.6) | copy-start | bytes 1348

commit v13 on v12

--- a/solution.py
+++ b/solution.py
@@ -173,6 +173,10 @@
     share = out_ref.shape[0] // n
     for j, target in enumerate(alternating(n)):
         out_ref[j * share : (j + 1) * share, :] = coarse[target * share : (target + 1) * share]
+
+
+def sum_kernel(parts_ref, out_ref):
+    out_ref[...] = jnp.sum(parts_ref[...], axis=0)
 
 
 def shards(n, col_size, a_tiles, neighbors, send_rows, p_tiles, p_index):
@@ -258,7 +262,7 @@
         2 * 10**8,
     )
     parts = exchange(partial.reshape(n, col_size * CP * B // n, CP * B))
-    return jnp.sum(parts, axis=0)
+    return call(sum_kernel, shape(*parts.shape[1:], dtype=f32), [], (parts,), 0, "sum")
 
 
 def solution(mesh):

time: 40.8 us -> 40.8 us (level)
  other arithmetic: 0.62 us -> 0 us
  Pallas kernels: 6.31 us -> 6.92 us
    pallas_call x3 -> x4, Pallas kernels: 4 us -> 4.62 us  [call(): pl.pallas_call(body, out_shape=out_shape, in_specs=[SMEM] * smem + [VMEM]...]
    reduce_sum x1 -> x0, other arithmetic: 0.62 us -> none  [shards(): return jnp.sum(parts, axis=0)]
where the time goes in v13:
time: 40.8 us; the launch traced here: 40.6 us
  starting transfers between devices  14.1 us (35%)
  blocking collectives  12 us (29%)
  waiting for transfers between devices  7.44 us (18%)
  Pallas kernels  6.92 us (17%)
    all_to_all x1, blocking collectives, exchange(): lax.all_to_all(x, 'row', split_axis=0, concat_axis=0, tiled=True, axis_in...  12 us
    all_to_all x1, starting transfers between devices, exchange(): lax.all_to_all(x, 'row', split_axis=0, concat_axis=0, tiled=True, axis_in...  8.46 us
    ppermute x2, waiting for transfers between devices, ring(): return lax.ppermute(x, 'row', [(i, (i + step) % n) for i in range(n)])  7.44 us
    ppermute x2, starting transfers between devices, ring(): return lax.ppermute(x, 'row', [(i, (i + step) % n) for i in range(n)])  5.67 us
    pallas_call x4, Pallas kernels, call(): pl.pallas_call(body, out_shape=out_shape, in_specs=[SMEM] * smem + [VMEM]...  4.62 us
    pallas_call x1, Pallas kernels, shards(): pl.pallas_call(functools.partial(own_kernel, n), out_shape=(blocks, shape...  2.3 us
  transfers between devices with their start and end apart: 4, of which 1 were waited for; matrix products, arithmetic and copies ran while one was open for 0% of the time, Pallas kernels for 6%

profile of v13, /device:TPU:0, one launch (start us, length us, event | category | flops | bytes accessed | tf_op | source)
XLA Modules:
  0.0 40.6 jit_solution(9295541777301284552)
XLA Ops:
  0.0 0.0 copy-start.2
  0.0 2.3 %own.1 = (bf16[16,136,128]{2,1,0:T(8,128)(2,1)}, bf16[528,128]{1,0:T(8,128)(2,1)}, bf16[136,128]{1,0:T(8,128)(2,1)}, bf16[136,128]{1,0:T(8,128)(2,1)}) custom-call(s32[1,128]{1,0:T(1,128)} %send_hbm.1, s32[1,16]{1,0:T(1,128)} %bitcast.9, bf16[16,4096]{1,0:T(8,128)(2,1)} %bitcast.8), custom_call_target="tpu_custom_call" | custom-call | flops 10000000 | bytes 1048576 | tf_op jit(solution)/shard_map/own/pallas_call | solution.py:214
  2.3 0.0 copy-start.4
  2.3 0.0 copy-start.3
  2.3 0.0 copy-start
  2.3 8.5 %all-to-all-start = ((bf16[16,136,128]{2,1,0:T(8,128)(2,1)}), bf16[16,136,128]{2,1,0:T(8,128)(2,1)S(1)}, u32[]{:S(2)}, u32[]{:S(2)}) async-start(bf16[16,136,128]{2,1,0:T(8,128)(2,1)} %get-tuple-element.18), calls=%async_computation | async-start | bytes 1114112 | tf_op jit(solution)/shard_map/all_to_all | solution.py:204
  10.8 0.0 copy-done.4
  10.8 2.0 %collective-permute-start = (bf16[136,128]{1,0:T(8,128)(2,1)S(1)}, bf16[136,128]{1,0:T(8,128)(2,1)S(1)}, u32[]{:S(2)}, u32[]{:S(2)}) collective-permute-start(bf16[136,128]{1,0:T(8,128)(2,1)S(1)} %copy-done.4), channel_id=1, source_target_pairs={{0,2},{2,4},{4,6},{6,8},{8,10},{10,12},{12,14},{14,16},{16,18},{18... | collective-permute-start | bytes 104456 | tf_op jit(solution)/shard_map/ppermute | solution.py:209
  12.8 0.0 copy-done.3
  12.8 3.7 %collective-permute-start.1 = (bf16[136,128]{1,0:T(8,128)(2,1)S(1)}, bf16[136,128]{1,0:T(8,128)(2,1)S(1)}, u32[]{:S(2)}, u32[]{:S(2)}) collective-permute-start(bf16[136,128]{1,0:T(8,128)(2,1)S(1)} %copy-done.3), channel_id=1, source_target_pairs={{0,30},{2,0},{4,2},{6,4},{8,6},{10,8},{12,10},{14,12},{16,14},{18,... | collective-permute-start | bytes 104456 | tf_op jit(solution)/shard_map/ppermute | solution.py:209
  16.5 0.0 copy-done
  16.5 0.0 collective-permute-start.2
  16.5 0.0 copy-done.2
  16.5 2.1 %coupling.1.coupling_ref = bf16[16,64,512]{2,1,0:T(8,128)(2,1)S(1)} custom-call(bf16[7,16,4096]{2,1,0:T(8,128)(2,1)S(1)} %bitcast.7), custom_call_target="tpu_custom_call" | custom-call | flops 2000000000 | bytes 1048576 | tf_op jit(solution)/shard_map/coupling/pallas_call | solution.py:189
  18.6 0.0 collective-permute-done.2.refs_1_
  18.6 0.0 copy-start.1
  18.6 0.3 restrict.1.restrict_ref
  18.9 7.4 %collective-permute-done.left_ref = bf16[136,128]{1,0:T(8,128)(2,1)S(1)} collective-permute-done((bf16[136,128]{1,0:T(8,128)(2,1)S(1)}, bf16[136,128]{1,0:T(8,128)(2,1)S(1)}, u32[]{:S(2)}, u32[]{:S(2)}) %collective-permute-start) | collective-permute-done | bytes 34848 | tf_op jit(solution)/shard_map/ppermute | solution.py:209
  26.4 0.0 collective-permute-done.1.right_ref
  26.4 0.0 all-to-all-done.ghost_ref
  26.4 0.0 copy-done.1
  26.4 1.6 %product.1 = f32[256,128]{1,0:T(8,128)S(1)} custom-call(s32[7,16]{1,0:T(8,128)S(1)} %bitcast.6, bf16[16,136,128]{2,1,0:T(8,128)(2,1)S(1)} %all-to-all-done.ghost_ref, bf16[136,128]{1,0:T(8,128)(2,1)S(1)} %collective-permute-done.left_ref, bf16[136,128]{1,0:T(8,128)(2,1)S(1)} %collective-permute-done.1.right_ref, bf16[528,128]{1,0:T(8,128)(2,1)S(1)} %copy-done, ...), custom_call_target="tpu_custom_call" | custom-call | flops 200000000 | bytes 1048576 | tf_op jit(solution)/shard_map/product/pallas_call | solution.py:189
  28.0 12.0 %all_to_all.10.parts_ref = f32[16,16,128]{2,1,0:T(8,128)S(1)} all-to-all(f32[16,16,128]{2,1,0:T(8,128)S(1)} %bitcast.5), channel_id=1, replica_groups={{0,16,8,24,2,18,10,26,4,20,12,28,6,22,14,30},{1,17,9,25,3,19,11,27,5,21..., dimensions={0} | all-to-all | bytes 262144 | tf_op jit(solution)/shard_map/all_to_all | solution.py:204
  39.9 0.6 %sum.1 = f32[16,128]{1,0:T(8,128)} custom-call(f32[16,16,128]{2,1,0:T(8,128)S(1)} %all_to_all.10.parts_ref), custom_call_target="tpu_custom_call" | custom-call | flops 10000000 | bytes 1048576 | tf_op jit(solution)/shard_map/sum/pallas_call | solution.py:189
Async XLA Ops:
  0.0 16.5 %copy-start.2 = (bf16[16,7,4096]{2,0,1:T(8,128)(2,1)S(1)}, bf16[16,7,4096]{2,0,1:T(8,128)(2,1)}, u32[]{:S(2)}) copy-start(bf16[16,7,4096]{2,0,1:T(8,128)(2,1)} %param.5) | copy-start | bytes 2752516
  2.3 8.5 %copy-start.4 = (bf16[136,128]{1,0:T(8,128)(2,1)S(1)}, bf16[136,128]{1,0:T(8,128)(2,1)}, u32[]{:S(2)}) copy-start(bf16[136,128]{1,0:T(8,128)(2,1)} %get-tuple-element.19) | copy-start | bytes 104452
  2.3 10.5 %copy-start.3 = (bf16[136,128]{1,0:T(8,128)(2,1)S(1)}, bf16[136,128]{1,0:T(8,128)(2,1)}, u32[]{:S(2)}) copy-start(bf16[136,128]{1,0:T(8,128)(2,1)} %get-tuple-element.20) | copy-start | bytes 104452
  2.3 14.2 %copy-start = (bf16[528,128]{1,0:T(8,128)(2,1)S(1)}, bf16[528,128]{1,0:T(8,128)(2,1)}, u32[]{:S(2)}) copy-start(bf16[528,128]{1,0:T(8,128)(2,1)} %get-tuple-element.21.refs_0_.own_ref) | copy-start | bytes 405508
  2.3 24.0 %all-to-all-start = ((bf16[16,136,128]{2,1,0:T(8,128)(2,1)}), bf16[16,136,128]{2,1,0:T(8,128)(2,1)S(1)}, u32[]{:S(2)}, u32[]{:S(2)}) async-start(bf16[16,136,128]{2,1,0:T(8,128)(2,1)} %get-tuple-element.18), calls=%async_computation | async-start | bytes 1114112 | tf_op jit(solution)/shard_map/all_to_all | solution.py:204
  10.8 15.5 %collective-permute-start = (bf16[136,128]{1,0:T(8,128)(2,1)S(1)}, bf16[136,128]{1,0:T(8,128)(2,1)S(1)}, u32[]{:S(2)}, u32[]{:S(2)}) collective-permute-start(bf16[136,128]{1,0:T(8,128)(2,1)S(1)} %copy-done.4), channel_id=1, source_target_pairs={{0,2},{2,4},{4,6},{6,8},{8,10},{10,12},{12,14},{14,16},{16,18},{18... | collective-permute-start | bytes 104456 | tf_op jit(solution)/shard_map/ppermute | solution.py:209
  12.8 13.6 %collective-permute-start.1 = (bf16[136,128]{1,0:T(8,128)(2,1)S(1)}, bf16[136,128]{1,0:T(8,128)(2,1)S(1)}, u32[]{:S(2)}, u32[]{:S(2)}) collective-permute-start(bf16[136,128]{1,0:T(8,128)(2,1)S(1)} %copy-done.3), channel_id=1, source_target_pairs={{0,30},{2,0},{4,2},{6,4},{8,6},{10,8},{12,10},{14,12},{16,14},{18,... | collective-permute-start | bytes 104456 | tf_op jit(solution)/shard_map/ppermute | solution.py:209
  16.5 2.1 %collective-permute-start.2 = (bf16[528,128]{1,0:T(8,128)(2,1)S(1)}, bf16[528,128]{1,0:T(8,128)(2,1)S(1)}, u32[]{:S(2)}, u32[]{:S(2)}) collective-permute-start(bf16[528,128]{1,0:T(8,128)(2,1)S(1)} %copy-done), channel_id=1, source_target_pairs={{0,1},{1,0},{2,3},{3,2},{4,5},{5,4},{6,7},{7,6},{8,9},{9,8},{10,11... | collective-permute-start | bytes 405512 | tf_op jit(solution)/shard_map/ppermute | solution.py:234
  18.6 7.8 %copy-start.1 = (s32[16,7]{0,1:T(8,128)S(1)}, s32[16,7]{0,1:T(8,128)}, u32[]{:S(2)}) copy-start(s32[16,7]{0,1:T(8,128)} %param.6) | copy-start | bytes 1348

commit v14 on v12

--- a/solution.py
+++ b/solution.py
@@ -142,9 +142,11 @@
         wide[pl.ds(pl.multiple_of(to + PACK, PACK), PACK), :] = odd
 
     def place_slots(first, ref, block):
+        masks = ref[(*block, pl.ds(S2 * PACK, 8), slice(None))].astype(jnp.float32)
         for s in range(S2):
             tile = ref[(*block, pl.ds(s * PACK, PACK), slice(None))]
-            place(rows + first + s, tile, ref[(*block, pl.ds(S2 * PACK + s, 1), slice(None))])
+            mask = jnp.broadcast_to(masks[s : s + 1], (PACK, LANES)).astype(BF16)
+            place(rows + first + s, tile, mask)
 
     for r in range(rows):
         place(r, own_ref[r * PACK : (r + 1) * PACK, :], own_ref[rows * PACK + r : rows * PACK + r + 1, :])

time: 40.8 us -> 40.8 us (level)
  no operation moved by 1% of the time
where the time goes in v14:
time: 40.8 us; the launch traced here: 40.5 us
  starting transfers between devices  14.1 us (35%)
  blocking collectives  12 us (29%)
  waiting for transfers between devices  7.44 us (18%)
  Pallas kernels  6.28 us (15%)
  other arithmetic  0.62 us (2%)
    all_to_all x1, blocking collectives, exchange(): lax.all_to_all(x, 'row', split_axis=0, concat_axis=0, tiled=True, axis_in...  12 us
    all_to_all x1, starting transfers between devices, exchange(): lax.all_to_all(x, 'row', split_axis=0, concat_axis=0, tiled=True, axis_in...  8.46 us
    ppermute x2, waiting for transfers between devices, ring(): return lax.ppermute(x, 'row', [(i, (i + step) % n) for i in range(n)])  7.44 us
    ppermute x2, starting transfers between devices, ring(): return lax.ppermute(x, 'row', [(i, (i + step) % n) for i in range(n)])  5.67 us
    pallas_call x3, Pallas kernels, call(): pl.pallas_call(body, out_shape=out_shape, in_specs=[SMEM] * smem + [VMEM]...  3.98 us
    pallas_call x1, Pallas kernels, shards(): pl.pallas_call(functools.partial(own_kernel, n), out_shape=(blocks, shape...  2.3 us
  transfers between devices with their start and end apart: 4, of which 1 were waited for; matrix products, arithmetic and copies ran while one was open for 0% of the time, Pallas kernels for 6%

profile of v14, /device:TPU:0, one launch (start us, length us, event | category | flops | bytes accessed | tf_op | source)
XLA Modules:
  0.0 40.5 jit_solution(6792949828551778673)
XLA Ops:
  0.0 0.0 copy-start.2
  0.0 2.3 %own.1 = (bf16[16,136,128]{2,1,0:T(8,128)(2,1)}, bf16[528,128]{1,0:T(8,128)(2,1)}, bf16[136,128]{1,0:T(8,128)(2,1)}, bf16[136,128]{1,0:T(8,128)(2,1)}) custom-call(s32[1,128]{1,0:T(1,128)} %send_hbm.1, s32[1,16]{1,0:T(1,128)} %bitcast.9, bf16[16,4096]{1,0:T(8,128)(2,1)} %bitcast.8), custom_call_target="tpu_custom_call" | custom-call | flops 10000000 | bytes 1048576 | tf_op jit(solution)/shard_map/own/pallas_call | solution.py:212
  2.3 0.0 copy-start.4
  2.3 0.0 copy-start.3
  2.3 0.0 copy-start
  2.3 8.5 %all-to-all-start = ((bf16[16,136,128]{2,1,0:T(8,128)(2,1)}), bf16[16,136,128]{2,1,0:T(8,128)(2,1)S(1)}, u32[]{:S(2)}, u32[]{:S(2)}) async-start(bf16[16,136,128]{2,1,0:T(8,128)(2,1)} %get-tuple-element.18), calls=%async_computation | async-start | bytes 1114112 | tf_op jit(solution)/shard_map/all_to_all | solution.py:202
  10.8 0.0 copy-done.4
  10.8 2.0 %collective-permute-start = (bf16[136,128]{1,0:T(8,128)(2,1)S(1)}, bf16[136,128]{1,0:T(8,128)(2,1)S(1)}, u32[]{:S(2)}, u32[]{:S(2)}) collective-permute-start(bf16[136,128]{1,0:T(8,128)(2,1)S(1)} %copy-done.4), channel_id=1, source_target_pairs={{0,2},{2,4},{4,6},{6,8},{8,10},{10,12},{12,14},{14,16},{16,18},{18... | collective-permute-start | bytes 104456 | tf_op jit(solution)/shard_map/ppermute | solution.py:207
  12.8 0.0 copy-done.3
  12.8 3.7 %collective-permute-start.1 = (bf16[136,128]{1,0:T(8,128)(2,1)S(1)}, bf16[136,128]{1,0:T(8,128)(2,1)S(1)}, u32[]{:S(2)}, u32[]{:S(2)}) collective-permute-start(bf16[136,128]{1,0:T(8,128)(2,1)S(1)} %copy-done.3), channel_id=1, source_target_pairs={{0,30},{2,0},{4,2},{6,4},{8,6},{10,8},{12,10},{14,12},{16,14},{18,... | collective-permute-start | bytes 104456 | tf_op jit(solution)/shard_map/ppermute | solution.py:207
  16.5 0.0 copy-done
  16.5 0.0 collective-permute-start.2
  16.5 0.0 copy-done.2
  16.5 2.1 %coupling.1.coupling_ref = bf16[16,64,512]{2,1,0:T(8,128)(2,1)S(1)} custom-call(bf16[7,16,4096]{2,1,0:T(8,128)(2,1)S(1)} %bitcast.7), custom_call_target="tpu_custom_call" | custom-call | flops 2000000000 | bytes 1048576 | tf_op jit(solution)/shard_map/coupling/pallas_call | solution.py:187
  18.6 0.0 collective-permute-done.2.refs_1_
  18.6 0.0 copy-start.1
  18.6 0.3 restrict.1.restrict_ref
  18.9 7.4 %collective-permute-done.left_ref = bf16[136,128]{1,0:T(8,128)(2,1)S(1)} collective-permute-done((bf16[136,128]{1,0:T(8,128)(2,1)S(1)}, bf16[136,128]{1,0:T(8,128)(2,1)S(1)}, u32[]{:S(2)}, u32[]{:S(2)}) %collective-permute-start) | collective-permute-done | bytes 34848 | tf_op jit(solution)/shard_map/ppermute | solution.py:207
  26.4 0.0 collective-permute-done.1.right_ref
  26.4 0.0 all-to-all-done.ghost_ref
  26.4 0.0 copy-done.1
  26.4 1.6 %product.1 = f32[256,128]{1,0:T(8,128)S(1)} custom-call(s32[7,16]{1,0:T(8,128)S(1)} %bitcast.6, bf16[16,136,128]{2,1,0:T(8,128)(2,1)S(1)} %all-to-all-done.ghost_ref, bf16[136,128]{1,0:T(8,128)(2,1)S(1)} %collective-permute-done.left_ref, bf16[136,128]{1,0:T(8,128)(2,1)S(1)} %collective-permute-done.1.right_ref, bf16[528,128]{1,0:T(8,128)(2,1)S(1)} %copy-done, ...), custom_call_target="tpu_custom_call" | custom-call | flops 200000000 | bytes 1048576 | tf_op jit(solution)/shard_map/product/pallas_call | solution.py:187
  28.0 12.0 %all_to_all.10 = f32[16,16,128]{2,1,0:T(8,128)S(1)} all-to-all(f32[16,16,128]{2,1,0:T(8,128)S(1)} %bitcast.5), channel_id=1, replica_groups={{0,16,8,24,2,18,10,26,4,20,12,28,6,22,14,30},{1,17,9,25,3,19,11,27,5,21..., dimensions={0} | all-to-all | bytes 262144 | tf_op jit(solution)/shard_map/all_to_all | solution.py:202
  39.9 0.6 %reduce_sum.9 = f32[16,128]{1,0:T(8,128)} reduce(f32[16,16,128]{2,1,0:T(8,128)S(1)} %all_to_all.10, f32[]{:T(128)} %constant.0.clone.1), dimensions={0}, to_apply=%region_0.0 | reduce | flops 30720 | bytes 139268 | tf_op jit(solution)/shard_map/reduce_sum | solution.py:263
Async XLA Ops:
  0.0 16.5 %copy-start.2 = (bf16[16,7,4096]{2,0,1:T(8,128)(2,1)S(1)}, bf16[16,7,4096]{2,0,1:T(8,128)(2,1)}, u32[]{:S(2)}) copy-start(bf16[16,7,4096]{2,0,1:T(8,128)(2,1)} %param.5) | copy-start | bytes 2752516
  2.3 8.5 %copy-start.4 = (bf16[136,128]{1,0:T(8,128)(2,1)S(1)}, bf16[136,128]{1,0:T(8,128)(2,1)}, u32[]{:S(2)}) copy-start(bf16[136,128]{1,0:T(8,128)(2,1)} %get-tuple-element.19) | copy-start | bytes 104452
  2.3 10.5 %copy-start.3 = (bf16[136,128]{1,0:T(8,128)(2,1)S(1)}, bf16[136,128]{1,0:T(8,128)(2,1)}, u32[]{:S(2)}) copy-start(bf16[136,128]{1,0:T(8,128)(2,1)} %get-tuple-element.20) | copy-start | bytes 104452
  2.3 14.2 %copy-start = (bf16[528,128]{1,0:T(8,128)(2,1)S(1)}, bf16[528,128]{1,0:T(8,128)(2,1)}, u32[]{:S(2)}) copy-start(bf16[528,128]{1,0:T(8,128)(2,1)} %get-tuple-element.21.refs_0_.own_ref) | copy-start | bytes 405508
  2.3 24.0 %all-to-all-start = ((bf16[16,136,128]{2,1,0:T(8,128)(2,1)}), bf16[16,136,128]{2,1,0:T(8,128)(2,1)S(1)}, u32[]{:S(2)}, u32[]{:S(2)}) async-start(bf16[16,136,128]{2,1,0:T(8,128)(2,1)} %get-tuple-element.18), calls=%async_computation | async-start | bytes 1114112 | tf_op jit(solution)/shard_map/all_to_all | solution.py:202
  10.8 15.5 %collective-permute-start = (bf16[136,128]{1,0:T(8,128)(2,1)S(1)}, bf16[136,128]{1,0:T(8,128)(2,1)S(1)}, u32[]{:S(2)}, u32[]{:S(2)}) collective-permute-start(bf16[136,128]{1,0:T(8,128)(2,1)S(1)} %copy-done.4), channel_id=1, source_target_pairs={{0,2},{2,4},{4,6},{6,8},{8,10},{10,12},{12,14},{14,16},{16,18},{18... | collective-permute-start | bytes 104456 | tf_op jit(solution)/shard_map/ppermute | solution.py:207
  12.8 13.6 %collective-permute-start.1 = (bf16[136,128]{1,0:T(8,128)(2,1)S(1)}, bf16[136,128]{1,0:T(8,128)(2,1)S(1)}, u32[]{:S(2)}, u32[]{:S(2)}) collective-permute-start(bf16[136,128]{1,0:T(8,128)(2,1)S(1)} %copy-done.3), channel_id=1, source_target_pairs={{0,30},{2,0},{4,2},{6,4},{8,6},{10,8},{12,10},{14,12},{16,14},{18,... | collective-permute-start | bytes 104456 | tf_op jit(solution)/shard_map/ppermute | solution.py:207
  16.5 2.1 %collective-permute-start.2 = (bf16[528,128]{1,0:T(8,128)(2,1)S(1)}, bf16[528,128]{1,0:T(8,128)(2,1)S(1)}, u32[]{:S(2)}, u32[]{:S(2)}) collective-permute-start(bf16[528,128]{1,0:T(8,128)(2,1)S(1)} %copy-done), channel_id=1, source_target_pairs={{0,1},{1,0},{2,3},{3,2},{4,5},{5,4},{6,7},{7,6},{8,9},{9,8},{10,11... | collective-permute-start | bytes 405512 | tf_op jit(solution)/shard_map/ppermute | solution.py:232
  18.6 7.8 %copy-start.1 = (s32[16,7]{0,1:T(8,128)S(1)}, s32[16,7]{0,1:T(8,128)}, u32[]{:S(2)}) copy-start(s32[16,7]{0,1:T(8,128)} %param.6) | copy-start | bytes 1348

commit v15 on v12

--- a/solution.py
+++ b/solution.py
@@ -77,9 +77,10 @@
     copies = [pltpu.make_async_copy(x, y, sems.at[i]) for i, (x, y) in enumerate(pairs)]
     for copy in copies:
         copy.start()
-    for copy in copies:
-        copy.wait()
+    copies[0].wait()
     unpack_rows(flat_ref, scratch)
+    copies[1].wait()
+    copies[2].wait()
     turn_rows(lambda r: index_ref[0, r], scratch, own_ref, 0)
     own_ref[rows * PACK :, :] = mask_table(lambda r: index_ref[0, r], rows).astype(BF16)
 

time: 40.8 us -> 40.8 us (level)
  no operation moved by 1% of the time
where the time goes in v15:
time: 40.8 us; the launch traced here: 40.5 us
  starting transfers between devices  14.1 us (35%)
  blocking collectives  12 us (29%)
  waiting for transfers between devices  7.44 us (18%)
  Pallas kernels  6.28 us (15%)
  other arithmetic  0.62 us (2%)
    all_to_all x1, blocking collectives, exchange(): lax.all_to_all(x, 'row', split_axis=0, concat_axis=0, tiled=True, axis_in...  12 us
    all_to_all x1, starting transfers between devices, exchange(): lax.all_to_all(x, 'row', split_axis=0, concat_axis=0, tiled=True, axis_in...  8.46 us
    ppermute x2, waiting for transfers between devices, ring(): return lax.ppermute(x, 'row', [(i, (i + step) % n) for i in range(n)])  7.44 us
    ppermute x2, starting transfers between devices, ring(): return lax.ppermute(x, 'row', [(i, (i + step) % n) for i in range(n)])  5.67 us
    pallas_call x3, Pallas kernels, call(): pl.pallas_call(body, out_shape=out_shape, in_specs=[SMEM] * smem + [VMEM]...  4 us
    pallas_call x1, Pallas kernels, shards(): pl.pallas_call(functools.partial(own_kernel, n), out_shape=(blocks, shape...  2.28 us
  transfers between devices with their start and end apart: 4, of which 1 were waited for; matrix products, arithmetic and copies ran while one was open for 0% of the time, Pallas kernels for 6%

profile of v15, /device:TPU:0, one launch (start us, length us, event | category | flops | bytes accessed | tf_op | source)
XLA Modules:
  0.0 40.5 jit_solution(15901580245911553153)
XLA Ops:
  0.0 0.0 copy-start.2
  0.0 2.3 %own.1 = (bf16[16,136,128]{2,1,0:T(8,128)(2,1)}, bf16[528,128]{1,0:T(8,128)(2,1)}, bf16[136,128]{1,0:T(8,128)(2,1)}, bf16[136,128]{1,0:T(8,128)(2,1)}) custom-call(s32[1,128]{1,0:T(1,128)} %send_hbm.1, s32[1,16]{1,0:T(1,128)} %bitcast.9, bf16[16,4096]{1,0:T(8,128)(2,1)} %bitcast.8), custom_call_target="tpu_custom_call" | custom-call | flops 10000000 | bytes 1048576 | tf_op jit(solution)/shard_map/own/pallas_call | solution.py:211
  2.3 0.0 copy-start.4
  2.3 0.0 copy-start.3
  2.3 0.0 copy-start
  2.3 8.5 %all-to-all-start = ((bf16[16,136,128]{2,1,0:T(8,128)(2,1)}), bf16[16,136,128]{2,1,0:T(8,128)(2,1)S(1)}, u32[]{:S(2)}, u32[]{:S(2)}) async-start(bf16[16,136,128]{2,1,0:T(8,128)(2,1)} %get-tuple-element.18), calls=%async_computation | async-start | bytes 1114112 | tf_op jit(solution)/shard_map/all_to_all | solution.py:201
  10.8 0.0 copy-done.4
  10.8 2.0 %collective-permute-start = (bf16[136,128]{1,0:T(8,128)(2,1)S(1)}, bf16[136,128]{1,0:T(8,128)(2,1)S(1)}, u32[]{:S(2)}, u32[]{:S(2)}) collective-permute-start(bf16[136,128]{1,0:T(8,128)(2,1)S(1)} %copy-done.4), channel_id=1, source_target_pairs={{0,2},{2,4},{4,6},{6,8},{8,10},{10,12},{12,14},{14,16},{16,18},{18... | collective-permute-start | bytes 104456 | tf_op jit(solution)/shard_map/ppermute | solution.py:206
  12.8 0.0 copy-done.3
  12.8 3.7 %collective-permute-start.1 = (bf16[136,128]{1,0:T(8,128)(2,1)S(1)}, bf16[136,128]{1,0:T(8,128)(2,1)S(1)}, u32[]{:S(2)}, u32[]{:S(2)}) collective-permute-start(bf16[136,128]{1,0:T(8,128)(2,1)S(1)} %copy-done.3), channel_id=1, source_target_pairs={{0,30},{2,0},{4,2},{6,4},{8,6},{10,8},{12,10},{14,12},{16,14},{18,... | collective-permute-start | bytes 104456 | tf_op jit(solution)/shard_map/ppermute | solution.py:206
  16.5 0.0 copy-done
  16.5 0.0 collective-permute-start.2
  16.5 0.0 copy-done.2
  16.5 2.1 %coupling.1.coupling_ref = bf16[16,64,512]{2,1,0:T(8,128)(2,1)S(1)} custom-call(bf16[7,16,4096]{2,1,0:T(8,128)(2,1)S(1)} %bitcast.7), custom_call_target="tpu_custom_call" | custom-call | flops 2000000000 | bytes 1048576 | tf_op jit(solution)/shard_map/coupling/pallas_call | solution.py:186
  18.6 0.0 collective-permute-done.2.refs_1_
  18.6 0.0 copy-start.1
  18.6 0.3 restrict.1.restrict_ref
  18.9 7.4 %collective-permute-done.left_ref = bf16[136,128]{1,0:T(8,128)(2,1)S(1)} collective-permute-done((bf16[136,128]{1,0:T(8,128)(2,1)S(1)}, bf16[136,128]{1,0:T(8,128)(2,1)S(1)}, u32[]{:S(2)}, u32[]{:S(2)}) %collective-permute-start) | collective-permute-done | bytes 34848 | tf_op jit(solution)/shard_map/ppermute | solution.py:206
  26.3 0.0 collective-permute-done.1.right_ref
  26.3 0.0 all-to-all-done.ghost_ref
  26.3 0.0 copy-done.1
  26.4 1.6 %product.1 = f32[256,128]{1,0:T(8,128)S(1)} custom-call(s32[7,16]{1,0:T(8,128)S(1)} %bitcast.6, bf16[16,136,128]{2,1,0:T(8,128)(2,1)S(1)} %all-to-all-done.ghost_ref, bf16[136,128]{1,0:T(8,128)(2,1)S(1)} %collective-permute-done.left_ref, bf16[136,128]{1,0:T(8,128)(2,1)S(1)} %collective-permute-done.1.right_ref, bf16[528,128]{1,0:T(8,128)(2,1)S(1)} %copy-done, ...), custom_call_target="tpu_custom_call" | custom-call | flops 200000000 | bytes 1048576 | tf_op jit(solution)/shard_map/product/pallas_call | solution.py:186
  28.0 12.0 %all_to_all.10 = f32[16,16,128]{2,1,0:T(8,128)S(1)} all-to-all(f32[16,16,128]{2,1,0:T(8,128)S(1)} %bitcast.5), channel_id=1, replica_groups={{0,16,8,24,2,18,10,26,4,20,12,28,6,22,14,30},{1,17,9,25,3,19,11,27,5,21..., dimensions={0} | all-to-all | bytes 262144 | tf_op jit(solution)/shard_map/all_to_all | solution.py:201
  39.9 0.6 %reduce_sum.9 = f32[16,128]{1,0:T(8,128)} reduce(f32[16,16,128]{2,1,0:T(8,128)S(1)} %all_to_all.10, f32[]{:T(128)} %constant.0.clone.1), dimensions={0}, to_apply=%region_0.0 | reduce | flops 30720 | bytes 139268 | tf_op jit(solution)/shard_map/reduce_sum | solution.py:262
Async XLA Ops:
  0.0 16.5 %copy-start.2 = (bf16[16,7,4096]{2,0,1:T(8,128)(2,1)S(1)}, bf16[16,7,4096]{2,0,1:T(8,128)(2,1)}, u32[]{:S(2)}) copy-start(bf16[16,7,4096]{2,0,1:T(8,128)(2,1)} %param.5) | copy-start | bytes 2752516
  2.3 8.5 %copy-start.4 = (bf16[136,128]{1,0:T(8,128)(2,1)S(1)}, bf16[136,128]{1,0:T(8,128)(2,1)}, u32[]{:S(2)}) copy-start(bf16[136,128]{1,0:T(8,128)(2,1)} %get-tuple-element.19) | copy-start | bytes 104452
  2.3 10.5 %copy-start.3 = (bf16[136,128]{1,0:T(8,128)(2,1)S(1)}, bf16[136,128]{1,0:T(8,128)(2,1)}, u32[]{:S(2)}) copy-start(bf16[136,128]{1,0:T(8,128)(2,1)} %get-tuple-element.20) | copy-start | bytes 104452
  2.3 14.2 %copy-start = (bf16[528,128]{1,0:T(8,128)(2,1)S(1)}, bf16[528,128]{1,0:T(8,128)(2,1)}, u32[]{:S(2)}) copy-start(bf16[528,128]{1,0:T(8,128)(2,1)} %get-tuple-element.21.refs_0_.own_ref) | copy-start | bytes 405508
  2.3 24.0 %all-to-all-start = ((bf16[16,136,128]{2,1,0:T(8,128)(2,1)}), bf16[16,136,128]{2,1,0:T(8,128)(2,1)S(1)}, u32[]{:S(2)}, u32[]{:S(2)}) async-start(bf16[16,136,128]{2,1,0:T(8,128)(2,1)} %get-tuple-element.18), calls=%async_computation | async-start | bytes 1114112 | tf_op jit(solution)/shard_map/all_to_all | solution.py:201
  10.8 15.5 %collective-permute-start = (bf16[136,128]{1,0:T(8,128)(2,1)S(1)}, bf16[136,128]{1,0:T(8,128)(2,1)S(1)}, u32[]{:S(2)}, u32[]{:S(2)}) collective-permute-start(bf16[136,128]{1,0:T(8,128)(2,1)S(1)} %copy-done.4), channel_id=1, source_target_pairs={{0,2},{2,4},{4,6},{6,8},{8,10},{10,12},{12,14},{14,16},{16,18},{18... | collective-permute-start | bytes 104456 | tf_op jit(solution)/shard_map/ppermute | solution.py:206
  12.8 13.6 %collective-permute-start.1 = (bf16[136,128]{1,0:T(8,128)(2,1)S(1)}, bf16[136,128]{1,0:T(8,128)(2,1)S(1)}, u32[]{:S(2)}, u32[]{:S(2)}) collective-permute-start(bf16[136,128]{1,0:T(8,128)(2,1)S(1)} %copy-done.3), channel_id=1, source_target_pairs={{0,30},{2,0},{4,2},{6,4},{8,6},{10,8},{12,10},{14,12},{16,14},{18,... | collective-permute-start | bytes 104456 | tf_op jit(solution)/shard_map/ppermute | solution.py:206
  16.5 2.1 %collective-permute-start.2 = (bf16[528,128]{1,0:T(8,128)(2,1)S(1)}, bf16[528,128]{1,0:T(8,128)(2,1)S(1)}, u32[]{:S(2)}, u32[]{:S(2)}) collective-permute-start(bf16[528,128]{1,0:T(8,128)(2,1)S(1)} %copy-done), channel_id=1, source_target_pairs={{0,1},{1,0},{2,3},{3,2},{4,5},{5,4},{6,7},{7,6},{8,9},{9,8},{10,11... | collective-permute-start | bytes 405512 | tf_op jit(solution)/shard_map/ppermute | solution.py:231
  18.6 7.8 %copy-start.1 = (s32[16,7]{0,1:T(8,128)S(1)}, s32[16,7]{0,1:T(8,128)}, u32[]{:S(2)}) copy-start(s32[16,7]{0,1:T(8,128)} %param.6) | copy-start | bytes 1348
